TPU v7x, 256 devices: a whole 4x4x8 slice. The times are simulated.
256 devices in a mesh: tm: 32 (over z_hi, x, core), space: 8 (over z_lo, y).
Axes of the slice: x: 4, y: 4, z: 8 (z_hi: 4, z_lo: 2; z = z_hi * 2 + z_lo), core: 2. Of those that a mesh axis runs over, the one named last changes fastest.
Arguments:
- input_frames: bfloat16 [256, 256, 768], P('tm', 'space'), may hold values from -6 to 6
- d_out: bfloat16 [256, 256, 768], P('tm', 'space'), may hold values from -6 to 6
- w_qkv: bfloat16 [768, 2304], replicated, may hold values from -0.21875 to 0.21875
- w_out: bfloat16 [768, 768], replicated, may hold values from -0.21875 to 0.21875
Outputs:
- input_gradient: bfloat16 [256, 256, 768], P('tm', 'space')
- grad_qkv: float32 [768, 2304], P(('tm', 'space'))
- grad_out: float32 [768, 768], P(('tm', 'space'))
All inputs are finite; a program needn't handle non-finite values.
Results may differ from a plain program's by a relative error of at most 0.013.
Values may be sent and summed in bfloat16 or wider, within the bound.
No kernel may reach another device: no remote copies, remote signals or barrier semaphores. Data moves between devices by JAX's collectives and lax.ppermute only.
A program may use at most 128 MiB of HBM per device.

v0:
```python
import jax
import jax.numpy as jnp
from jax import lax
from jax.sharding import PartitionSpec as P

HEADS = 12


def times_transposed(left, right):
    return lax.dot_general(
        left, right, (((1,), (1,)), ((), ())), preferred_element_type=jnp.float32
    )


def inner_rows(left, right):
    return lax.dot_general(
        left, right, (((0,), (0,)), ((), ())), preferred_element_type=jnp.float32
    )


def layer_normalize(tokens_rows):
    x_rows = tokens_rows.astype(jnp.float32)
    row_mean = jnp.mean(x_rows, axis=1, keepdims=True)
    centered_rows = x_rows - row_mean
    inverse_deviation = 1.0 / jnp.sqrt(
        jnp.mean(centered_rows * centered_rows, axis=1, keepdims=True) + 1e-05
    )
    standardized_input = centered_rows * inverse_deviation
    return (standardized_input, inverse_deviation, standardized_input.astype(jnp.bfloat16))


def attend(qkv_t, dattn_t):
    frames, items, triple = qkv_t.shape
    feature_width = triple // 3
    head_dim = feature_width // HEADS
    scale = 1.0 / head_dim**0.5
    parts = qkv_t.reshape(frames, items, 3, HEADS, head_dim)
    query, keys, values = (parts[:, :, 0], parts[:, :, 1], parts[:, :, 2])
    scores = jnp.einsum("fphe,gphe->phfg", query, keys, preferred_element_type=jnp.float32) * scale
    probs = jax.nn.softmax(scores, axis=-1)
    probs_b = probs.astype(jnp.bfloat16)
    attn = jnp.einsum(
        "phfg,gphe->fphe", probs_b, values, preferred_element_type=jnp.float32
    ).astype(jnp.bfloat16)
    dattn = dattn_t.reshape(frames, items, HEADS, head_dim)
    dvalue = jnp.einsum(
        "phfg,fphe->gphe", probs_b, dattn, preferred_element_type=jnp.float32
    ).astype(jnp.bfloat16)
    dprobs = jnp.einsum("fphe,gphe->phfg", dattn, values, preferred_element_type=jnp.float32)
    delta = jnp.sum(dattn.astype(jnp.float32) * attn.astype(jnp.float32), axis=-1)
    dscores = probs * (dprobs - jnp.transpose(delta, (1, 2, 0))[:, :, :, None]) * scale
    dscores_b = dscores.astype(jnp.bfloat16)
    dquery = jnp.einsum(
        "phfg,gphe->fphe", dscores_b, keys, preferred_element_type=jnp.float32
    ).astype(jnp.bfloat16)
    dkey = jnp.einsum(
        "phfg,fphe->gphe", dscores_b, query, preferred_element_type=jnp.float32
    ).astype(jnp.bfloat16)
    dqkv = jnp.stack([dquery, dkey, dvalue], axis=2).reshape(frames, items, triple)
    return (attn.reshape(frames, items, feature_width), dqkv)


def local(input_frames, d_out, w_qkv, w_out):
    frame_count, patch_count, feature_width = input_frames.shape
    token_rows = frame_count * patch_count
    standardized_input, inverse_deviation, normalized_rows = layer_normalize(
        input_frames.reshape(token_rows, feature_width)
    )
    qkv = jnp.dot(normalized_rows, w_qkv, preferred_element_type=jnp.float32).astype(jnp.bfloat16)
    qkv = qkv.reshape(frame_count, patch_count, 3 * feature_width)
    output_gradient_rows = d_out.reshape(token_rows, feature_width)
    dattn = (
        times_transposed(output_gradient_rows, w_out)
        .astype(jnp.bfloat16)
        .reshape(frame_count, patch_count, feature_width)
    )
    qkv_t, dattn_t = (
        lax.all_to_all(qkv, "tm", split_axis=1, concat_axis=0, tiled=True),
        lax.all_to_all(dattn, "tm", split_axis=1, concat_axis=0, tiled=True),
    )
    attn_t, dqkv_t = attend(qkv_t, dattn_t)
    attn_back, dqkv = (
        lax.all_to_all(attn_t, "tm", split_axis=0, concat_axis=1, tiled=True),
        lax.all_to_all(dqkv_t, "tm", split_axis=0, concat_axis=1, tiled=True),
    )
    left = attn_back.reshape(token_rows, feature_width)
    dqkv_rows = dqkv.reshape(token_rows, 3 * feature_width)
    grad_qkv = lax.psum_scatter(
        inner_rows(normalized_rows, dqkv_rows), ("tm", "space"), scatter_dimension=0, tiled=True
    )
    grad_out = lax.psum_scatter(
        inner_rows(left, output_gradient_rows), ("tm", "space"), scatter_dimension=0, tiled=True
    )
    normalized_gradient = times_transposed(dqkv_rows, w_qkv)
    first_term = jnp.mean(normalized_gradient, axis=1, keepdims=True)
    second_term = jnp.mean(normalized_gradient * standardized_input, axis=1, keepdims=True)
    row_gradient = (
        output_gradient_rows.astype(jnp.float32)
        + inverse_deviation * (normalized_gradient - first_term - standardized_input * second_term)
    ).astype(jnp.bfloat16)
    input_gradient = row_gradient.reshape(frame_count, patch_count, feature_width)
    return (input_gradient, grad_qkv, grad_out)


def solution(mesh):
    placed = (P("tm", "space", None), P("tm", "space", None), P(), P())
    return jax.shard_map(
        local,
        mesh=mesh,
        in_specs=placed,
        out_specs=(P("tm", "space", None), P(("tm", "space"), None), P(("tm", "space"), None)),
        check_vma=False,
    )
```

profile of v0, /device:TPU:1, one launch (start us, length us, event | category | flops | bytes accessed | tf_op | source)
XLA Modules:
  0.0 467.7 jit_solution(17713384288994787403)
XLA Ops:
  7.2 2.0 convolution_convert_fusion.5
  10.2 12.6 %all-to-all-start.1 = ((bf16[8,32,768]{2,0,1:T(8,128)(2,1)}), bf16[8,32,768]{2,0,1:T(8,128)(2,1)}, u32[]{:S(2)}, u32[]{:S(2)}) async-start(bf16[8,32,768]{2,0,1:T(8,128)(2,1)} %copy.35), calls=%async_computation.1 | async-start | bytes 786432 | tf_op jit(solution)/shard_map/all_to_all | solution.py:79
  29.5 9.5 %all-to-all-done.1 = bf16[8,32,768]{2,0,1:T(8,128)(2,1)} async-done(((bf16[8,32,768]{2,0,1:T(8,128)(2,1)}), bf16[8,32,768]{2,0,1:T(8,128)(2,1)}, u32[]{:S(2)}, u32[]{:S(2)}) %all-to-all-start.1) | async-done | bytes 393248 | tf_op jit(solution)/shard_map/all_to_all | solution.py:79
  38.9 4.5 all-to-all-start
  43.4 2.4 reshape.178
  45.8 2.6 copy.37
  50.3 2.8 reshape.186
  53.1 3.2 copy.39
  56.3 16.5 %all-to-all-done = bf16[8,32,2304]{2,0,1:T(8,128)(2,1)} async-done(((bf16[8,32,2304]{2,0,1:T(8,128)(2,1)}), bf16[8,32,2304]{2,0,1:T(8,128)(2,1)}, u32[]{:S(2)}, u32[]{:S(2)}) %all-to-all-start) | async-done | bytes 1179680 | tf_op jit(solution)/shard_map/all_to_all | solution.py:78
  72.7 4.7 reshape.174
  77.4 3.8 fusion.20
  81.2 2.6 copy.57
  83.8 2.6 copy.56
  88.1 2.4 fusion.21
  90.5 2.6 copy.58
  93.1 2.3 fusion.5
  98.9 2.6 reduce.8
  101.5 1.9 copy.64
  105.3 6.7 %all-to-all-start.3 = ((bf16[32,2,3072]{2,1,0:T(2,128)(2,1)}), bf16[32,2,3072]{2,1,0:T(2,128)(2,1)}, u32[]{:S(2)}, u32[]{:S(2)}) async-start(bf16[32,2,3072]{2,1,0:T(2,128)(2,1)} %reshape.189), calls=%async_computation.3 | async-start | bytes 786432 | tf_op jit(solution)/shard_map/all_to_all | solution.py:83
  112.0 3.0 multiply_convert_fusion
  118.2 3.5 reduce.7
  121.7 2.4 copy.63
  124.1 3.9 reshape.187
  128.0 9.8 %all-to-all-start.2 = ((bf16[32,2,9216]{2,1,0:T(2,128)(2,1)}), bf16[32,2,9216]{2,1,0:T(2,128)(2,1)}, u32[]{:S(2)}, u32[]{:S(2)}) async-start(bf16[32,2,9216]{2,1,0:T(2,128)(2,1)} %reshape.187), calls=%async_computation.2 | async-start | bytes 2359296 | tf_op jit(solution)/shard_map/all_to_all | solution.py:84
  137.9 1.9 multiply_convert_fusion.1
  139.8 3.5 reshape.190
  144.5 2.9 fusion.23
  147.5 21.9 %all-to-all-done.2 = bf16[32,2,9216]{2,1,0:T(2,128)(2,1)} async-done(((bf16[32,2,9216]{2,1,0:T(2,128)(2,1)}), bf16[32,2,9216]{2,1,0:T(2,128)(2,1)}, u32[]{:S(2)}, u32[]{:S(2)}) %all-to-all-start.2) | async-done | bytes 1179680 | tf_op jit(solution)/shard_map/all_to_all | solution.py:84
  169.3 5.8 %reshape.188 = bf16[256,1,2304]{2,1,0:T(2,128)(2,1)} reshape(bf16[32,2,9216]{2,1,0:T(2,128)(2,1)} %all-to-all-done.2) | data formatting | bytes 2359296
  178.2 4.1 fusion.22
  183.0 2.7 fusion.19
  186.8 271.1 %all-reduce.5.cloned.1.call-done = (f32[768,2304]{1,0:T(8,128)}, f32[768,768]{1,0:T(8,128)}) async-done(((f32[768,2304]{1,0:T(8,128)}, f32[768,768]{1,0:T(8,128)}), (f32[768,2304]{1,0:T(8,128)}, f32[768,768]{1,0:T(8,128)})) %all-reduce.5.cloned.1.call-update) | async-done | bytes 9437200
  (70 shorter events, 28.8 us)
Async XLA Ops:
  7.2 19.5 %copy-start = (bf16[768,2304]{1,0:T(8,128)(2,1)S(1)}, bf16[768,2304]{1,0:T(8,128)(2,1)}, u32[]{:S(2)}) copy-start(bf16[768,2304]{1,0:T(8,128)(2,1)} %param.6) | copy-start | bytes 10616836
  10.2 28.7 %all-to-all-start.1 = ((bf16[8,32,768]{2,0,1:T(8,128)(2,1)}), bf16[8,32,768]{2,0,1:T(8,128)(2,1)}, u32[]{:S(2)}, u32[]{:S(2)}) async-start(bf16[8,32,768]{2,0,1:T(8,128)(2,1)} %copy.35), calls=%async_computation.1 | async-start | bytes 786432 | tf_op jit(solution)/shard_map/all_to_all | solution.py:79
  24.0 3.8 copy-start.12
  25.3 2.4 copy-start.16
  25.3 2.4 copy-start.14
  25.4 2.4 copy-start.18
  38.9 33.8 %all-to-all-start = ((bf16[8,32,2304]{2,0,1:T(8,128)(2,1)}), bf16[8,32,2304]{2,0,1:T(8,128)(2,1)}, u32[]{:S(2)}, u32[]{:S(2)}) async-start(bf16[8,32,2304]{2,0,1:T(8,128)(2,1)} %copy.32), calls=%async_computation | async-start | bytes 2359296 | tf_op jit(solution)/shard_map/all_to_all | solution.py:78
  93.1 3.5 copy-start.8
  93.1 3.5 copy-start.11
  95.4 1.2 copy-start.1
  105.3 22.6 %all-to-all-start.3 = ((bf16[32,2,3072]{2,1,0:T(2,128)(2,1)}), bf16[32,2,3072]{2,1,0:T(2,128)(2,1)}, u32[]{:S(2)}, u32[]{:S(2)}) async-start(bf16[32,2,3072]{2,1,0:T(2,128)(2,1)} %reshape.189), calls=%async_computation.3 | async-start | bytes 786432 | tf_op jit(solution)/shard_map/all_to_all | solution.py:83
  112.0 3.0 copy-start.2
  112.0 3.0 copy-start.10
  115.1 1.0 copy-start.6
  115.1 1.6 copy-start.7
  124.1 13.8 %copy-start.13 = (f32[8,32]{1,0:T(8,128)S(1)}, f32[8,32]{1,0:T(8,128)}, u32[]{:S(2)}) copy-start(f32[8,32]{1,0:T(8,128)} %copy-done.12) | copy-start | bytes 3076
  124.1 13.8 %copy-start.15 = (f32[8,32]{1,0:T(8,128)S(1)}, f32[8,32]{1,0:T(8,128)}, u32[]{:S(2)}) copy-start(f32[8,32]{1,0:T(8,128)} %copy-done.14) | copy-start | bytes 3076
  128.0 41.4 %all-to-all-start.2 = ((bf16[32,2,9216]{2,1,0:T(2,128)(2,1)}), bf16[32,2,9216]{2,1,0:T(2,128)(2,1)}, u32[]{:S(2)}, u32[]{:S(2)}) async-start(bf16[32,2,9216]{2,1,0:T(2,128)(2,1)} %reshape.187), calls=%async_computation.2 | async-start | bytes 2359296 | tf_op jit(solution)/shard_map/all_to_all | solution.py:84
  137.8 320.1 %all-reduce.5.cloned.1.call-start = ((), (), s32[]{:S(2)}) async-start(), calls=%async_computation.4 | async-start | bytes 18874368
  175.1 3.1 copy-start.9
  177.2 1.0 copy-start.4
  182.3 0.7 copy-start.17
  182.3 0.7 copy-start.19
  183.0 2.7 copy-start.3
  183.0 2.7 copy-start.5
Sparse Core Ops, SparseCore 0:
  182.4 275.4 all-reduce.4
where the time goes:
time: 470 us; the launch traced here: 468 us
  waiting for transfers between devices  319 us (68%)
  local copies, waits for them, and re-layouts  59.4 us (13%)
  starting transfers between devices  33.6 us (7%)
  matrix products  20.9 us (4%)
  other arithmetic  20.5 us (4%)
  between operations  14.4 us (3%)
    unnamed x2, waiting for transfers between devices  271 us
    unnamed x53, local copies, waits for them, and re-layouts  36.3 us
    all_to_all x1, waiting for transfers between devices, local(): lax.all_to_all(dqkv_t, 'tm', split_axis=0, concat_axis=1, tiled=True)  21.9 us
    all_to_all x1, waiting for transfers between devices, local(): lax.all_to_all(qkv, 'tm', split_axis=1, concat_axis=0, tiled=True)  16.5 us
    all_to_all x1, starting transfers between devices, local(): lax.all_to_all(dattn, 'tm', split_axis=1, concat_axis=0, tiled=True)  12.6 us
    all_to_all x1, starting transfers between devices, local(): lax.all_to_all(dqkv_t, 'tm', split_axis=0, concat_axis=1, tiled=True)  9.84 us
    all_to_all x1, waiting for transfers between devices, local(): lax.all_to_all(dattn, 'tm', split_axis=1, concat_axis=0, tiled=True)  9.46 us
  transfers between devices with their start and end apart: 5, of which 4 were waited for; matrix products, arithmetic and copies ran while one was open for 10% of the time, Pallas kernels for 0%

commit v1 on v0

v1 whole, which is shorter than its diff:
```python
import functools

import jax
import jax.numpy as jnp
import numpy as np
from jax import lax
from jax.experimental import pallas as pl
from jax.experimental.pallas import tpu as pltpu
from jax.sharding import Mesh, PartitionSpec as P

HEAD = 64
BF = jnp.bfloat16
F32 = jnp.float32
VM = pl.BlockSpec(memory_space=pltpu.VMEM)
SM = pl.BlockSpec(memory_space=pltpu.SMEM)


def nn(a, b):
    return lax.dot_general(a, b, (((1,), (0,)), ((), ())), preferred_element_type=F32)


def nt(a, b):
    return lax.dot_general(a, b, (((1,), (1,)), ((), ())), preferred_element_type=F32)


def call(body, outs, ins, scratch=(), smem=(), flops=0, nbytes=0, limit=48):
    return pl.pallas_call(
        body,
        out_shape=[jax.ShapeDtypeStruct(s, d) for s, d in outs],
        in_specs=[SM if i in smem else VM for i in range(len(ins))],
        out_specs=[VM] * len(outs),
        scratch_shapes=list(scratch),
        compiler_params=pltpu.CompilerParams(vmem_limit_bytes=limit * 2**20),
        cost_estimate=pl.CostEstimate(flops=flops, bytes_accessed=nbytes, transcendentals=0),
    )(*ins)


def selection(rows, source):
    at = lax.broadcasted_iota(jnp.int32, (rows, source.shape[1]), 0)
    return (at == source).astype(F32).astype(BF)


def home_table():
    f, p = np.divmod(np.arange(256), 32)
    return ((p // 2) * 16 + (p % 2) * 8 + f).astype(np.int32)[None]


def feature_table(n):
    f = np.arange(n)
    d, j = f // 3, f % 3
    s8, up = d % 8, d // 8
    return (s8 * (n // 8) + up * 3 + j).astype(np.int32)[None]


def second_table():
    out = np.full((8, 384), -4096, np.int32)
    out[2] = 0
    for i in range(384):
        if i < 288:
            t, rem = divmod(i, 96)
            half = 0
        else:
            t, rem = 3, (i - 288) % 48
            half = (i - 288) // 48
        zh, rem = divmod(rem, 24)
        x, rem = divmod(rem, 6)
        c, j = divmod(rem, 3)
        if t < 2:
            row, half = j, t
        elif t == 2:
            row, half = 3 + j // 2, j % 2
        else:
            row = 5 + j
            out[2, i] = 32
        out[half, i] = (x * 4 + zh) * 16 + c * 8 + row
    return out


def pack_body(x_ref, d_ref, home_ref, o_ref):
    sel = selection(256, home_ref[...])
    o_ref[:, 0:16, :] = nn(sel, x_ref[...]).astype(BF).reshape(16, 16, 768)
    o_ref[:, 16:32, :] = nn(sel, d_ref[...]).astype(BF).reshape(16, 16, 768)


def rows_of(ref, first):
    start = first // 16 * 16
    block = ref[:, start : start + 16, :].astype(F32)
    return block[:, first - start : first - start + 8, :].reshape(128, 768)


def normalize(x):
    mean = jnp.mean(x, axis=1, keepdims=True)
    cen = x - mean
    inv = 1.0 / jnp.sqrt(jnp.mean(cen * cen, axis=1, keepdims=True) + 1e-05)
    return cen * inv, inv


def main_body(own_ref, oth_ref, w_ref, wo_ref, feat_ref, feat2_ref, g_ref, dqkv_ref,
              n_s, d_s, qkv_s, a_s, kt_s, vt_s, at_s, dqt_s, att_s, nt_s):
    for patch in range(2):
        for side, ref in enumerate((own_ref, oth_ref)):
            at = patch * 256 + side * 128
            n_s[at : at + 128, :] = normalize(rows_of(ref, patch * 8))[0].astype(BF)
            d_s[at : at + 128, :] = rows_of(ref, 16 + patch * 8).astype(BF)
    for t in range(3):
        qkv_s[:, t * 384 : (t + 1) * 384] = nn(n_s[...], w_ref[:, t * 384 : (t + 1) * 384]).astype(BF)
    a_s[...] = nt(d_s[...], wo_ref[...]).astype(BF)
    kt_s[...] = (qkv_s[:, 384:768] * 0.125).T
    vt_s[...] = qkv_s[:, 768:1152].T
    at_s[...] = a_s[...].T
    lane = lax.broadcasted_iota(jnp.int32, (1, 128), 1)

    def unit(u, carry):
        patch, pair = u // 3, lax.rem(u, 3)
        rows = pl.ds(pl.multiple_of(patch * 256, 256), 256)

        def cols(base):
            return pl.ds(pl.multiple_of(base + pair * 128, 128), 128)

        q = qkv_s[rows, cols(0)] * 0.125
        k = qkv_s[rows, cols(384)]
        v = qkv_s[rows, cols(768)]
        a = a_s[rows, cols(0)]
        dks, dvs = [], []
        for h in range(2):
            keep = ((lane >= h * HEAD) & (lane < (h + 1) * HEAD)).astype(F32).astype(BF)
            hr = pl.ds(pl.multiple_of(pair * 128 + h * HEAD, HEAD), HEAD)
            qh, ah = q * keep, a * keep
            st = nt(k, qh)
            e = jnp.exp(st - jnp.max(st, axis=0, keepdims=True))
            p = e * (1.0 / jnp.sum(e, axis=0, keepdims=True))
            pb = p.astype(BF)
            attn = nn(vt_s[hr, rows], pb).astype(BF)
            att_s[hr, rows] = attn
            delta = jnp.sum(at_s[hr, rows].astype(F32) * attn.astype(F32), axis=0, keepdims=True)
            ds = (p * (nt(v, ah) - delta)).astype(BF)
            dqt_s[hr, rows] = nn(kt_s[hr, rows], ds).astype(BF)
            dvs.append(nn(pb, ah))
            dks.append(nn(ds, qh))
        dqkv_ref[rows, cols(384)] = (dks[0] + dks[1]).astype(BF)
        dqkv_ref[rows, cols(768)] = (dvs[0] + dvs[1]).astype(BF)
        return carry

    lax.fori_loop(0, 6, unit, 0)
    dqkv_ref[:, 0:384] = dqt_s[...].T
    nt_s[...] = nt(selection(768, feat_ref[...]), n_s[...]).astype(BF)
    for t in range(3):
        g = nn(nt_s[...], dqkv_ref[:, t * 384 : (t + 1) * 384]).astype(BF)
        g_ref[:, t * 96 : (t + 1) * 96, :] = g.reshape(8, 96, 384)
    attp = nn(selection(384, feat2_ref[...]), att_s[...]).astype(BF)
    for t in range(2):
        g = nn(attp, d_s[:, t * 384 : (t + 1) * 384]).astype(BF)
        g_ref[:, 288 + t * 48 : 288 + (t + 1) * 48, :] = g.reshape(8, 48, 384)


def dnormed_body(dqkv_ref, w_ref, own_ref, oth_ref):
    part = nt(dqkv_ref[...], w_ref[...])
    for patch in range(2):
        own_ref[patch * 128 : (patch + 1) * 128, :] = part[patch * 256 : patch * 256 + 128]
        oth_ref[patch * 128 : (patch + 1) * 128, :] = part[patch * 256 + 128 : patch * 256 + 256].astype(BF)


def input_gradient_body(part_ref, got_ref, own_ref, o_ref):
    outs = []
    for patch in range(2):
        xhat, inv = normalize(rows_of(own_ref, patch * 8))
        dout = rows_of(own_ref, 16 + patch * 8)
        at = pl.ds(patch * 128, 128)
        dn = part_ref[at, :] + got_ref[at, :].astype(F32)
        first = jnp.mean(dn, axis=1, keepdims=True)
        second = jnp.mean(dn * xhat, axis=1, keepdims=True)
        outs.append((dout + inv * (dn - first - xhat * second)).reshape(16, 8, 768))
    o_ref[...] = jnp.concatenate(outs, axis=1).astype(BF)


def second_body(core_ref, r_ref, ig_ref, table_ref, o_ref):
    total = r_ref[0].astype(F32)
    for s in range(1, 8):
        total = total + r_ref[s].astype(F32)
    total = total.astype(BF)
    shift = table_ref[2:3, :] * core_ref[0]
    o_ref[:, 0:16, :] = ig_ref[...]
    for h in range(2):
        part = nn(selection(256, table_ref[h : h + 1, :] + shift), total).astype(BF)
        o_ref[:, 16:32, h * 384 : (h + 1) * 384] = part.reshape(16, 16, 384)


def home_body(core_ref, r_ref, home_ref, ig_ref, own_ref, oth_ref):
    sel = selection(256, home_ref[...])
    back = lax.dot_general(
        sel, r_ref[:, 0:16, :].reshape(256, 768), (((0,), (0,)), ((), ())), preferred_element_type=F32
    )
    ig_ref[...] = back.astype(BF)
    total = r_ref[0, 16:32, :].astype(F32)
    for s in range(1, 16):
        total = total + r_ref[s, 16:32, :].astype(F32)
    low = core_ref[0] == 0
    own_ref[...] = jnp.where(low, total[0:8], total[8:16])
    oth_ref[...] = jnp.where(low, total[8:16], total[0:8])


def last_body(core_ref, own_ref, got_ref, gq_ref, go_ref):
    own, got = own_ref[...], got_ref[...]
    low = core_ref[0] == 0
    halves = (jnp.where(low, own, got), jnp.where(low, got, own))
    for h, m in enumerate(halves):
        at = h * 384
        gq_ref[:, at : at + 384] = m[0:3, 0:384]
        gq_ref[:, 768 + at : 768 + at + 384] = m[0:3, 384:768]
        gq_ref[0:1, 1536 + at : 1536 + at + 384] = m[3:4, 0:384]
        gq_ref[1:2, 1536 + at : 1536 + at + 384] = m[3:4, 384:768]
        gq_ref[2:3, 1536 + at : 1536 + at + 384] = m[4:5, 0:384]
    go_ref[...] = own[5:8] + got[5:8]


def local(x, d, w_qkv, w_out):
    core = lax.axis_index("c")
    core1 = core.reshape(1).astype(jnp.int32)
    home = jnp.asarray(home_table())
    feat, feat2 = jnp.asarray(feature_table(768)), jnp.asarray(feature_table(384))
    slots = jnp.asarray(second_table())

    def swap(v):
        return lax.ppermute(v, "c", [(0, 1), (1, 0)])

    packed, = call(pack_body, [((16, 32, 768), BF)], [x.reshape(256, 768), d.reshape(256, 768), home])
    own = lax.all_to_all(packed, ("x", "zh"), split_axis=0, concat_axis=0, tiled=True)
    oth = swap(own)
    w = lax.dynamic_slice(w_qkv.reshape(768, 3, 768), (0, 0, core * 384), (768, 3, 384)).reshape(768, 1152)
    wo = lax.dynamic_slice(w_out, (core * 384, 0), (384, 768))
    scr = lambda *s: pltpu.VMEM(s, BF)
    grads, dqkv = call(
        main_body,
        [((8, 384, 384), BF), ((512, 1152), BF)],
        [own, oth, w, wo, feat, feat2],
        scratch=[scr(512, 768), scr(512, 768), scr(512, 1152), scr(512, 384), scr(384, 512), scr(384, 512),
                 scr(384, 512), scr(384, 512), scr(384, 512), scr(768, 512)],
        flops=6 * 10**9,
        nbytes=10**7,
    )
    part = lax.all_to_all(grads, ("zl", "y"), split_axis=0, concat_axis=0, tiled=True)
    mine, theirs = call(
        dnormed_body, [((256, 768), F32), ((256, 768), BF)], [dqkv, w], flops=10**9, nbytes=5 * 10**6
    )
    got = swap(theirs)
    ig, = call(input_gradient_body, [((16, 16, 768), BF)], [mine, got, own], nbytes=3 * 10**6)
    mixed, = call(second_body, [((16, 32, 768), BF)], [core1, part, ig, slots], smem=(0,))
    back = lax.all_to_all(mixed, ("x", "zh"), split_axis=0, concat_axis=0, tiled=True)
    ig_home, own8, oth8 = call(
        home_body, [((256, 768), BF), ((8, 768), F32), ((8, 768), F32)], [core1, back, home], smem=(0,)
    )
    grad_qkv, grad_out = call(
        last_body, [((3, 2304), F32), ((3, 768), F32)], [core1, own8, swap(oth8)], smem=(0,)
    )
    return ig_home.reshape(8, 32, 768), grad_qkv, grad_out


def solution(mesh):
    fine = Mesh(mesh.devices.reshape(4, 4, 2, 2, 4), ("zh", "x", "c", "zl", "y"))
    tm, space = ("zh", "x", "c"), ("zl", "y")
    tokens, rows = P(tm, space, None), P(tm + space, None)
    return jax.shard_map(
        local,
        mesh=fine,
        in_specs=(tokens, tokens, P(), P()),
        out_specs=(tokens, rows, rows),
        check_vma=False,
    )
```

time: 470 us -> 136 us (0.29)
  waiting for transfers between devices: 319 us -> 23.9 us
  blocking collectives: 0 us -> 57.4 us
  local copies, waits for them, and re-layouts: 59.4 us -> 22.3 us
  starting transfers between devices: 33.6 us -> 10.9 us
  matrix products: 20.9 us -> 0 us
  other arithmetic: 20.5 us -> 0 us
  Pallas kernels: 0 us -> 19.4 us
  between operations: 14.4 us -> 0.76 us
    unnamed x2 -> x0, waiting for transfers between devices: 271 us -> none
    all_to_all x0 -> x2, blocking collectives: none -> 57.4 us  [the longest x1 34.1 us: local(): lax.all_to_all(packed, ('x', 'zh'), split_axis=0, concat_axis=0, tiled=True)]
    all_to_all x4 -> x1, starting transfers between devices: 33.6 us -> 4.2 us  [local(): lax.all_to_all(grads, ('zl', 'y'), split_axis=0, concat_axis=0, tiled=True)]
    all_to_all x4 -> x1, waiting for transfers between devices: 47.8 us -> 21.7 us  [local(): lax.all_to_all(grads, ('zl', 'y'), split_axis=0, concat_axis=0, tiled=True)]
    dot_general x11 -> x0, matrix products: 20.9 us -> none  [the longest x2 6.96 us: inner_rows(): lax.dot_general(left, right, (((0,), (0,)), ((), ())), preferred_element_...]
    unnamed x53 -> x33, local copies, waits for them, and re-layouts: 36.3 us -> 15.5 us
    pallas_call x0 -> x7, Pallas kernels: none -> 19.4 us  [call(): pl.pallas_call(body, out_shape=[jax.ShapeDtypeStruct(s, d) for s, d in ou...]
    convert_element_type x5 -> x0, other arithmetic: 8.44 us -> none  [the longest x2 3.15 us: layer_normalize(): standardized_input.astype(jnp.bfloat16)]
  transfers between devices with their start and end apart: 5 -> 4, of which waited for: 4 -> 3; matrix products, arithmetic and copies ran while one was open for 10% -> 9% of each run, Pallas kernels for 0% -> 1%
where the time goes in v1:
time: 136 us; the launch traced here: 135 us
  blocking collectives  57.4 us (42%)
  waiting for transfers between devices  23.9 us (18%)
  local copies, waits for them, and re-layouts  22.3 us (16%)
  Pallas kernels  19.4 us (14%)
  starting transfers between devices  10.9 us (8%)
    all_to_all x1, blocking collectives, local(): lax.all_to_all(packed, ('x', 'zh'), split_axis=0, concat_axis=0, tiled=True)  34.1 us
    all_to_all x1, blocking collectives, local(): lax.all_to_all(mixed, ('x', 'zh'), split_axis=0, concat_axis=0, tiled=True)  23.3 us
    all_to_all x1, waiting for transfers between devices, local(): lax.all_to_all(grads, ('zl', 'y'), split_axis=0, concat_axis=0, tiled=True)  21.7 us
    pallas_call x7, Pallas kernels, call(): pl.pallas_call(body, out_shape=[jax.ShapeDtypeStruct(s, d) for s, d in ou...  19.4 us
    unnamed x33, local copies, waits for them, and re-layouts  15.5 us
    ppermute x3, starting transfers between devices, swap(): return lax.ppermute(v, 'c', [(0, 1), (1, 0)])  6.71 us
    all_to_all x1, starting transfers between devices, local(): lax.all_to_all(grads, ('zl', 'y'), split_axis=0, concat_axis=0, tiled=True)  4.2 us
    reshape x1, local copies, waits for them, and re-layouts, local(): lax.dynamic_slice(w_qkv.reshape(768, 3, 768), (0, 0, core * 384), (768, 3...  3.89 us
  transfers between devices with their start and end apart: 4, of which 3 were waited for; matrix products, arithmetic and copies ran while one was open for 9% of the time, Pallas kernels for 1%

profile of v1, /device:TPU:1, one launch (start us, length us, event | category | flops | bytes accessed | tf_op | source)
XLA Modules:
  0.0 134.7 jit_solution(2563471307418152945)
XLA Ops:
  0.6 0.0 copy-start
  0.7 1.1 copy-done.7
  1.7 1.0 copy-done.8
  2.7 0.7 copy-done.10
  3.4 0.4 shard_map.103
  3.8 34.1 %all_to_all.15.own_ref = bf16[16,32,768]{2,1,0:T(8,128)(2,1)S(1)} all-to-all(bf16[16,32,768]{2,1,0:T(8,128)(2,1)S(1)} %shard_map.103), channel_id=1, replica_groups=mesh['zh'=4,'x'=4,'c'=2,'zl'=2,'y'=4] {'x','zh'}, dimensions={0} | all-to-all | bytes 1572864 | tf_op jit(solution)/shard_map/all_to_all | solution.py:227
  37.9 3.0 %collective-permute-start = (bf16[16,32,768]{2,1,0:T(8,128)(2,1)S(1)}, bf16[16,32,768]{2,1,0:T(8,128)(2,1)S(1)}, u32[]{:S(2)}, u32[]{:S(2)}) collective-permute-start(bf16[16,32,768]{2,1,0:T(8,128)(2,1)S(1)} %all_to_all.15.own_ref), channel_id=1, source_target_pairs={{0,8},{8,0},{1,9},{9,1},{2,10},{10,2},{3,11},{11,3},{4,12},{12,4},... | collective-permute-start | bytes 2359304 | tf_op jit(solution)/shard_map/ppermute | solution.py:224
  40.8 5.8 %copy.11 = bf16[768,2304]{0,1:T(8,128)(2,1)} copy(bf16[768,2304]{1,0:T(8,128)(2,1)} %param.10) | data formatting | bytes 7077888 | tf_op args[2]
  46.6 2.8 %constant_dynamic-slice_fusion.1 = bf16[768,3,384]{0,2,1:T(8,128)(2,1)} fusion(bf16[768,3,768]{0,2,1:T(8,128)(2,1)} %bitcast.8, s32[]{:T(128)S(6)} %select_n.4), kind=kLoop, calls=%fused_computation.1 | loop fusion | bytes 3538948 | tf_op jit(solution)/shard_map/dynamic_slice | solution.py:229
  49.4 3.9 %copy.12.w_ref = bf16[768,1152]{1,0:T(8,128)(2,1)} copy(bf16[768,1152]{0,1:T(8,128)(2,1)} %bitcast.9) | data formatting | bytes 3538944 | tf_op jit(solution)/shard_map/reshape | solution.py:229
  53.4 0.0 collective-permute-done.oth_ref
  53.4 1.5 %copy-done.3 = bf16[768,1152]{1,0:T(8,128)(2,1)S(1)} copy-done((bf16[768,1152]{1,0:T(8,128)(2,1)S(1)}, bf16[768,1152]{1,0:T(8,128)(2,1)}, u32[]{:S(2)}) %copy-start.3) | copy-done | bytes 1769496
  54.9 14.9 %shard_map.104 = (bf16[8,384,384]{2,1,0:T(8,128)(2,1)}, bf16[512,1152]{1,0:T(8,128)(2,1)S(1)}) custom-call(bf16[16,32,768]{2,1,0:T(8,128)(2,1)S(1)} %all_to_all.15.own_ref, bf16[16,32,768]{2,1,0:T(8,128)(2,1)S(1)} %collective-permute-done.oth_ref, bf16[768,1152]{1,0:T(8,128)(2,1)S(1)} %copy-done.3, bf16[384,768]{1,0:T(8,128)(2,1)S(1)} %constant_dynamic-slice_fusion.wo_ref, ...), custom_call_target="tpu_custom_call" | custom-call | flops 6000000000 | bytes 10000000 | tf_op jit(solution)/shard_map/pallas_call | solution.py:27
  69.8 1.0 copy-done.14
  70.9 4.2 %all-to-all-start.1 = ((bf16[8,384,384]{2,1,0:T(8,128)(2,1)}), bf16[8,384,384]{2,1,0:T(8,128)(2,1)S(1)}, u32[]{:S(2)}, u32[]{:S(2)}) async-start(bf16[8,384,384]{2,1,0:T(8,128)(2,1)} %get-tuple-element.12), calls=%async_computation.1 | async-start | bytes 4718592 | tf_op jit(solution)/shard_map/all_to_all | solution.py:241
  75.1 1.5 %copy-done.4 = bf16[768,1152]{1,0:T(8,128)(2,1)S(1)} copy-done((bf16[768,1152]{1,0:T(8,128)(2,1)S(1)}, bf16[768,1152]{1,0:T(8,128)(2,1)}, u32[]{:S(2)}) %copy-start.4) | copy-done | bytes 1769496
  76.5 1.3 copy-done.15
  77.8 1.2 shard_map.105
  79.0 0.0 copy-start.9
  79.0 0.6 collective-permute-start.1
  79.7 1.3 %collective-permute-done.1.got_ref = bf16[256,768]{1,0:T(8,128)(2,1)S(1)} collective-permute-done((bf16[256,768]{1,0:T(8,128)(2,1)S(1)}, bf16[256,768]{1,0:T(8,128)(2,1)S(1)}, u32[]{:S(2)}, u32[]{:S(2)}) %collective-permute-start.1) | collective-permute-done | bytes 393248 | tf_op jit(solution)/shard_map/ppermute | solution.py:224
  81.0 0.6 shard_map.106.ig_ref
  81.6 0.0 copy-start.5
  81.6 0.7 copy-done.5
  82.4 21.7 %all-to-all-done.1.r_ref = bf16[8,384,384]{2,1,0:T(8,128)(2,1)S(1)} async-done(((bf16[8,384,384]{2,1,0:T(8,128)(2,1)}), bf16[8,384,384]{2,1,0:T(8,128)(2,1)S(1)}, u32[]{:S(2)}, u32[]{:S(2)}) %all-to-all-start.1) | async-done | bytes 2359328 | tf_op jit(solution)/shard_map/all_to_all | solution.py:241
  104.1 1.0 copy-done.6
  105.1 0.7 shard_map.107
  105.7 23.3 %all_to_all.16.r_ref = bf16[16,32,768]{2,1,0:T(8,128)(2,1)S(1)} all-to-all(bf16[16,32,768]{2,1,0:T(8,128)(2,1)S(1)} %shard_map.107), channel_id=1, replica_groups=mesh['zh'=4,'x'=4,'c'=2,'zl'=2,'y'=4] {'x','zh'}, dimensions={0} | all-to-all | bytes 1572864 | tf_op jit(solution)/shard_map/all_to_all | solution.py:248
  129.1 1.1 shard_map.108
  130.1 3.1 %collective-permute-start.2 = (f32[8,768]{1,0:T(8,128)S(1)}, f32[8,768]{1,0:T(8,128)S(1)}, u32[]{:S(2)}, u32[]{:S(2)}) collective-permute-start(f32[8,768]{1,0:T(8,128)S(1)} %get-tuple-element.18), channel_id=1, source_target_pairs={{0,8},{8,0},{1,9},{9,1},{2,10},{10,2},{3,11},{11,3},{4,12},{12,4},... | collective-permute-start | bytes 73736 | tf_op jit(solution)/shard_map/ppermute | solution.py:224
  133.2 0.8 collective-permute-done.2.got_ref
  134.1 0.6 shard_map.109
  (21 shorter events, 0.1 us)
Async XLA Ops:
  0.6 52.7 %copy-start = (bf16[768,768]{1,0:T(8,128)(2,1)S(1)}, bf16[768,768]{1,0:T(8,128)(2,1)}, u32[]{:S(2)}) copy-start(bf16[768,768]{1,0:T(8,128)(2,1)} %param.11) | copy-start | bytes 3538948
  0.6 1.1 copy-start.7
  1.7 1.0 copy-start.8
  2.7 0.7 copy-start.10
  37.9 15.5 %copy-start.1 = (bf16[16,32,768]{2,1,0:T(8,128)(2,1)}, bf16[16,32,768]{2,1,0:T(8,128)(2,1)S(1)}, u32[]{:S(2)}) copy-start(bf16[16,32,768]{2,1,0:T(8,128)(2,1)S(1)} %all_to_all.15.own_ref) | copy-start | bytes 2359300
  37.9 15.5 %collective-permute-start = (bf16[16,32,768]{2,1,0:T(8,128)(2,1)S(1)}, bf16[16,32,768]{2,1,0:T(8,128)(2,1)S(1)}, u32[]{:S(2)}, u32[]{:S(2)}) collective-permute-start(bf16[16,32,768]{2,1,0:T(8,128)(2,1)S(1)} %all_to_all.15.own_ref), channel_id=1, source_target_pairs={{0,8},{8,0},{1,9},{9,1},{2,10},{10,2},{3,11},{11,3},{4,12},{12,4},... | collective-permute-start | bytes 2359304 | tf_op jit(solution)/shard_map/ppermute | solution.py:224
  49.4 4.0 %copy-start.12 = (s32[1,768]{1,0:T(1,128)S(1)}, s32[1,768]{1,0:T(1,128)}, u32[]{:S(2)}) copy-start(s32[1,768]{1,0:T(1,128)} %constant.21.clone.feat_ref) | copy-start | bytes 9220
  49.4 4.0 %copy-start.13 = (s32[1,384]{1,0:T(1,128)S(1)}, s32[1,384]{1,0:T(1,128)}, u32[]{:S(2)}) copy-start(s32[1,384]{1,0:T(1,128)} %constant.22.clone.feat2_ref) | copy-start | bytes 4612
  53.4 1.5 %copy-start.3 = (bf16[768,1152]{1,0:T(8,128)(2,1)S(1)}, bf16[768,1152]{1,0:T(8,128)(2,1)}, u32[]{:S(2)}) copy-start(bf16[768,1152]{1,0:T(8,128)(2,1)} %copy.12.w_ref) | copy-start | bytes 5308420
  69.8 1.0 copy-start.14
  70.9 33.2 %all-to-all-start.1 = ((bf16[8,384,384]{2,1,0:T(8,128)(2,1)}), bf16[8,384,384]{2,1,0:T(8,128)(2,1)S(1)}, u32[]{:S(2)}, u32[]{:S(2)}) async-start(bf16[8,384,384]{2,1,0:T(8,128)(2,1)} %get-tuple-element.12), calls=%async_computation.1 | async-start | bytes 4718592 | tf_op jit(solution)/shard_map/all_to_all | solution.py:241
  75.1 1.5 %copy-start.4 = (bf16[768,1152]{1,0:T(8,128)(2,1)S(1)}, bf16[768,1152]{1,0:T(8,128)(2,1)}, u32[]{:S(2)}) copy-start(bf16[768,1152]{1,0:T(8,128)(2,1)} %copy.12.w_ref) | copy-start | bytes 5308420
  76.5 1.3 copy-start.15
  77.8 3.2 %copy-start.2 = (bf16[16,32,768]{2,1,0:T(8,128)(2,1)S(1)}, bf16[16,32,768]{2,1,0:T(8,128)(2,1)}, u32[]{:S(2)}) copy-start(bf16[16,32,768]{2,1,0:T(8,128)(2,1)} %copy-done.1) | copy-start | bytes 2359300
  79.0 25.0 %copy-start.9 = (s32[8,384]{1,0:T(8,128)S(1)}, s32[8,384]{1,0:T(8,128)}, u32[]{:S(2)}) copy-start(s32[8,384]{1,0:T(8,128)} %constant.23.clone.table_ref) | copy-start | bytes 36868
  79.0 2.0 %collective-permute-start.1 = (bf16[256,768]{1,0:T(8,128)(2,1)S(1)}, bf16[256,768]{1,0:T(8,128)(2,1)S(1)}, u32[]{:S(2)}, u32[]{:S(2)}) collective-permute-start(bf16[256,768]{1,0:T(8,128)(2,1)S(1)} %get-tuple-element.15), channel_id=1, source_target_pairs={{0,8},{8,0},{1,9},{9,1},{2,10},{10,2},{3,11},{11,3},{4,12},{12,4},... | collective-permute-start | bytes 1179656 | tf_op jit(solution)/shard_map/ppermute | solution.py:224
  81.6 0.7 copy-start.5
  104.1 1.0 copy-start.6
  105.1 24.0 %copy-start.11 = (s32[1,256]{1,0:T(1,128)S(1)}, s32[1,256]{1,0:T(1,128)}, u32[]{:S(2)}) copy-start(s32[1,256]{1,0:T(1,128)} %constant.20.clone.home_ref) | copy-start | bytes 3076
  130.1 3.9 %collective-permute-start.2 = (f32[8,768]{1,0:T(8,128)S(1)}, f32[8,768]{1,0:T(8,128)S(1)}, u32[]{:S(2)}, u32[]{:S(2)}) collective-permute-start(f32[8,768]{1,0:T(8,128)S(1)} %get-tuple-element.18), channel_id=1, source_target_pairs={{0,8},{8,0},{1,9},{9,1},{2,10},{10,2},{3,11},{11,3},{4,12},{12,4},... | collective-permute-start | bytes 73736 | tf_op jit(solution)/shard_map/ppermute | solution.py:224

commit v2 on v1

v2 whole, which is shorter than its diff:
```python
import jax
import jax.numpy as jnp
from jax import lax
from jax.experimental import pallas as pl
from jax.experimental.pallas import tpu as pltpu
from jax.sharding import Mesh, PartitionSpec as P

HEAD = 64
BF = jnp.bfloat16
F32 = jnp.float32
VM = pl.BlockSpec(memory_space=pltpu.VMEM)
SM = pl.BlockSpec(memory_space=pltpu.SMEM)
HB = pl.BlockSpec(memory_space=pltpu.HBM)


def nn(a, b):
    return lax.dot_general(a, b, (((1,), (0,)), ((), ())), preferred_element_type=F32)


def nt(a, b):
    return lax.dot_general(a, b, (((1,), (1,)), ((), ())), preferred_element_type=F32)


def call(body, outs, ins, scratch=(), smem=(), hbm=(), flops=0, nbytes=0, limit=16):
    space = {i: SM for i in smem} | {i: HB for i in hbm}
    return pl.pallas_call(
        body,
        out_shape=[jax.ShapeDtypeStruct(s, d) for s, d in outs],
        in_specs=[space.get(i, VM) for i in range(len(ins))],
        out_specs=[VM] * len(outs),
        scratch_shapes=list(scratch),
        compiler_params=pltpu.CompilerParams(vmem_limit_bytes=limit * 2**20),
        cost_estimate=pl.CostEstimate(flops=flops, bytes_accessed=nbytes, transcendentals=0),
    )(*ins)


def selection(rows, source):
    at = lax.broadcasted_iota(jnp.int32, (rows, source.shape[1]), 0)
    return (at == source).astype(F32).astype(BF)


def lanes(n):
    return lax.broadcasted_iota(jnp.int32, (1, n), 1)


def third(i):
    return (i * 21846) >> 16


def home_order():
    i = lanes(256)
    f, p = i >> 5, i & 31
    return ((p >> 1) << 4) + ((p & 1) << 3) + f


def feature_order(n, x0, y0):
    f = lanes(n)
    d = third(f)
    c = (d >> 3) & 1
    x, y = (((d >> 4) & 3) - x0) & 3, ((d & 3) - y0) & 3
    first, second = jnp.where(c == 0, x, y), jnp.where(c == 0, y, x)
    low = (d >> 6) * 6 + ((d >> 2) & 1) * 3 + (f - 3 * d)
    return c * (n // 2) + first * (n // 8) + second * (n // 32) + low


def split_order():
    i = lanes(384)
    m = jnp.where(i < 96, 0, jnp.where(i < 192, 1, 2))
    hh = jnp.where(i < 336, 0, 1)
    low, high = i - 96 * m, i - 288 - 48 * hh
    t1 = jnp.where(low < 24, 0, jnp.where(low < 48, 1, jnp.where(low < 72, 2, 3)))
    t2 = jnp.where(high < 12, 0, jnp.where(high < 24, 1, jnp.where(high < 36, 2, 3)))
    return jnp.where(i < 288, t1 * 72 + m * 24 + low, t2 * 84 + 72 + hh * 12 + high)


def slot_order(core):
    i = lanes(192)
    c = jnp.where(i < 96, 0, 1)
    i = i - 96 * c
    big = i < 72
    m = jnp.where(i < 24, 0, jnp.where(i < 48, 1, 2))
    hh = jnp.where(i < 84, 0, 1)
    rem = jnp.where(big, i - 24 * m, i - 72 - 12 * hh)
    d = third(rem)
    j = rem - 3 * d
    row = jnp.where(big, jnp.where(m < 2, j, 3 + (j >> 1)), 5 + j)
    half = jnp.where(big, jnp.where(m < 2, m, j & 1), hh)
    return ((d + jnp.where(big, 0, 4 * core)) << 4) + (c << 3) + row, half


def pack_body(x_ref, d_ref, o_ref, x_s, d_s, sems):
    copies = [pltpu.make_async_copy(r, s, sems.at[i]) for i, (r, s) in enumerate(((x_ref, x_s), (d_ref, d_s)))]
    for copy in copies:
        copy.start()
    sel = selection(256, home_order())
    copies[0].wait()
    o_ref[:, 0:16, :] = nn(sel, x_s[...]).astype(BF).reshape(16, 16, 768)
    copies[1].wait()
    o_ref[:, 16:32, :] = nn(sel, d_s[...]).astype(BF).reshape(16, 16, 768)


def rows_of(ref, first):
    start = first // 16 * 16
    block = ref[:, start : start + 16, :].astype(F32)
    return block[:, first - start : first - start + 8, :].reshape(128, 768)


def normalize(x):
    mean = jnp.mean(x, axis=1, keepdims=True)
    cen = x - mean
    inv = 1.0 / jnp.sqrt(jnp.mean(cen * cen, axis=1, keepdims=True) + 1e-05)
    return cen * inv, inv


def weight_copies(core, source, target, sems):
    copies = []
    for t in range(3):
        cols = pl.ds(pl.multiple_of(t * 768 + core * 384, 128), 384)
        copies.append(pltpu.make_async_copy(source.at[:, cols], target.at[:, t * 384 : (t + 1) * 384], sems.at[t]))
    return copies


def main_body(at_ref, own_ref, oth_ref, wqkv_ref, wout_ref, dqkv_ref, *rest):
    g_refs = rest[:8]
    (n_s, d_s, qkv_s, a_s, kt_s, vt_s, at_s, dqt_s, att_s, nt_s, w_ref, wo_ref,
     sems) = rest[8:]
    copies = weight_copies(at_ref[0], wqkv_ref, w_ref, sems)
    rows = pl.ds(pl.multiple_of(at_ref[0] * 384, 128), 384)
    copies.append(pltpu.make_async_copy(wout_ref.at[rows, :], wo_ref, sems.at[3]))
    for copy in copies:
        copy.start()
    for patch in range(2):
        for side, ref in enumerate((own_ref, oth_ref)):
            at = patch * 256 + side * 128
            n_s[at : at + 128, :] = normalize(rows_of(ref, patch * 8))[0].astype(BF)
            d_s[at : at + 128, :] = rows_of(ref, 16 + patch * 8).astype(BF)
    for t in range(3):
        copies[t].wait()
        qkv_s[:, t * 384 : (t + 1) * 384] = nn(n_s[...], w_ref[:, t * 384 : (t + 1) * 384]).astype(BF)
    copies[3].wait()
    a_s[...] = nt(d_s[...], wo_ref[...]).astype(BF)
    kt_s[...] = (qkv_s[:, 384:768] * 0.125).T
    vt_s[...] = qkv_s[:, 768:1152].T
    at_s[...] = a_s[...].T
    lane = lax.broadcasted_iota(jnp.int32, (1, 128), 1)

    keeps = [((lane >= h * HEAD) & (lane < (h + 1) * HEAD)).astype(F32).astype(BF) for h in range(2)]
    work = []
    for pair in range(3):
        for patch in range(2):
            rows, at = slice(patch * 256, (patch + 1) * 256), pair * 128
            q = qkv_s[rows, at : at + 128] * 0.125
            k = qkv_s[rows, 384 + at : 384 + at + 128]
            v = qkv_s[rows, 768 + at : 768 + at + 128]
            a = a_s[rows, at : at + 128]
            for h in range(2):
                work.append((rows, at, slice(at + h * HEAD, at + (h + 1) * HEAD), q * keeps[h], a * keeps[h], k, v))
    sts = [nt(k, qh) for _, _, _, qh, _, k, _ in work]
    dps = [nt(v, ah) for _, _, _, _, ah, _, v in work]
    ps = []
    for st in sts:
        e = jnp.exp(st - jnp.max(st, axis=0, keepdims=True))
        ps.append(e * (1.0 / jnp.sum(e, axis=0, keepdims=True)))
    pbs = [p.astype(BF) for p in ps]
    dss = []
    for (rows, _, hr, _, _, _, _), p, pb, dp in zip(work, ps, pbs, dps):
        attn = nn(vt_s[hr, rows], pb).astype(BF)
        att_s[hr, rows] = attn
        delta = jnp.sum(at_s[hr, rows].astype(F32) * attn.astype(F32), axis=0, keepdims=True)
        dss.append((p * (dp - delta)).astype(BF))
    for i in range(0, 12, 2):
        rows, at = work[i][:2]
        dv = nn(pbs[i], work[i][4]) + nn(pbs[i + 1], work[i + 1][4])
        dk = nn(dss[i], work[i][3]) + nn(dss[i + 1], work[i + 1][3])
        dqkv_ref[rows, 768 + at : 768 + at + 128] = dv.astype(BF)
        dqkv_ref[rows, 384 + at : 384 + at + 128] = dk.astype(BF)
    for (rows, _, hr, _, _, _, _), ds in zip(work, dss):
        dqt_s[hr, rows] = nn(kt_s[hr, rows], ds).astype(BF)
    dqkv_ref[:, 0:384] = dqt_s[...].T
    nt_s[...] = nt(selection(768, feature_order(768, at_ref[1], at_ref[2])), n_s[...]).astype(BF)
    for t in range(3):
        g = nn(nt_s[...], dqkv_ref[:, t * 384 : (t + 1) * 384]).astype(BF)
        for i, ref in enumerate(g_refs):
            ref[t * 96 : (t + 1) * 96, :] = g[i * 96 : (i + 1) * 96]
    attp = nn(selection(384, feature_order(384, at_ref[1], at_ref[2])), att_s[...]).astype(BF)
    for t in range(2):
        g = nn(attp, d_s[:, t * 384 : (t + 1) * 384]).astype(BF)
        for i, ref in enumerate(g_refs):
            ref[288 + t * 48 : 288 + (t + 1) * 48, :] = g[i * 48 : (i + 1) * 48]


def dnormed_body(at_ref, dqkv_ref, wqkv_ref, mine_ref, theirs_ref, w_ref, sems):
    copies = weight_copies(at_ref[0], wqkv_ref, w_ref, sems)
    for copy in copies:
        copy.start()
    for copy in copies:
        copy.wait()
    part = nt(dqkv_ref[...], w_ref[...])
    for patch in range(2):
        mine_ref[patch * 128 : (patch + 1) * 128, :] = part[patch * 256 : patch * 256 + 128]
        theirs_ref[patch * 128 : (patch + 1) * 128, :] = part[patch * 256 + 128 : patch * 256 + 256].astype(BF)


def input_gradient_body(part_ref, got_ref, own_ref, o_ref):
    outs = []
    for patch in range(2):
        xhat, inv = normalize(rows_of(own_ref, patch * 8))
        dout = rows_of(own_ref, 16 + patch * 8)
        at = pl.ds(patch * 128, 128)
        dn = part_ref[at, :] + got_ref[at, :].astype(F32)
        first = jnp.mean(dn, axis=1, keepdims=True)
        second = jnp.mean(dn * xhat, axis=1, keepdims=True)
        outs.append((dout + inv * (dn - first - xhat * second)).reshape(16, 8, 768))
    o_ref[...] = jnp.concatenate(outs, axis=1).astype(BF)


def added(refs):
    total = refs[0][...].astype(F32)
    for ref in refs[1:]:
        total = total + ref[...].astype(F32)
    return total.astype(BF)


def split_body(*refs):
    sel = selection(384, split_order())
    for half in range(2):
        out = nn(sel, added(refs[half * 4 : half * 4 + 4])).astype(BF)
        for t in range(4):
            refs[8 + half * 4 + t][...] = out[t * 96 : (t + 1) * 96]


def slot_body(at_ref, back_ref, *refs):
    total = jnp.concatenate([added(refs[0:4]), added(refs[4:8])], axis=0)
    slot, half = slot_order(at_ref[0])
    for h in range(2):
        part = nn(selection(128, jnp.where(half == h, slot, -1)), total).astype(BF)
        refs[8][:, :, h * 384 : (h + 1) * 384] = part.reshape(8, 16, 384)


def home_body(r_ref, ig_ref):
    sel = selection(256, home_order())
    back = lax.dot_general(
        sel, r_ref[...].reshape(256, 768), (((0,), (0,)), ((), ())), preferred_element_type=F32
    )
    ig_ref[...] = back.astype(BF)


def sum_body(at_ref, r_ref, own_ref, oth_ref):
    total = r_ref[0].astype(F32)
    for s in range(1, 8):
        total = total + r_ref[s].astype(F32)
    low = at_ref[0] == 0
    own_ref[...] = jnp.where(low, total[0:8], total[8:16])
    oth_ref[...] = jnp.where(low, total[8:16], total[0:8])


def last_body(at_ref, own_ref, got_ref, gq_ref, go_ref):
    own, got = own_ref[...], got_ref[...]
    low = at_ref[0] == 0
    halves = (jnp.where(low, own, got), jnp.where(low, got, own))
    for h, m in enumerate(halves):
        at = h * 384
        gq_ref[:, at : at + 384] = m[0:3, 0:384]
        gq_ref[:, 768 + at : 768 + at + 384] = m[0:3, 384:768]
        gq_ref[0:1, 1536 + at : 1536 + at + 384] = m[3:4, 0:384]
        gq_ref[1:2, 1536 + at : 1536 + at + 384] = m[3:4, 384:768]
        gq_ref[2:3, 1536 + at : 1536 + at + 384] = m[4:5, 0:384]
    go_ref[...] = own[5:8] + got[5:8]


def local(x, d, w_qkv, w_out):
    at = jnp.stack([lax.axis_index("c"), lax.axis_index("x"), lax.axis_index("y")]).astype(jnp.int32)

    def swap(v):
        return lax.ppermute(v, "c", [(0, 1), (1, 0)])

    def spread(blocks, axis):
        return [blocks[0]] + [
            lax.ppermute(blocks[s], axis, [(i, (i + s) % 4) for i in range(4)]) for s in (2, 1, 3)
        ]

    scr = lambda *s: pltpu.VMEM(s, BF)
    packed, = call(
        pack_body,
        [((16, 32, 768), BF)],
        [x.reshape(256, 768), d.reshape(256, 768)],
        scratch=[scr(256, 768), scr(256, 768), pltpu.SemaphoreType.DMA((2,))],
        hbm=(0, 1),
        limit=63,
    )
    own = lax.all_to_all(packed, ("x", "zh"), split_axis=0, concat_axis=0, tiled=True)
    oth = swap(own)
    dqkv, *grads = call(
        main_body,
        [((512, 1152), BF)] + [((384, 384), BF)] * 8,
        [at, own, oth, w_qkv, w_out],
        scratch=[scr(512, 768), scr(512, 768), scr(512, 1152), scr(512, 384), scr(384, 512),
                 scr(384, 512), scr(384, 512), scr(384, 512), scr(384, 512), scr(768, 512), scr(768, 1152),
                 scr(384, 768), pltpu.SemaphoreType.DMA((4,))],
        smem=(0,),
        hbm=(3, 4),
        limit=58,
        flops=6 * 10**9,
        nbytes=10**7,
    )
    first = spread(grads[:4], "x") + spread(grads[4:], "y")
    mine, theirs = call(
        dnormed_body,
        [((256, 768), F32), ((256, 768), BF)],
        [at, dqkv, w_qkv],
        scratch=[scr(768, 1152), pltpu.SemaphoreType.DMA((3,))],
        smem=(0,),
        hbm=(2,),
        flops=10**9,
        nbytes=5 * 10**6,
        limit=16,
    )
    got = swap(theirs)
    ig, = call(input_gradient_body, [((16, 16, 768), BF)], [mine, got, own], nbytes=3 * 10**6)
    back = lax.all_to_all(ig, ("x", "zh"), split_axis=0, concat_axis=0, tiled=True)
    second = call(split_body, [((96, 384), BF)] * 8, first, flops=4_000_000_000)
    second = spread(second[:4], "y") + spread(second[4:], "x")
    slots, = call(slot_body, [((8, 16, 768), BF)], [at, back, *second], smem=(0,), hbm=(1,))
    ig_home, = call(home_body, [((256, 768), BF)], [back])
    last = lax.all_to_all(slots, ("zh", "zl"), split_axis=0, concat_axis=0, tiled=True)
    own8, oth8 = call(sum_body, [((8, 768), F32)] * 2, [at, last], smem=(0,))
    grad_qkv, grad_out = call(
        last_body, [((3, 2304), F32), ((3, 768), F32)], [at, own8, swap(oth8)], smem=(0,)
    )
    return ig_home.reshape(8, 32, 768), grad_qkv, grad_out


def solution(mesh):
    fine = Mesh(mesh.devices.reshape(4, 4, 2, 2, 4), ("zh", "x", "c", "zl", "y"))
    tm, space = ("zh", "x", "c"), ("zl", "y")
    tokens, rows = P(tm, space, None), P(tm + space, None)
    return jax.shard_map(
        local,
        mesh=fine,
        in_specs=(tokens, tokens, P(), P()),
        out_specs=(tokens, rows, rows),
        check_vma=False,
    )
```

time: 136 us -> 115 us (0.85)
  local copies, waits for them, and re-layouts: 22.3 us -> 2.18 us
  starting transfers between devices: 10.9 us -> 30.5 us
  waiting for transfers between devices: 23.9 us -> 10.5 us
  blocking collectives: 57.4 us -> 47.8 us
  Pallas kernels: 19.4 us -> 22.1 us
    all_to_all x1, waiting for transfers between devices: 21.7 us -> 0.01 us  [local(): lax.all_to_all(ig, ('x', 'zh'), split_axis=0, concat_axis=0, tiled=True)]
    ppermute x0 -> x12, starting transfers between devices: none -> 17.4 us  [spread(): lax.ppermute(blocks[s], axis, [(i, (i + s) % 4) for i in range(4)])]
    unnamed x33 -> x20, local copies, waits for them, and re-layouts: 15.5 us -> 2.18 us
    all_to_all x1, blocking collectives: 23.3 us -> 13.6 us  [local(): lax.all_to_all(slots, ('zh', 'zl'), split_axis=0, concat_axis=0, tiled=True)]
    ppermute x0 -> x12, waiting for transfers between devices: none -> 9.18 us  [spread(): lax.ppermute(blocks[s], axis, [(i, (i + s) % 4) for i in range(4)])]
    reshape x1 -> x0, local copies, waits for them, and re-layouts: 3.89 us -> none  [local(): lax.dynamic_slice(w_qkv.reshape(768, 3, 768), (0, 0, core * 384), (768, 3...]
    ppermute x3, starting transfers between devices: 6.71 us -> 9.59 us  [swap(): return lax.ppermute(v, 'c', [(0, 1), (1, 0)])]
    dynamic_slice x2 -> x0, local copies, waits for them, and re-layouts: 2.86 us -> none  [the longest x1 2.82 us: local(): lax.dynamic_slice(w_qkv.reshape(768, 3, 768), (0, 0, core * 384), (768, 3...]
  transfers between devices with their start and end apart: 4 -> 16, of which waited for: 3 -> 8; matrix products, arithmetic and copies ran while one was open for 9% -> 1% of each run, Pallas kernels for 1% -> 3%
where the time goes in v2:
time: 115 us; the launch traced here: 114 us
  blocking collectives  47.8 us (42%)
  starting transfers between devices  30.5 us (27%)
  Pallas kernels  22.1 us (19%)
  waiting for transfers between devices  10.5 us (9%)
  local copies, waits for them, and re-layouts  2.18 us (2%)
    all_to_all x1, blocking collectives, local(): lax.all_to_all(packed, ('x', 'zh'), split_axis=0, concat_axis=0, tiled=True)  34.3 us
    pallas_call x9, Pallas kernels, call(): pl.pallas_call(body, out_shape=[jax.ShapeDtypeStruct(s, d) for s, d in ou...  22.1 us
    ppermute x12, starting transfers between devices, spread(): lax.ppermute(blocks[s], axis, [(i, (i + s) % 4) for i in range(4)])  17.4 us
    all_to_all x1, blocking collectives, local(): lax.all_to_all(slots, ('zh', 'zl'), split_axis=0, concat_axis=0, tiled=True)  13.6 us
    ppermute x3, starting transfers between devices, swap(): return lax.ppermute(v, 'c', [(0, 1), (1, 0)])  9.59 us
    ppermute x12, waiting for transfers between devices, spread(): lax.ppermute(blocks[s], axis, [(i, (i + s) % 4) for i in range(4)])  9.18 us
    all_to_all x1, starting transfers between devices, local(): lax.all_to_all(ig, ('x', 'zh'), split_axis=0, concat_axis=0, tiled=True)  3.55 us
  transfers between devices with their start and end apart: 16, of which 8 were waited for; matrix products, arithmetic and copies ran while one was open for 1% of the time, Pallas kernels for 3%

profile of v2, /device:TPU:1, one launch (start us, length us, event | category | flops | bytes accessed | tf_op | source)
XLA Modules:
  0.0 114.4 jit_solution(14865175957933898586)
XLA Ops:
  0.6 2.5 %shard_map.67 = bf16[16,32,768]{2,1,0:T(8,128)(2,1)} custom-call(bf16[256,768]{1,0:T(8,128)(2,1)} %bitcast.7, bf16[256,768]{1,0:T(8,128)(2,1)} %bitcast.8), custom_call_target="tpu_custom_call" | custom-call | tf_op jit(solution)/shard_map/pallas_call | solution.py:26
  3.1 34.3 %all_to_all.15.own_ref = bf16[16,32,768]{2,1,0:T(8,128)(2,1)S(1)} all-to-all(bf16[16,32,768]{2,1,0:T(8,128)(2,1)} %shard_map.67), channel_id=1, replica_groups=mesh['zh'=4,'x'=4,'c'=2,'zl'=2,'y'=4] {'x','zh'}, dimensions={0} | all-to-all | bytes 1572864 | tf_op jit(solution)/shard_map/all_to_all | solution.py:291
  37.4 3.0 %collective-permute-start = (bf16[16,32,768]{2,1,0:T(8,128)(2,1)S(1)}, bf16[16,32,768]{2,1,0:T(8,128)(2,1)S(1)}, u32[]{:S(2)}, u32[]{:S(2)}) collective-permute-start(bf16[16,32,768]{2,1,0:T(8,128)(2,1)S(1)} %all_to_all.15.own_ref), channel_id=1, source_target_pairs={{0,8},{8,0},{1,9},{9,1},{2,10},{10,2},{3,11},{11,3},{4,12},{12,4},... | collective-permute-start | bytes 2359304 | tf_op jit(solution)/shard_map/ppermute | solution.py:275
  40.4 0.6 pad_add_fusion.at_ref
  41.0 1.3 %collective-permute-done.oth_ref = bf16[16,32,768]{2,1,0:T(8,128)(2,1)S(1)} collective-permute-done((bf16[16,32,768]{2,1,0:T(8,128)(2,1)S(1)}, bf16[16,32,768]{2,1,0:T(8,128)(2,1)S(1)}, u32[]{:S(2)}, u32[]{:S(2)}) %collective-permute-start) | collective-permute-done | bytes 786464 | tf_op jit(solution)/shard_map/ppermute | solution.py:275
  42.3 0.9 copy-done.7
  43.2 12.0 %shard_map.68 = (bf16[512,1152]{1,0:T(8,128)(2,1)}, bf16[384,384]{1,0:T(8,128)(2,1)}, bf16[384,384]{1,0:T(8,128)(2,1)}, bf16[384,384]{1,0:T(8,128)(2,1)}, bf16[3...) custom-call(s32[3]{0:T(128)} %pad_add_fusion.at_ref, ...), custom_call_target="tpu_custom_call" | custom-call | flops 6000000000 | bytes 10000000 | tf_op jit(solution)/shard_map/pallas_call | solution.py:26
  55.2 1.3 %copy-done.3 = bf16[512,1152]{1,0:T(8,128)(2,1)S(1)} copy-done((bf16[512,1152]{1,0:T(8,128)(2,1)S(1)}, bf16[512,1152]{1,0:T(8,128)(2,1)}, u32[]{:S(2)}) %copy-start.3) | copy-done | bytes 1179672
  56.5 2.0 %shard_map.69 = (f32[256,768]{1,0:T(8,128)S(1)}, bf16[256,768]{1,0:T(8,128)(2,1)S(1)}) custom-call(s32[3]{0:T(128)S(1)} %copy-done.4, bf16[512,1152]{1,0:T(8,128)(2,1)S(1)} %copy-done.3, bf16[768,2304]{1,0:T(8,128)(2,1)S(1)} %copy-done), custom_call_target="tpu_custom_call" | custom-call | flops 1000000000 | bytes 5000000 | tf_op jit(solution)/shard_map/pallas_call | solution.py:26
  60.1 2.1 %collective-permute-start.4 = (bf16[384,384]{1,0:T(8,128)(2,1)}, bf16[384,384]{1,0:T(8,128)(2,1)S(1)}, u32[]{:S(2)}, u32[]{:S(2)}) collective-permute-start(bf16[384,384]{1,0:T(8,128)(2,1)} %get-tuple-element.32), channel_id=1, source_target_pairs={{0,48},{16,0},{32,16},{48,32},{1,49},{17,1},{33,17},{49,33},{2,50}... | collective-permute-start | bytes 884744 | tf_op jit(solution)/shard_map/ppermute | solution.py:279
  62.2 2.9 %collective-permute-start.5 = (bf16[384,384]{1,0:T(8,128)(2,1)}, bf16[384,384]{1,0:T(8,128)(2,1)S(1)}, u32[]{:S(2)}, u32[]{:S(2)}) collective-permute-start(bf16[384,384]{1,0:T(8,128)(2,1)} %get-tuple-element.34), channel_id=1, source_target_pairs={{0,2},{1,3},{2,0},{3,1},{4,6},{5,7},{6,4},{7,5},{8,10},{9,11},{10,... | collective-permute-start | bytes 884744 | tf_op jit(solution)/shard_map/ppermute | solution.py:279
  65.1 3.8 %collective-permute-done.2.refs_1_ = bf16[384,384]{1,0:T(8,128)(2,1)S(1)} collective-permute-done((bf16[384,384]{1,0:T(8,128)(2,1)S(1)}, bf16[384,384]{1,0:T(8,128)(2,1)S(1)}, u32[]{:S(2)}, u32[]{:S(2)}) %collective-permute-start.2) | collective-permute-done | bytes 294944 | tf_op jit(solution)/shard_map/ppermute | solution.py:279
  68.9 1.3 %collective-permute-start.6 = (bf16[384,384]{1,0:T(8,128)(2,1)}, bf16[384,384]{1,0:T(8,128)(2,1)S(1)}, u32[]{:S(2)}, u32[]{:S(2)}) collective-permute-start(bf16[384,384]{1,0:T(8,128)(2,1)} %get-tuple-element.35), channel_id=1, source_target_pairs={{0,1},{1,2},{2,3},{3,0},{4,5},{5,6},{6,7},{7,4},{8,9},{9,10},{10,1... | collective-permute-start | bytes 884744 | tf_op jit(solution)/shard_map/ppermute | solution.py:279
  70.2 1.5 %collective-permute-start.7 = (bf16[384,384]{1,0:T(8,128)(2,1)S(1)}, bf16[384,384]{1,0:T(8,128)(2,1)S(1)}, u32[]{:S(2)}, u32[]{:S(2)}) collective-permute-start(bf16[384,384]{1,0:T(8,128)(2,1)S(1)} %copy-done.8), channel_id=1, source_target_pairs={{0,3},{1,0},{2,1},{3,2},{4,7},{5,4},{6,5},{7,6},{8,11},{9,8},{10,9... | collective-permute-start | bytes 884744 | tf_op jit(solution)/shard_map/ppermute | solution.py:279
  71.8 1.3 %shard_map.70 = bf16[16,16,768]{2,1,0:T(8,128)(2,1)} custom-call(f32[256,768]{1,0:T(8,128)S(1)} %get-tuple-element.27.part_ref, bf16[256,768]{1,0:T(8,128)(2,1)S(1)} %collective-permute-done.1.got_ref, bf16[16,32,768]{2,1,0:T(8,128)(2,1)S(1)} %copy-done.2), custom_call_target="tpu_custom_call" | custom-call | bytes 3000000 | tf_op jit(solution)/shard_map/pallas_call | solution.py:26
  73.1 3.6 %all-to-all-start.1 = ((bf16[16,16,768]{2,1,0:T(8,128)(2,1)}), bf16[16,16,768]{2,1,0:T(8,128)(2,1)S(1)}, u32[]{:S(2)}, u32[]{:S(2)}) async-start(bf16[16,16,768]{2,1,0:T(8,128)(2,1)} %shard_map.70), calls=%async_computation.1 | async-start | bytes 786432 | tf_op jit(solution)/shard_map/all_to_all | solution.py:320
  76.7 0.8 collective-permute-done.6.refs_6_
  77.6 0.7 shard_map.72
  78.3 2.5 %collective-permute-start.10 = (bf16[96,384]{1,0:T(8,128)(2,1)S(1)}, bf16[96,384]{1,0:T(8,128)(2,1)S(1)}, u32[]{:S(2)}, u32[]{:S(2)}) collective-permute-start(bf16[96,384]{1,0:T(8,128)(2,1)S(1)} %get-tuple-element.40), channel_id=1, source_target_pairs={{0,3},{1,0},{2,1},{3,2},{4,7},{5,4},{6,5},{7,6},{8,11},{9,8},{10,9... | collective-permute-start | bytes 221192 | tf_op jit(solution)/shard_map/ppermute | solution.py:279
  80.8 1.8 %collective-permute-start.11 = (bf16[96,384]{1,0:T(8,128)(2,1)S(1)}, bf16[96,384]{1,0:T(8,128)(2,1)S(1)}, u32[]{:S(2)}, u32[]{:S(2)}) collective-permute-start(bf16[96,384]{1,0:T(8,128)(2,1)S(1)} %get-tuple-element.42), channel_id=1, source_target_pairs={{0,32},{16,48},{32,0},{48,16},{1,33},{17,49},{33,1},{49,17},{2,34}... | collective-permute-start | bytes 221192 | tf_op jit(solution)/shard_map/ppermute | solution.py:279
  82.6 2.7 %collective-permute-start.13 = (bf16[96,384]{1,0:T(8,128)(2,1)S(1)}, bf16[96,384]{1,0:T(8,128)(2,1)S(1)}, u32[]{:S(2)}, u32[]{:S(2)}) collective-permute-start(bf16[96,384]{1,0:T(8,128)(2,1)S(1)} %get-tuple-element.44), channel_id=1, source_target_pairs={{0,48},{16,0},{32,16},{48,32},{1,49},{17,1},{33,17},{49,33},{2,50}... | collective-permute-start | bytes 221192 | tf_op jit(solution)/shard_map/ppermute | solution.py:279
  85.3 0.6 collective-permute-start.8
  85.9 0.8 collective-permute-start.9
  86.7 1.1 collective-permute-done.12.refs_6_
  87.7 1.2 %collective-permute-done.13.refs_7_ = bf16[96,384]{1,0:T(8,128)(2,1)S(1)} collective-permute-done((bf16[96,384]{1,0:T(8,128)(2,1)S(1)}, bf16[96,384]{1,0:T(8,128)(2,1)S(1)}, u32[]{:S(2)}, u32[]{:S(2)}) %collective-permute-start.13) | collective-permute-done | bytes 73760 | tf_op jit(solution)/shard_map/ppermute | solution.py:279
  89.0 1.3 %collective-permute-done.8.refs_1_ = bf16[96,384]{1,0:T(8,128)(2,1)S(1)} collective-permute-done((bf16[96,384]{1,0:T(8,128)(2,1)S(1)}, bf16[96,384]{1,0:T(8,128)(2,1)S(1)}, u32[]{:S(2)}, u32[]{:S(2)}) %collective-permute-start.8) | collective-permute-done | bytes 73760 | tf_op jit(solution)/shard_map/ppermute | solution.py:279
  90.3 0.8 collective-permute-done.9.refs_2_
  91.1 0.8 shard_map.73
  91.9 13.6 %all_to_all.16.r_ref = bf16[8,16,768]{2,1,0:T(8,128)(2,1)S(1)} all-to-all(bf16[8,16,768]{2,1,0:T(8,128)(2,1)S(1)} %shard_map.73), channel_id=1, replica_groups=mesh['zh'=4,'x'=4,'c'=2,'zl'=2,'y'=4] {'zh','zl'}, dimensions={0} | all-to-all | bytes 393216 | tf_op jit(solution)/shard_map/all_to_all | solution.py:325
  106.0 6.1 %collective-permute-start.14 = (f32[8,768]{1,0:T(8,128)S(1)}, f32[8,768]{1,0:T(8,128)S(1)}, u32[]{:S(2)}, u32[]{:S(2)}) collective-permute-start(f32[8,768]{1,0:T(8,128)S(1)} %get-tuple-element.46), channel_id=1, source_target_pairs={{0,8},{8,0},{1,9},{9,1},{2,10},{10,2},{3,11},{11,3},{4,12},{12,4},... | collective-permute-start | bytes 73736 | tf_op jit(solution)/shard_map/ppermute | solution.py:275
  112.2 1.1 shard_map.71
  113.3 1.2 %shard_map.75 = (f32[3,2304]{1,0:T(4,128)}, f32[3,768]{1,0:T(4,128)}) custom-call(s32[3]{0:T(128)S(1)} %copy-done.4, f32[8,768]{1,0:T(8,128)S(1)} %get-tuple-element.45.own_ref, f32[8,768]{1,0:T(8,128)S(1)} %collective-permute-done.14.got_ref), custom_call_target="tpu_custom_call" | custom-call | tf_op jit(solution)/shard_map/pallas_call | solution.py:26
  (32 shorter events, 2.4 us)
Async XLA Ops:
  37.4 4.9 %copy-start.1 = (bf16[16,32,768]{2,1,0:T(8,128)(2,1)}, bf16[16,32,768]{2,1,0:T(8,128)(2,1)S(1)}, u32[]{:S(2)}) copy-start(bf16[16,32,768]{2,1,0:T(8,128)(2,1)S(1)} %all_to_all.15.own_ref) | copy-start | bytes 2359300
  37.4 4.9 %collective-permute-start = (bf16[16,32,768]{2,1,0:T(8,128)(2,1)S(1)}, bf16[16,32,768]{2,1,0:T(8,128)(2,1)S(1)}, u32[]{:S(2)}, u32[]{:S(2)}) collective-permute-start(bf16[16,32,768]{2,1,0:T(8,128)(2,1)S(1)} %all_to_all.15.own_ref), channel_id=1, source_target_pairs={{0,8},{8,0},{1,9},{9,1},{2,10},{10,2},{3,11},{11,3},{4,12},{12,4},... | collective-permute-start | bytes 2359304 | tf_op jit(solution)/shard_map/ppermute | solution.py:275
  41.0 14.2 %copy-start = (bf16[768,2304]{1,0:T(8,128)(2,1)S(1)}, bf16[768,2304]{1,0:T(8,128)(2,1)}, u32[]{:S(2)}) copy-start(bf16[768,2304]{1,0:T(8,128)(2,1)} %wqkv_ref.3) | copy-start | bytes 10616836
  41.0 14.2 %copy-start.4 = (s32[3]{0:T(128)S(1)}, s32[3]{0:T(128)}, u32[]{:S(2)}) copy-start(s32[3]{0:T(128)} %pad_add_fusion.at_ref) | copy-start | bytes 40
  42.3 0.9 copy-start.7
  55.2 1.3 %copy-start.3 = (bf16[512,1152]{1,0:T(8,128)(2,1)S(1)}, bf16[512,1152]{1,0:T(8,128)(2,1)}, u32[]{:S(2)}) copy-start(bf16[512,1152]{1,0:T(8,128)(2,1)} %get-tuple-element.26.dqkv_ref) | copy-start | bytes 3538948
  56.5 2.5 %copy-start.9 = (bf16[384,384]{1,0:T(8,128)(2,1)S(1)}, bf16[384,384]{1,0:T(8,128)(2,1)}, u32[]{:S(2)}) copy-start(bf16[384,384]{1,0:T(8,128)(2,1)} %get-tuple-element.30) | copy-start | bytes 884740
  56.5 13.8 %copy-start.8 = (bf16[384,384]{1,0:T(8,128)(2,1)S(1)}, bf16[384,384]{1,0:T(8,128)(2,1)}, u32[]{:S(2)}) copy-start(bf16[384,384]{1,0:T(8,128)(2,1)} %get-tuple-element.36) | copy-start | bytes 884740
  56.5 15.3 %copy-start.2 = (bf16[16,32,768]{2,1,0:T(8,128)(2,1)S(1)}, bf16[16,32,768]{2,1,0:T(8,128)(2,1)}, u32[]{:S(2)}) copy-start(bf16[16,32,768]{2,1,0:T(8,128)(2,1)} %copy-done.1) | copy-start | bytes 2359300
  58.5 11.8 %collective-permute-start.1 = (bf16[256,768]{1,0:T(8,128)(2,1)S(1)}, bf16[256,768]{1,0:T(8,128)(2,1)S(1)}, u32[]{:S(2)}, u32[]{:S(2)}) collective-permute-start(bf16[256,768]{1,0:T(8,128)(2,1)S(1)} %get-tuple-element.28), channel_id=1, source_target_pairs={{0,8},{8,0},{1,9},{9,1},{2,10},{10,2},{3,11},{11,3},{4,12},{12,4},... | collective-permute-start | bytes 1179656 | tf_op jit(solution)/shard_map/ppermute | solution.py:275
  58.9 10.0 %collective-permute-start.2 = (bf16[384,384]{1,0:T(8,128)(2,1)S(1)}, bf16[384,384]{1,0:T(8,128)(2,1)S(1)}, u32[]{:S(2)}, u32[]{:S(2)}) collective-permute-start(bf16[384,384]{1,0:T(8,128)(2,1)S(1)} %copy-done.9), channel_id=1, source_target_pairs={{0,32},{16,48},{32,0},{48,16},{1,33},{17,49},{33,1},{49,17},{2,34}... | collective-permute-start | bytes 884744 | tf_op jit(solution)/shard_map/ppermute | solution.py:279
  59.5 17.1 %collective-permute-start.3 = (bf16[384,384]{1,0:T(8,128)(2,1)}, bf16[384,384]{1,0:T(8,128)(2,1)S(1)}, u32[]{:S(2)}, u32[]{:S(2)}) collective-permute-start(bf16[384,384]{1,0:T(8,128)(2,1)} %get-tuple-element.31), channel_id=1, source_target_pairs={{0,16},{16,32},{32,48},{48,0},{1,17},{17,33},{33,49},{49,1},{2,18}... | collective-permute-start | bytes 884744 | tf_op jit(solution)/shard_map/ppermute | solution.py:279
  60.1 16.6 %collective-permute-start.4 = (bf16[384,384]{1,0:T(8,128)(2,1)}, bf16[384,384]{1,0:T(8,128)(2,1)S(1)}, u32[]{:S(2)}, u32[]{:S(2)}) collective-permute-start(bf16[384,384]{1,0:T(8,128)(2,1)} %get-tuple-element.32), channel_id=1, source_target_pairs={{0,48},{16,0},{32,16},{48,32},{1,49},{17,1},{33,17},{49,33},{2,50}... | collective-permute-start | bytes 884744 | tf_op jit(solution)/shard_map/ppermute | solution.py:279
  62.2 14.5 %collective-permute-start.5 = (bf16[384,384]{1,0:T(8,128)(2,1)}, bf16[384,384]{1,0:T(8,128)(2,1)S(1)}, u32[]{:S(2)}, u32[]{:S(2)}) collective-permute-start(bf16[384,384]{1,0:T(8,128)(2,1)} %get-tuple-element.34), channel_id=1, source_target_pairs={{0,2},{1,3},{2,0},{3,1},{4,6},{5,7},{6,4},{7,5},{8,10},{9,11},{10,... | collective-permute-start | bytes 884744 | tf_op jit(solution)/shard_map/ppermute | solution.py:279
  68.9 8.5 %collective-permute-start.6 = (bf16[384,384]{1,0:T(8,128)(2,1)}, bf16[384,384]{1,0:T(8,128)(2,1)S(1)}, u32[]{:S(2)}, u32[]{:S(2)}) collective-permute-start(bf16[384,384]{1,0:T(8,128)(2,1)} %get-tuple-element.35), channel_id=1, source_target_pairs={{0,1},{1,2},{2,3},{3,0},{4,5},{5,6},{6,7},{7,4},{8,9},{9,10},{10,1... | collective-permute-start | bytes 884744 | tf_op jit(solution)/shard_map/ppermute | solution.py:279
  70.2 7.4 %collective-permute-start.7 = (bf16[384,384]{1,0:T(8,128)(2,1)S(1)}, bf16[384,384]{1,0:T(8,128)(2,1)S(1)}, u32[]{:S(2)}, u32[]{:S(2)}) collective-permute-start(bf16[384,384]{1,0:T(8,128)(2,1)S(1)} %copy-done.8), channel_id=1, source_target_pairs={{0,3},{1,0},{2,1},{3,2},{4,7},{5,4},{6,5},{7,6},{8,11},{9,8},{10,9... | collective-permute-start | bytes 884744 | tf_op jit(solution)/shard_map/ppermute | solution.py:279
  71.8 5.8 %copy-start.5 = (bf16[384,384]{1,0:T(8,128)(2,1)S(1)}, bf16[384,384]{1,0:T(8,128)(2,1)}, u32[]{:S(2)}) copy-start(bf16[384,384]{1,0:T(8,128)(2,1)} %get-tuple-element.29.refs_0_) | copy-start | bytes 884740
  71.8 5.8 %copy-start.6 = (bf16[384,384]{1,0:T(8,128)(2,1)S(1)}, bf16[384,384]{1,0:T(8,128)(2,1)}, u32[]{:S(2)}) copy-start(bf16[384,384]{1,0:T(8,128)(2,1)} %get-tuple-element.33.refs_4_) | copy-start | bytes 884740
  73.1 18.0 %all-to-all-start.1 = ((bf16[16,16,768]{2,1,0:T(8,128)(2,1)}), bf16[16,16,768]{2,1,0:T(8,128)(2,1)S(1)}, u32[]{:S(2)}, u32[]{:S(2)}) async-start(bf16[16,16,768]{2,1,0:T(8,128)(2,1)} %shard_map.70), calls=%async_computation.1 | async-start | bytes 786432 | tf_op jit(solution)/shard_map/all_to_all | solution.py:320
  78.3 7.6 %collective-permute-start.10 = (bf16[96,384]{1,0:T(8,128)(2,1)S(1)}, bf16[96,384]{1,0:T(8,128)(2,1)S(1)}, u32[]{:S(2)}, u32[]{:S(2)}) collective-permute-start(bf16[96,384]{1,0:T(8,128)(2,1)S(1)} %get-tuple-element.40), channel_id=1, source_target_pairs={{0,3},{1,0},{2,1},{3,2},{4,7},{5,4},{6,5},{7,6},{8,11},{9,8},{10,9... | collective-permute-start | bytes 221192 | tf_op jit(solution)/shard_map/ppermute | solution.py:279
  80.8 5.8 %collective-permute-start.11 = (bf16[96,384]{1,0:T(8,128)(2,1)S(1)}, bf16[96,384]{1,0:T(8,128)(2,1)S(1)}, u32[]{:S(2)}, u32[]{:S(2)}) collective-permute-start(bf16[96,384]{1,0:T(8,128)(2,1)S(1)} %get-tuple-element.42), channel_id=1, source_target_pairs={{0,32},{16,48},{32,0},{48,16},{1,33},{17,49},{33,1},{49,17},{2,34}... | collective-permute-start | bytes 221192 | tf_op jit(solution)/shard_map/ppermute | solution.py:279
  82.6 5.1 %collective-permute-start.12 = (bf16[96,384]{1,0:T(8,128)(2,1)S(1)}, bf16[96,384]{1,0:T(8,128)(2,1)S(1)}, u32[]{:S(2)}, u32[]{:S(2)}) collective-permute-start(bf16[96,384]{1,0:T(8,128)(2,1)S(1)} %get-tuple-element.43), channel_id=1, source_target_pairs={{0,16},{16,32},{32,48},{48,0},{1,17},{17,33},{33,49},{49,1},{2,18}... | collective-permute-start | bytes 221192 | tf_op jit(solution)/shard_map/ppermute | solution.py:279
  82.6 6.4 %collective-permute-start.13 = (bf16[96,384]{1,0:T(8,128)(2,1)S(1)}, bf16[96,384]{1,0:T(8,128)(2,1)S(1)}, u32[]{:S(2)}, u32[]{:S(2)}) collective-permute-start(bf16[96,384]{1,0:T(8,128)(2,1)S(1)} %get-tuple-element.44), channel_id=1, source_target_pairs={{0,48},{16,0},{32,16},{48,32},{1,49},{17,1},{33,17},{49,33},{2,50}... | collective-permute-start | bytes 221192 | tf_op jit(solution)/shard_map/ppermute | solution.py:279
  85.3 5.0 %collective-permute-start.8 = (bf16[96,384]{1,0:T(8,128)(2,1)S(1)}, bf16[96,384]{1,0:T(8,128)(2,1)S(1)}, u32[]{:S(2)}, u32[]{:S(2)}) collective-permute-start(bf16[96,384]{1,0:T(8,128)(2,1)S(1)} %get-tuple-element.38), channel_id=1, source_target_pairs={{0,2},{1,3},{2,0},{3,1},{4,6},{5,7},{6,4},{7,5},{8,10},{9,11},{10,... | collective-permute-start | bytes 221192 | tf_op jit(solution)/shard_map/ppermute | solution.py:279
  85.9 5.2 %collective-permute-start.9 = (bf16[96,384]{1,0:T(8,128)(2,1)S(1)}, bf16[96,384]{1,0:T(8,128)(2,1)S(1)}, u32[]{:S(2)}, u32[]{:S(2)}) collective-permute-start(bf16[96,384]{1,0:T(8,128)(2,1)S(1)} %get-tuple-element.39), channel_id=1, source_target_pairs={{0,1},{1,2},{2,3},{3,0},{4,5},{5,6},{6,7},{7,4},{8,9},{9,10},{10,1... | collective-permute-start | bytes 221192 | tf_op jit(solution)/shard_map/ppermute | solution.py:279
  106.0 7.2 %collective-permute-start.14 = (f32[8,768]{1,0:T(8,128)S(1)}, f32[8,768]{1,0:T(8,128)S(1)}, u32[]{:S(2)}, u32[]{:S(2)}) collective-permute-start(f32[8,768]{1,0:T(8,128)S(1)} %get-tuple-element.46), channel_id=1, source_target_pairs={{0,8},{8,0},{1,9},{9,1},{2,10},{10,2},{3,11},{11,3},{4,12},{12,4},... | collective-permute-start | bytes 73736 | tf_op jit(solution)/shard_map/ppermute | solution.py:275

commit v3 on v2

--- a/solution.py
+++ b/solution.py
@@ -6,6 +6,7 @@
 from jax.sharding import Mesh, PartitionSpec as P
 
 HEAD = 64
+ORDER = ((0, 2), (1, 2), (0, 1), (1, 1), (0, 3), (1, 3))
 BF = jnp.bfloat16
 F32 = jnp.float32
 VM = pl.BlockSpec(memory_space=pltpu.VMEM)
@@ -120,10 +121,10 @@
     return copies
 
 
-def main_body(at_ref, own_ref, oth_ref, wqkv_ref, wout_ref, dqkv_ref, *rest):
-    g_refs = rest[:8]
-    (n_s, d_s, qkv_s, a_s, kt_s, vt_s, at_s, dqt_s, att_s, nt_s, w_ref, wo_ref,
-     sems) = rest[8:]
+def main_body(at_ref, own_ref, oth_ref, wqkv_ref, wout_ref, mine_ref, theirs_ref, xd_ref, *rest):
+    g_refs = rest[:7]
+    (dqkv_ref, n_s, d_s, qkv_s, a_s, kt_s, vt_s, at_s, dqt_s, att_s, nt_s, w_ref, wo_ref,
+     sems) = rest[7:]
     copies = weight_copies(at_ref[0], wqkv_ref, w_ref, sems)
     rows = pl.ds(pl.multiple_of(at_ref[0] * 384, 128), 384)
     copies.append(pltpu.make_async_copy(wout_ref.at[rows, :], wo_ref, sems.at[3]))
@@ -132,8 +133,12 @@
     for patch in range(2):
         for side, ref in enumerate((own_ref, oth_ref)):
             at = patch * 256 + side * 128
-            n_s[at : at + 128, :] = normalize(rows_of(ref, patch * 8))[0].astype(BF)
-            d_s[at : at + 128, :] = rows_of(ref, 16 + patch * 8).astype(BF)
+            x, d = rows_of(ref, patch * 8), rows_of(ref, 16 + patch * 8).astype(BF)
+            n_s[at : at + 128, :] = normalize(x)[0].astype(BF)
+            d_s[at : at + 128, :] = d
+            if side == 0:
+                xd_ref[patch * 128 : patch * 128 + 128, :] = x.astype(BF)
+                xd_ref[256 + patch * 128 : 256 + patch * 128 + 128, :] = d
     for t in range(3):
         copies[t].wait()
         qkv_s[:, t * 384 : (t + 1) * 384] = nn(n_s[...], w_ref[:, t * 384 : (t + 1) * 384]).astype(BF)
@@ -177,35 +182,33 @@
     for (rows, _, hr, _, _, _, _), ds in zip(work, dss):
         dqt_s[hr, rows] = nn(kt_s[hr, rows], ds).astype(BF)
     dqkv_ref[:, 0:384] = dqt_s[...].T
-    nt_s[...] = nt(selection(768, feature_order(768, at_ref[1], at_ref[2])), n_s[...]).astype(BF)
-    for t in range(3):
-        g = nn(nt_s[...], dqkv_ref[:, t * 384 : (t + 1) * 384]).astype(BF)
-        for i, ref in enumerate(g_refs):
-            ref[t * 96 : (t + 1) * 96, :] = g[i * 96 : (i + 1) * 96]
-    attp = nn(selection(384, feature_order(384, at_ref[1], at_ref[2])), att_s[...]).astype(BF)
-    for t in range(2):
-        g = nn(attp, d_s[:, t * 384 : (t + 1) * 384]).astype(BF)
-        for i, ref in enumerate(g_refs):
-            ref[288 + t * 48 : 288 + (t + 1) * 48, :] = g[i * 48 : (i + 1) * 48]
-
-
-def dnormed_body(at_ref, dqkv_ref, wqkv_ref, mine_ref, theirs_ref, w_ref, sems):
-    copies = weight_copies(at_ref[0], wqkv_ref, w_ref, sems)
-    for copy in copies:
-        copy.start()
-    for copy in copies:
-        copy.wait()
     part = nt(dqkv_ref[...], w_ref[...])
     for patch in range(2):
         mine_ref[patch * 128 : (patch + 1) * 128, :] = part[patch * 256 : patch * 256 + 128]
         theirs_ref[patch * 128 : (patch + 1) * 128, :] = part[patch * 256 + 128 : patch * 256 + 256].astype(BF)
 
-
-def input_gradient_body(part_ref, got_ref, own_ref, o_ref):
+    def put(i, row, value):
+        half, s = divmod(i, 4)
+        ref, row = (g_refs[6], half * 384 + row) if s == 0 else (g_refs[half * 3 + s - 1], row)
+        ref[row : row + value.shape[0], :] = value
+
+    nt_s[...] = nt(selection(768, feature_order(768, at_ref[1], at_ref[2])), n_s[...]).astype(BF)
+    for t in range(3):
+        g = nn(nt_s[...], dqkv_ref[:, t * 384 : (t + 1) * 384]).astype(BF)
+        for i in range(8):
+            put(i, t * 96, g[i * 96 : (i + 1) * 96])
+    attp = nn(selection(384, feature_order(384, at_ref[1], at_ref[2])), att_s[...]).astype(BF)
+    for t in range(2):
+        g = nn(attp, d_s[:, t * 384 : (t + 1) * 384]).astype(BF)
+        for i in range(8):
+            put(i, 288 + t * 48, g[i * 48 : (i + 1) * 48])
+
+
+def input_gradient_body(part_ref, got_ref, xd_ref, o_ref):
     outs = []
     for patch in range(2):
-        xhat, inv = normalize(rows_of(own_ref, patch * 8))
-        dout = rows_of(own_ref, 16 + patch * 8)
+        xhat, inv = normalize(xd_ref[patch * 128 : patch * 128 + 128, :].astype(F32))
+        dout = xd_ref[256 + patch * 128 : 256 + patch * 128 + 128, :].astype(F32)
         at = pl.ds(patch * 128, 128)
         dn = part_ref[at, :] + got_ref[at, :].astype(F32)
         first = jnp.mean(dn, axis=1, keepdims=True)
@@ -214,50 +217,48 @@
     o_ref[...] = jnp.concatenate(outs, axis=1).astype(BF)
 
 
-def added(refs):
-    total = refs[0][...].astype(F32)
-    for ref in refs[1:]:
-        total = total + ref[...].astype(F32)
+def added(refs, half):
+    rows = refs[6].shape[0] // 2
+    total = refs[6][half * rows : (half + 1) * rows].astype(F32)
+    for (i, _), ref in zip(ORDER, refs):
+        if i == half:
+            total = total + ref[...].astype(F32)
     return total.astype(BF)
 
 
 def split_body(*refs):
     sel = selection(384, split_order())
     for half in range(2):
-        out = nn(sel, added(refs[half * 4 : half * 4 + 4])).astype(BF)
-        for t in range(4):
-            refs[8 + half * 4 + t][...] = out[t * 96 : (t + 1) * 96]
-
-
-def slot_body(at_ref, back_ref, *refs):
-    total = jnp.concatenate([added(refs[0:4]), added(refs[4:8])], axis=0)
+        out = nn(sel, added(refs, half)).astype(BF)
+        refs[13][half * 96 : half * 96 + 96] = out[0:96]
+        for t in range(3):
+            refs[7 + half * 3 + t][...] = out[(t + 1) * 96 : (t + 2) * 96]
+
+
+def slot_body(at_ref, done_ref, *refs):
+    total = jnp.concatenate([added(refs, 0), added(refs, 1)], axis=0)
     slot, half = slot_order(at_ref[0])
     for h in range(2):
         part = nn(selection(128, jnp.where(half == h, slot, -1)), total).astype(BF)
-        refs[8][:, :, h * 384 : (h + 1) * 384] = part.reshape(8, 16, 384)
-
-
-def home_body(r_ref, ig_ref):
+        refs[7][:, :, h * 384 : (h + 1) * 384] = part.reshape(16, 8, 384)
+
+
+def home_body(r_ref, ig_ref, done_ref):
     sel = selection(256, home_order())
     back = lax.dot_general(
         sel, r_ref[...].reshape(256, 768), (((0,), (0,)), ((), ())), preferred_element_type=F32
     )
     ig_ref[...] = back.astype(BF)
-
-
-def sum_body(at_ref, r_ref, own_ref, oth_ref):
-    total = r_ref[0].astype(F32)
-    for s in range(1, 8):
-        total = total + r_ref[s].astype(F32)
-    low = at_ref[0] == 0
-    own_ref[...] = jnp.where(low, total[0:8], total[8:16])
-    oth_ref[...] = jnp.where(low, total[8:16], total[0:8])
-
-
-def last_body(at_ref, own_ref, got_ref, gq_ref, go_ref):
-    own, got = own_ref[...], got_ref[...]
-    low = at_ref[0] == 0
-    halves = (jnp.where(low, own, got), jnp.where(low, got, own))
+    done_ref[...] = jnp.zeros_like(done_ref)
+
+
+def last_body(r_ref, gq_ref, go_ref):
+    halves = []
+    for h in range(2):
+        total = r_ref[h].astype(F32)
+        for z in range(1, 8):
+            total = total + r_ref[2 * z + h].astype(F32)
+        halves.append(total)
     for h, m in enumerate(halves):
         at = h * 384
         gq_ref[:, at : at + 384] = m[0:3, 0:384]
@@ -265,7 +266,7 @@
         gq_ref[0:1, 1536 + at : 1536 + at + 384] = m[3:4, 0:384]
         gq_ref[1:2, 1536 + at : 1536 + at + 384] = m[3:4, 384:768]
         gq_ref[2:3, 1536 + at : 1536 + at + 384] = m[4:5, 0:384]
-    go_ref[...] = own[5:8] + got[5:8]
+    go_ref[...] = halves[0][5:8] + halves[1][5:8]
 
 
 def local(x, d, w_qkv, w_out):
@@ -274,10 +275,11 @@
     def swap(v):
         return lax.ppermute(v, "c", [(0, 1), (1, 0)])
 
-    def spread(blocks, axis):
-        return [blocks[0]] + [
-            lax.ppermute(blocks[s], axis, [(i, (i + s) % 4) for i in range(4)]) for s in (2, 1, 3)
+    def spread(blocks, axes):
+        moved = [
+            lax.ppermute(blocks[i * 3 + s - 1], axes[i], [(j, (j + s) % 4) for j in range(4)]) for i, s in ORDER
         ]
+        return moved + [blocks[6]]
 
     scr = lambda *s: pltpu.VMEM(s, BF)
     packed, = call(
@@ -290,43 +292,29 @@
     )
     own = lax.all_to_all(packed, ("x", "zh"), split_axis=0, concat_axis=0, tiled=True)
     oth = swap(own)
-    dqkv, *grads = call(
+    mine, theirs, xd, *grads = call(
         main_body,
-        [((512, 1152), BF)] + [((384, 384), BF)] * 8,
+        [((256, 768), F32), ((256, 768), BF), ((512, 768), BF)] + [((384, 384), BF)] * 6 + [((768, 384), BF)],
         [at, own, oth, w_qkv, w_out],
-        scratch=[scr(512, 768), scr(512, 768), scr(512, 1152), scr(512, 384), scr(384, 512),
+        scratch=[scr(512, 1152), scr(512, 768), scr(512, 768), scr(512, 1152), scr(512, 384), scr(384, 512),
                  scr(384, 512), scr(384, 512), scr(384, 512), scr(384, 512), scr(768, 512), scr(768, 1152),
                  scr(384, 768), pltpu.SemaphoreType.DMA((4,))],
         smem=(0,),
         hbm=(3, 4),
-        limit=58,
+        limit=50,
         flops=6 * 10**9,
         nbytes=10**7,
     )
-    first = spread(grads[:4], "x") + spread(grads[4:], "y")
-    mine, theirs = call(
-        dnormed_body,
-        [((256, 768), F32), ((256, 768), BF)],
-        [at, dqkv, w_qkv],
-        scratch=[scr(768, 1152), pltpu.SemaphoreType.DMA((3,))],
-        smem=(0,),
-        hbm=(2,),
-        flops=10**9,
-        nbytes=5 * 10**6,
-        limit=16,
-    )
+    first = spread(grads, "xy")
     got = swap(theirs)
-    ig, = call(input_gradient_body, [((16, 16, 768), BF)], [mine, got, own], nbytes=3 * 10**6)
+    ig, = call(input_gradient_body, [((16, 16, 768), BF)], [mine, got, xd], nbytes=3 * 10**6)
     back = lax.all_to_all(ig, ("x", "zh"), split_axis=0, concat_axis=0, tiled=True)
-    second = call(split_body, [((96, 384), BF)] * 8, first, flops=4_000_000_000)
-    second = spread(second[:4], "y") + spread(second[4:], "x")
-    slots, = call(slot_body, [((8, 16, 768), BF)], [at, back, *second], smem=(0,), hbm=(1,))
-    ig_home, = call(home_body, [((256, 768), BF)], [back])
-    last = lax.all_to_all(slots, ("zh", "zl"), split_axis=0, concat_axis=0, tiled=True)
-    own8, oth8 = call(sum_body, [((8, 768), F32)] * 2, [at, last], smem=(0,))
-    grad_qkv, grad_out = call(
-        last_body, [((3, 2304), F32), ((3, 768), F32)], [at, own8, swap(oth8)], smem=(0,)
-    )
+    second = call(split_body, [((96, 384), BF)] * 6 + [((192, 384), BF)], first, flops=4_000_000_000)
+    second = spread(second, "yx")
+    ig_home, done = call(home_body, [((256, 768), BF), ((8, 128), F32)], [back])
+    slots, = call(slot_body, [((16, 8, 768), BF)], [at, done, *second], smem=(0,))
+    last = lax.all_to_all(slots, ("zh", "zl", "c"), split_axis=0, concat_axis=0, tiled=True)
+    grad_qkv, grad_out = call(last_body, [((3, 2304), F32), ((3, 768), F32)], [last])
     return ig_home.reshape(8, 32, 768), grad_qkv, grad_out
 
 

time: 115 us -> 110 us (0.957)
  starting transfers between devices: 30.5 us -> 23.2 us
  blocking collectives: 47.8 us -> 52.2 us
  Pallas kernels: 22.1 us -> 19.6 us
    ppermute x3 -> x2, starting transfers between devices: 9.59 us -> 3.36 us  [swap(): return lax.ppermute(v, 'c', [(0, 1), (1, 0)])]
    all_to_all x1, blocking collectives: 13.6 us -> 18 us  [local(): lax.all_to_all(slots, ('zh', 'zl', 'c'), split_axis=0, concat_axis=0, til...]
    ppermute x12, waiting for transfers between devices: 9.18 us -> 5.61 us  [spread(): lax.ppermute(blocks[i * 3 + s - 1], axes[i], [(j, (j + s) % 4) for j in r...]
    all_to_all x1, waiting for transfers between devices: 0.01 us -> 3.18 us  [local(): lax.all_to_all(ig, ('x', 'zh'), split_axis=0, concat_axis=0, tiled=True)]
    pallas_call x9 -> x7, Pallas kernels: 22.1 us -> 19.6 us  [call(): pl.pallas_call(body, out_shape=[jax.ShapeDtypeStruct(s, d) for s, d in ou...]
    unnamed x20 -> x8, local copies, waits for them, and re-layouts: 2.18 us -> 3.04 us
  transfers between devices with their start and end apart: 16 -> 15, of which waited for: 8 -> 3; matrix products, arithmetic and copies ran while one was open for 1% -> 0% of each run, Pallas kernels for 3% -> 4%
where the time goes in v3:
time: 110 us
  blocking collectives  52.2 us (47%)
  starting transfers between devices  23.2 us (21%)
  Pallas kernels  19.6 us (18%)
  waiting for transfers between devices  10.8 us (10%)
  local copies, waits for them, and re-layouts  3.04 us (3%)
    all_to_all x1, blocking collectives, local(): lax.all_to_all(packed, ('x', 'zh'), split_axis=0, concat_axis=0, tiled=True)  34.3 us
    pallas_call x7, Pallas kernels, call(): pl.pallas_call(body, out_shape=[jax.ShapeDtypeStruct(s, d) for s, d in ou...  19.6 us
    all_to_all x1, blocking collectives, local(): lax.all_to_all(slots, ('zh', 'zl', 'c'), split_axis=0, concat_axis=0, til...  18 us
    ppermute x12, starting transfers between devices, spread(): lax.ppermute(blocks[i * 3 + s - 1], axes[i], [(j, (j + s) % 4) for j in r...  16.3 us
    ppermute x12, waiting for transfers between devices, spread(): lax.ppermute(blocks[i * 3 + s - 1], axes[i], [(j, (j + s) % 4) for j in r...  5.61 us
    all_to_all x1, starting transfers between devices, local(): lax.all_to_all(ig, ('x', 'zh'), split_axis=0, concat_axis=0, tiled=True)  3.55 us
    ppermute x2, starting transfers between devices, swap(): return lax.ppermute(v, 'c', [(0, 1), (1, 0)])  3.36 us
    all_to_all x1, waiting for transfers between devices, local(): lax.all_to_all(ig, ('x', 'zh'), split_axis=0, concat_axis=0, tiled=True)  3.18 us
  transfers between devices with their start and end apart: 15, of which 3 were waited for; matrix products, arithmetic and copies ran while one was open for 0% of the time, Pallas kernels for 4%

profile of v3, /device:TPU:1, one launch (start us, length us, event | category | flops | bytes accessed | tf_op | source)
XLA Modules:
  0.0 109.6 jit_solution(15571788127228393358)
XLA Ops:
  0.6 2.5 %shard_map.67 = bf16[16,32,768]{2,1,0:T(8,128)(2,1)} custom-call(bf16[256,768]{1,0:T(8,128)(2,1)} %bitcast.6, bf16[256,768]{1,0:T(8,128)(2,1)} %bitcast.7), custom_call_target="tpu_custom_call" | custom-call | tf_op jit(solution)/shard_map/pallas_call | solution.py:27
  3.1 34.3 %all_to_all.15.own_ref = bf16[16,32,768]{2,1,0:T(8,128)(2,1)S(1)} all-to-all(bf16[16,32,768]{2,1,0:T(8,128)(2,1)} %shard_map.67), channel_id=1, replica_groups=mesh['zh'=4,'x'=4,'c'=2,'zl'=2,'y'=4] {'x','zh'}, dimensions={0} | all-to-all | bytes 1572864 | tf_op jit(solution)/shard_map/all_to_all | solution.py:293
  37.4 3.0 %collective-permute-start = (bf16[16,32,768]{2,1,0:T(8,128)(2,1)S(1)}, bf16[16,32,768]{2,1,0:T(8,128)(2,1)}, u32[]{:S(2)}, u32[]{:S(2)}) collective-permute-start(bf16[16,32,768]{2,1,0:T(8,128)(2,1)S(1)} %all_to_all.15.own_ref), channel_id=1, source_target_pairs={{0,8},{8,0},{1,9},{9,1},{2,10},{10,2},{3,11},{11,3},{4,12},{12,4},... | collective-permute-start | bytes 2359304 | tf_op jit(solution)/shard_map/ppermute | solution.py:276
  40.4 0.1 pad_add_fusion.at_ref
  40.5 2.0 %collective-permute-done.oth_ref = bf16[16,32,768]{2,1,0:T(8,128)(2,1)} collective-permute-done((bf16[16,32,768]{2,1,0:T(8,128)(2,1)S(1)}, bf16[16,32,768]{2,1,0:T(8,128)(2,1)}, u32[]{:S(2)}, u32[]{:S(2)}) %collective-permute-start) | collective-permute-done | bytes 786464 | tf_op jit(solution)/shard_map/ppermute | solution.py:276
  42.4 11.5 %shard_map.68 = (f32[256,768]{1,0:T(8,128)S(1)}, bf16[256,768]{1,0:T(8,128)(2,1)S(1)}, bf16[512,768]{1,0:T(8,128)(2,1)}, bf16[384,384]{1,0:T(8,128)(2,1)S(1)}, b...) custom-call(s32[3]{0:T(128)S(1)} %pad_add_fusion.at_ref, ...), custom_call_target="tpu_custom_call" | custom-call | flops 6000000000 | bytes 10000000 | tf_op jit(solution)/shard_map/pallas_call | solution.py:27
  53.9 0.8 copy-done.1
  54.8 0.4 collective-permute-start.1
  55.2 0.6 collective-permute-start.2
  55.7 2.9 %collective-permute-start.3 = (bf16[384,384]{1,0:T(8,128)(2,1)S(1)}, bf16[384,384]{1,0:T(8,128)(2,1)S(1)}, u32[]{:S(2)}, u32[]{:S(2)}) collective-permute-start(bf16[384,384]{1,0:T(8,128)(2,1)S(1)} %get-tuple-element.30), channel_id=1, source_target_pairs={{0,2},{1,3},{2,0},{3,1},{4,6},{5,7},{6,4},{7,5},{8,10},{9,11},{10,... | collective-permute-start | bytes 884744 | tf_op jit(solution)/shard_map/ppermute | solution.py:280
  58.6 0.6 collective-permute-start.4
  59.2 0.4 collective-permute-start.5
  59.6 5.6 %collective-permute-done.2.refs_0_ = bf16[384,384]{1,0:T(8,128)(2,1)S(1)} collective-permute-done((bf16[384,384]{1,0:T(8,128)(2,1)S(1)}, bf16[384,384]{1,0:T(8,128)(2,1)S(1)}, u32[]{:S(2)}, u32[]{:S(2)}) %collective-permute-start.2) | collective-permute-done | bytes 294944 | tf_op jit(solution)/shard_map/ppermute | solution.py:280
  65.2 0.5 collective-permute-start.6
  65.7 0.0 collective-permute-done.1.got_ref
  65.7 2.7 %collective-permute-start.7 = (bf16[384,384]{1,0:T(8,128)(2,1)S(1)}, bf16[384,384]{1,0:T(8,128)(2,1)}, u32[]{:S(2)}, u32[]{:S(2)}) collective-permute-start(bf16[384,384]{1,0:T(8,128)(2,1)S(1)} %get-tuple-element.34), channel_id=1, source_target_pairs={{0,3},{1,0},{2,1},{3,2},{4,7},{5,4},{6,5},{7,6},{8,11},{9,8},{10,9... | collective-permute-start | bytes 884744 | tf_op jit(solution)/shard_map/ppermute | solution.py:280
  68.4 1.1 %copy-done = bf16[512,768]{1,0:T(8,128)(2,1)S(1)} copy-done((bf16[512,768]{1,0:T(8,128)(2,1)S(1)}, bf16[512,768]{1,0:T(8,128)(2,1)}, u32[]{:S(2)}) %copy-start) | copy-done | bytes 786456
  69.6 1.3 %shard_map.69 = bf16[16,16,768]{2,1,0:T(8,128)(2,1)} custom-call(f32[256,768]{1,0:T(8,128)S(1)} %get-tuple-element.24.part_ref, bf16[256,768]{1,0:T(8,128)(2,1)S(1)} %collective-permute-done.1.got_ref, bf16[512,768]{1,0:T(8,128)(2,1)S(1)} %copy-done), custom_call_target="tpu_custom_call" | custom-call | bytes 3000000 | tf_op jit(solution)/shard_map/pallas_call | solution.py:27
  70.9 3.6 %all-to-all-start.1 = ((bf16[16,16,768]{2,1,0:T(8,128)(2,1)}), bf16[16,16,768]{2,1,0:T(8,128)(2,1)S(1)}, u32[]{:S(2)}, u32[]{:S(2)}) async-start(bf16[16,16,768]{2,1,0:T(8,128)(2,1)} %shard_map.69), calls=%async_computation.1 | async-start | bytes 786432 | tf_op jit(solution)/shard_map/all_to_all | solution.py:311
  74.5 1.1 copy-done.2
  75.6 1.7 %shard_map.71 = (bf16[96,384]{1,0:T(8,128)(2,1)S(1)}, bf16[96,384]{1,0:T(8,128)(2,1)S(1)}, bf16[96,384]{1,0:T(8,128)(2,1)S(1)}, bf16[96,384]{1,0:T(8,128)(2,1)S(...) custom-call(bf16[384,384]{1,0:T(8,128)(2,1)S(1)} %collective-permute-done.2.refs_0_, ...), custom_call_target="tpu_custom_call" | custom-call | flops 4000000000 | tf_op jit(solution)/shard_map/pallas_call | solution.py:27
  77.3 1.6 %collective-permute-start.8 = (bf16[96,384]{1,0:T(8,128)(2,1)S(1)}, bf16[96,384]{1,0:T(8,128)(2,1)S(1)}, u32[]{:S(2)}, u32[]{:S(2)}) collective-permute-start(bf16[96,384]{1,0:T(8,128)(2,1)S(1)} %get-tuple-element.36), channel_id=1, source_target_pairs={{0,2},{1,3},{2,0},{3,1},{4,6},{5,7},{6,4},{7,5},{8,10},{9,11},{10,... | collective-permute-start | bytes 221192 | tf_op jit(solution)/shard_map/ppermute | solution.py:280
  78.9 1.7 %collective-permute-start.9 = (bf16[96,384]{1,0:T(8,128)(2,1)S(1)}, bf16[96,384]{1,0:T(8,128)(2,1)S(1)}, u32[]{:S(2)}, u32[]{:S(2)}) collective-permute-start(bf16[96,384]{1,0:T(8,128)(2,1)S(1)} %get-tuple-element.37), channel_id=1, source_target_pairs={{0,32},{16,48},{32,0},{48,16},{1,33},{17,49},{33,1},{49,17},{2,34}... | collective-permute-start | bytes 221192 | tf_op jit(solution)/shard_map/ppermute | solution.py:280
  80.5 0.7 collective-permute-start.10
  81.2 0.3 collective-permute-start.11
  81.5 2.1 %collective-permute-start.12 = (bf16[96,384]{1,0:T(8,128)(2,1)S(1)}, bf16[96,384]{1,0:T(8,128)(2,1)S(1)}, u32[]{:S(2)}, u32[]{:S(2)}) collective-permute-start(bf16[96,384]{1,0:T(8,128)(2,1)S(1)} %get-tuple-element.40), channel_id=1, source_target_pairs={{0,3},{1,0},{2,1},{3,2},{4,7},{5,4},{6,5},{7,6},{8,11},{9,8},{10,9... | collective-permute-start | bytes 221192 | tf_op jit(solution)/shard_map/ppermute | solution.py:280
  83.6 2.3 %collective-permute-start.13 = (bf16[96,384]{1,0:T(8,128)(2,1)S(1)}, bf16[96,384]{1,0:T(8,128)(2,1)S(1)}, u32[]{:S(2)}, u32[]{:S(2)}) collective-permute-start(bf16[96,384]{1,0:T(8,128)(2,1)S(1)} %get-tuple-element.41), channel_id=1, source_target_pairs={{0,48},{16,0},{32,16},{48,32},{1,49},{17,1},{33,17},{49,33},{2,50}... | collective-permute-start | bytes 221192 | tf_op jit(solution)/shard_map/ppermute | solution.py:280
  85.9 3.2 %all-to-all-done.1.r_ref = bf16[16,16,768]{2,1,0:T(8,128)(2,1)S(1)} async-done(((bf16[16,16,768]{2,1,0:T(8,128)(2,1)}), bf16[16,16,768]{2,1,0:T(8,128)(2,1)S(1)}, u32[]{:S(2)}, u32[]{:S(2)}) %all-to-all-start.1) | async-done | bytes 393248 | tf_op jit(solution)/shard_map/all_to_all | solution.py:311
  89.1 1.1 shard_map.70
  90.2 0.8 shard_map.72
  91.0 18.0 %all_to_all.16.r_ref = bf16[16,8,768]{2,1,0:T(8,128)(2,1)S(1)} all-to-all(bf16[16,8,768]{2,1,0:T(8,128)(2,1)S(1)} %shard_map.72), channel_id=1, replica_groups=mesh['zh'=4,'x'=4,'c'=2,'zl'=2,'y'=4] {'zh','zl','c'}, dimensions={0} | all-to-all | bytes 393216 | tf_op jit(solution)/shard_map/all_to_all | solution.py:316
  109.0 0.7 shard_map.73
  (16 shorter events, 0.0 us)
Async XLA Ops:
  37.4 5.0 %copy-start.3 = (bf16[16,32,768]{2,1,0:T(8,128)(2,1)}, bf16[16,32,768]{2,1,0:T(8,128)(2,1)S(1)}, u32[]{:S(2)}) copy-start(bf16[16,32,768]{2,1,0:T(8,128)(2,1)S(1)} %all_to_all.15.own_ref) | copy-start | bytes 2359300
  37.4 5.0 %collective-permute-start = (bf16[16,32,768]{2,1,0:T(8,128)(2,1)S(1)}, bf16[16,32,768]{2,1,0:T(8,128)(2,1)}, u32[]{:S(2)}, u32[]{:S(2)}) collective-permute-start(bf16[16,32,768]{2,1,0:T(8,128)(2,1)S(1)} %all_to_all.15.own_ref), channel_id=1, source_target_pairs={{0,8},{8,0},{1,9},{9,1},{2,10},{10,2},{3,11},{11,3},{4,12},{12,4},... | collective-permute-start | bytes 2359304 | tf_op jit(solution)/shard_map/ppermute | solution.py:276
  53.9 0.8 copy-start.1
  54.8 10.9 %collective-permute-start.1 = (bf16[256,768]{1,0:T(8,128)(2,1)S(1)}, bf16[256,768]{1,0:T(8,128)(2,1)S(1)}, u32[]{:S(2)}, u32[]{:S(2)}) collective-permute-start(bf16[256,768]{1,0:T(8,128)(2,1)S(1)} %get-tuple-element.25), channel_id=1, source_target_pairs={{0,8},{8,0},{1,9},{9,1},{2,10},{10,2},{3,11},{11,3},{4,12},{12,4},... | collective-permute-start | bytes 1179656 | tf_op jit(solution)/shard_map/ppermute | solution.py:276
  55.2 10.0 %collective-permute-start.2 = (bf16[384,384]{1,0:T(8,128)(2,1)S(1)}, bf16[384,384]{1,0:T(8,128)(2,1)S(1)}, u32[]{:S(2)}, u32[]{:S(2)}) collective-permute-start(bf16[384,384]{1,0:T(8,128)(2,1)S(1)} %get-tuple-element.29), channel_id=1, source_target_pairs={{0,32},{16,48},{32,0},{48,16},{1,33},{17,49},{33,1},{49,17},{2,34}... | collective-permute-start | bytes 884744 | tf_op jit(solution)/shard_map/ppermute | solution.py:280
  55.7 18.7 %collective-permute-start.3 = (bf16[384,384]{1,0:T(8,128)(2,1)S(1)}, bf16[384,384]{1,0:T(8,128)(2,1)S(1)}, u32[]{:S(2)}, u32[]{:S(2)}) collective-permute-start(bf16[384,384]{1,0:T(8,128)(2,1)S(1)} %get-tuple-element.30), channel_id=1, source_target_pairs={{0,2},{1,3},{2,0},{3,1},{4,6},{5,7},{6,4},{7,5},{8,10},{9,11},{10,... | collective-permute-start | bytes 884744 | tf_op jit(solution)/shard_map/ppermute | solution.py:280
  58.6 15.8 %collective-permute-start.4 = (bf16[384,384]{1,0:T(8,128)(2,1)S(1)}, bf16[384,384]{1,0:T(8,128)(2,1)S(1)}, u32[]{:S(2)}, u32[]{:S(2)}) collective-permute-start(bf16[384,384]{1,0:T(8,128)(2,1)S(1)} %get-tuple-element.31), channel_id=1, source_target_pairs={{0,16},{16,32},{32,48},{48,0},{1,17},{17,33},{33,49},{49,1},{2,18}... | collective-permute-start | bytes 884744 | tf_op jit(solution)/shard_map/ppermute | solution.py:280
  59.2 15.3 %collective-permute-start.5 = (bf16[384,384]{1,0:T(8,128)(2,1)S(1)}, bf16[384,384]{1,0:T(8,128)(2,1)S(1)}, u32[]{:S(2)}, u32[]{:S(2)}) collective-permute-start(bf16[384,384]{1,0:T(8,128)(2,1)S(1)} %get-tuple-element.32), channel_id=1, source_target_pairs={{0,1},{1,2},{2,3},{3,0},{4,5},{5,6},{6,7},{7,4},{8,9},{9,10},{10,1... | collective-permute-start | bytes 884744 | tf_op jit(solution)/shard_map/ppermute | solution.py:280
  65.2 9.3 %collective-permute-start.6 = (bf16[384,384]{1,0:T(8,128)(2,1)S(1)}, bf16[384,384]{1,0:T(8,128)(2,1)}, u32[]{:S(2)}, u32[]{:S(2)}) collective-permute-start(bf16[384,384]{1,0:T(8,128)(2,1)S(1)} %get-tuple-element.33), channel_id=1, source_target_pairs={{0,48},{16,0},{32,16},{48,32},{1,49},{17,1},{33,17},{49,33},{2,50}... | collective-permute-start | bytes 884744 | tf_op jit(solution)/shard_map/ppermute | solution.py:280
  65.7 8.8 %collective-permute-start.7 = (bf16[384,384]{1,0:T(8,128)(2,1)S(1)}, bf16[384,384]{1,0:T(8,128)(2,1)}, u32[]{:S(2)}, u32[]{:S(2)}) collective-permute-start(bf16[384,384]{1,0:T(8,128)(2,1)S(1)} %get-tuple-element.34), channel_id=1, source_target_pairs={{0,3},{1,0},{2,1},{3,2},{4,7},{5,4},{6,5},{7,6},{8,11},{9,8},{10,9... | collective-permute-start | bytes 884744 | tf_op jit(solution)/shard_map/ppermute | solution.py:280
  68.4 1.1 %copy-start = (bf16[512,768]{1,0:T(8,128)(2,1)S(1)}, bf16[512,768]{1,0:T(8,128)(2,1)}, u32[]{:S(2)}) copy-start(bf16[512,768]{1,0:T(8,128)(2,1)} %get-tuple-element.26.xd_ref) | copy-start | bytes 2359300
  70.9 18.2 %all-to-all-start.1 = ((bf16[16,16,768]{2,1,0:T(8,128)(2,1)}), bf16[16,16,768]{2,1,0:T(8,128)(2,1)S(1)}, u32[]{:S(2)}, u32[]{:S(2)}) async-start(bf16[16,16,768]{2,1,0:T(8,128)(2,1)} %shard_map.69), calls=%async_computation.1 | async-start | bytes 786432 | tf_op jit(solution)/shard_map/all_to_all | solution.py:311
  74.5 1.1 copy-start.2
  77.3 6.3 %collective-permute-start.8 = (bf16[96,384]{1,0:T(8,128)(2,1)S(1)}, bf16[96,384]{1,0:T(8,128)(2,1)S(1)}, u32[]{:S(2)}, u32[]{:S(2)}) collective-permute-start(bf16[96,384]{1,0:T(8,128)(2,1)S(1)} %get-tuple-element.36), channel_id=1, source_target_pairs={{0,2},{1,3},{2,0},{3,1},{4,6},{5,7},{6,4},{7,5},{8,10},{9,11},{10,... | collective-permute-start | bytes 221192 | tf_op jit(solution)/shard_map/ppermute | solution.py:280
  78.9 11.3 %collective-permute-start.9 = (bf16[96,384]{1,0:T(8,128)(2,1)S(1)}, bf16[96,384]{1,0:T(8,128)(2,1)S(1)}, u32[]{:S(2)}, u32[]{:S(2)}) collective-permute-start(bf16[96,384]{1,0:T(8,128)(2,1)S(1)} %get-tuple-element.37), channel_id=1, source_target_pairs={{0,32},{16,48},{32,0},{48,16},{1,33},{17,49},{33,1},{49,17},{2,34}... | collective-permute-start | bytes 221192 | tf_op jit(solution)/shard_map/ppermute | solution.py:280
  80.5 9.6 %collective-permute-start.10 = (bf16[96,384]{1,0:T(8,128)(2,1)S(1)}, bf16[96,384]{1,0:T(8,128)(2,1)S(1)}, u32[]{:S(2)}, u32[]{:S(2)}) collective-permute-start(bf16[96,384]{1,0:T(8,128)(2,1)S(1)} %get-tuple-element.38), channel_id=1, source_target_pairs={{0,1},{1,2},{2,3},{3,0},{4,5},{5,6},{6,7},{7,4},{8,9},{9,10},{10,1... | collective-permute-start | bytes 221192 | tf_op jit(solution)/shard_map/ppermute | solution.py:280
  81.2 8.9 %collective-permute-start.11 = (bf16[96,384]{1,0:T(8,128)(2,1)S(1)}, bf16[96,384]{1,0:T(8,128)(2,1)S(1)}, u32[]{:S(2)}, u32[]{:S(2)}) collective-permute-start(bf16[96,384]{1,0:T(8,128)(2,1)S(1)} %get-tuple-element.39), channel_id=1, source_target_pairs={{0,16},{16,32},{32,48},{48,0},{1,17},{17,33},{33,49},{49,1},{2,18}... | collective-permute-start | bytes 221192 | tf_op jit(solution)/shard_map/ppermute | solution.py:280
  81.5 8.6 %collective-permute-start.12 = (bf16[96,384]{1,0:T(8,128)(2,1)S(1)}, bf16[96,384]{1,0:T(8,128)(2,1)S(1)}, u32[]{:S(2)}, u32[]{:S(2)}) collective-permute-start(bf16[96,384]{1,0:T(8,128)(2,1)S(1)} %get-tuple-element.40), channel_id=1, source_target_pairs={{0,3},{1,0},{2,1},{3,2},{4,7},{5,4},{6,5},{7,6},{8,11},{9,8},{10,9... | collective-permute-start | bytes 221192 | tf_op jit(solution)/shard_map/ppermute | solution.py:280
  83.6 6.5 %collective-permute-start.13 = (bf16[96,384]{1,0:T(8,128)(2,1)S(1)}, bf16[96,384]{1,0:T(8,128)(2,1)S(1)}, u32[]{:S(2)}, u32[]{:S(2)}) collective-permute-start(bf16[96,384]{1,0:T(8,128)(2,1)S(1)} %get-tuple-element.41), channel_id=1, source_target_pairs={{0,48},{16,0},{32,16},{48,32},{1,49},{17,1},{33,17},{49,33},{2,50}... | collective-permute-start | bytes 221192 | tf_op jit(solution)/shard_map/ppermute | solution.py:280

commit v4 on v3

--- a/solution.py
+++ b/solution.py
@@ -6,7 +6,6 @@
 from jax.sharding import Mesh, PartitionSpec as P
 
 HEAD = 64
-ORDER = ((0, 2), (1, 2), (0, 1), (1, 1), (0, 3), (1, 3))
 BF = jnp.bfloat16
 F32 = jnp.float32
 VM = pl.BlockSpec(memory_space=pltpu.VMEM)
@@ -22,13 +21,15 @@
     return lax.dot_general(a, b, (((1,), (1,)), ((), ())), preferred_element_type=F32)
 
 
-def call(body, outs, ins, scratch=(), smem=(), hbm=(), flops=0, nbytes=0, limit=16):
-    space = {i: SM for i in smem} | {i: HB for i in hbm}
+def call(body, outs, ins, scratch=(), smem=(), hbm=(), passed=None, flops=0, nbytes=0, limit=8):
+    passed = passed or {}
+    space = {i: SM for i in smem} | {i: HB for i in (*hbm, *passed)}
     return pl.pallas_call(
         body,
         out_shape=[jax.ShapeDtypeStruct(s, d) for s, d in outs],
         in_specs=[space.get(i, VM) for i in range(len(ins))],
-        out_specs=[VM] * len(outs),
+        out_specs=[HB if i in passed.values() else VM for i in range(len(outs))],
+        input_output_aliases=passed,
         scratch_shapes=list(scratch),
         compiler_params=pltpu.CompilerParams(vmem_limit_bytes=limit * 2**20),
         cost_estimate=pl.CostEstimate(flops=flops, bytes_accessed=nbytes, transcendentals=0),
@@ -54,14 +55,14 @@
     return ((p >> 1) << 4) + ((p & 1) << 3) + f
 
 
-def feature_order(n, x0, y0):
+def feature_order(n, role, x0, y0):
     f = lanes(n)
     d = third(f)
     c = (d >> 3) & 1
     x, y = (((d >> 4) & 3) - x0) & 3, ((d & 3) - y0) & 3
     first, second = jnp.where(c == 0, x, y), jnp.where(c == 0, y, x)
     low = (d >> 6) * 6 + ((d >> 2) & 1) * 3 + (f - 3 * d)
-    return c * (n // 2) + first * (n // 8) + second * (n // 32) + low
+    return (c ^ role) * (n // 2) + first * (n // 8) + second * (n // 32) + low
 
 
 def split_order():
@@ -74,10 +75,10 @@
     return jnp.where(i < 288, t1 * 72 + m * 24 + low, t2 * 84 + 72 + hh * 12 + high)
 
 
-def slot_order(core):
+def slot_order():
     i = lanes(192)
-    c = jnp.where(i < 96, 0, 1)
-    i = i - 96 * c
+    k = jnp.where(i < 96, 0, 1)
+    i = i - 96 * k
     big = i < 72
     m = jnp.where(i < 24, 0, jnp.where(i < 48, 1, 2))
     hh = jnp.where(i < 84, 0, 1)
@@ -86,7 +87,7 @@
     j = rem - 3 * d
     row = jnp.where(big, jnp.where(m < 2, j, 3 + (j >> 1)), 5 + j)
     half = jnp.where(big, jnp.where(m < 2, m, j & 1), hh)
-    return ((d + jnp.where(big, 0, 4 * core)) << 4) + (c << 3) + row, half
+    return ((d + jnp.where(big, 0, 4 * k)) << 4) + (k << 3) + row, half
 
 
 def pack_body(x_ref, d_ref, o_ref, x_s, d_s, sems):
@@ -121,29 +122,45 @@
     return copies
 
 
-def main_body(at_ref, own_ref, oth_ref, wqkv_ref, wout_ref, mine_ref, theirs_ref, xd_ref, *rest):
-    g_refs = rest[:7]
-    (dqkv_ref, n_s, d_s, qkv_s, a_s, kt_s, vt_s, at_s, dqt_s, att_s, nt_s, w_ref, wo_ref,
-     sems) = rest[7:]
+def tokens_of(ref):
+    x, d = ([rows_of(ref, first + patch * 8) for patch in range(2)] for first in (0, 16))
+    return jnp.concatenate(x, axis=0), jnp.concatenate(d, axis=0).astype(BF)
+
+
+def own_body(at_ref, own_ref, wqkv_ref, wout_ref, xd_ref, qkv_ref, a_ref, nt_ref, w_ref, wo_ref, sems):
     copies = weight_copies(at_ref[0], wqkv_ref, w_ref, sems)
     rows = pl.ds(pl.multiple_of(at_ref[0] * 384, 128), 384)
     copies.append(pltpu.make_async_copy(wout_ref.at[rows, :], wo_ref, sems.at[3]))
     for copy in copies:
         copy.start()
-    for patch in range(2):
-        for side, ref in enumerate((own_ref, oth_ref)):
-            at = patch * 256 + side * 128
-            x, d = rows_of(ref, patch * 8), rows_of(ref, 16 + patch * 8).astype(BF)
-            n_s[at : at + 128, :] = normalize(x)[0].astype(BF)
-            d_s[at : at + 128, :] = d
-            if side == 0:
-                xd_ref[patch * 128 : patch * 128 + 128, :] = x.astype(BF)
-                xd_ref[256 + patch * 128 : 256 + patch * 128 + 128, :] = d
+    x, d = tokens_of(own_ref)
+    xd_ref[0:256, :] = x.astype(BF)
+    xd_ref[256:512, :] = d
+    n = normalize(x)[0].astype(BF)
+    nt_ref[...] = nt(selection(768, feature_order(768, at_ref[3], at_ref[1], at_ref[2])), n).astype(BF)
     for t in range(3):
         copies[t].wait()
-        qkv_s[:, t * 384 : (t + 1) * 384] = nn(n_s[...], w_ref[:, t * 384 : (t + 1) * 384]).astype(BF)
+        qkv_ref[:, t * 384 : (t + 1) * 384] = nn(n, w_ref[:, t * 384 : (t + 1) * 384]).astype(BF)
     copies[3].wait()
-    a_s[...] = nt(d_s[...], wo_ref[...]).astype(BF)
+    a_ref[...] = nt(d, wo_ref[...]).astype(BF)
+
+
+def main_body(at_ref, oth_ref, xd_ref, qkv0_ref, a0_ref, nt0_ref, w_ref, wo_ref, mine_ref, theirs_ref, *rest):
+    stay_refs, go_ref = rest[:4], rest[4]
+    dqkv_ref, d_s, qkv_s, a_s, kt_s, vt_s, at_s, dqt_s, att_s, nt_s = rest[5:]
+    x, d = tokens_of(oth_ref)
+    n = normalize(x)[0].astype(BF)
+    nt1 = nt(selection(768, feature_order(768, at_ref[3], at_ref[1], at_ref[2])), n).astype(BF)
+    a1 = nt(d, wo_ref[...]).astype(BF)
+    qkv1 = [nn(n, w_ref[:, t * 384 : (t + 1) * 384]).astype(BF) for t in range(3)]
+    for patch in range(2):
+        here = slice(patch * 128, (patch + 1) * 128)
+        one, two = (slice(patch * 256 + side * 128, patch * 256 + side * 128 + 128) for side in range(2))
+        qkv_s[one, :], a_s[one, :], nt_s[:, one] = qkv0_ref[here, :], a0_ref[here, :], nt0_ref[:, here]
+        d_s[one, :] = xd_ref[256 + patch * 128 : 384 + patch * 128, :]
+        a_s[two, :], nt_s[:, two], d_s[two, :] = a1[here], nt1[:, here], d[here]
+        for t in range(3):
+            qkv_s[two, t * 384 : (t + 1) * 384] = qkv1[t][here]
     kt_s[...] = (qkv_s[:, 384:768] * 0.125).T
     vt_s[...] = qkv_s[:, 768:1152].T
     at_s[...] = a_s[...].T
@@ -188,23 +205,23 @@
         theirs_ref[patch * 128 : (patch + 1) * 128, :] = part[patch * 256 + 128 : patch * 256 + 256].astype(BF)
 
     def put(i, row, value):
-        half, s = divmod(i, 4)
-        ref, row = (g_refs[6], half * 384 + row) if s == 0 else (g_refs[half * 3 + s - 1], row)
+        ref, row = (stay_refs[i], row) if i < 4 else (go_ref, (i - 4) * 384 + row)
         ref[row : row + value.shape[0], :] = value
 
-    nt_s[...] = nt(selection(768, feature_order(768, at_ref[1], at_ref[2])), n_s[...]).astype(BF)
     for t in range(3):
         g = nn(nt_s[...], dqkv_ref[:, t * 384 : (t + 1) * 384]).astype(BF)
         for i in range(8):
             put(i, t * 96, g[i * 96 : (i + 1) * 96])
-    attp = nn(selection(384, feature_order(384, at_ref[1], at_ref[2])), att_s[...]).astype(BF)
+    attp = nn(selection(384, feature_order(384, at_ref[3], at_ref[1], at_ref[2])), att_s[...]).astype(BF)
     for t in range(2):
         g = nn(attp, d_s[:, t * 384 : (t + 1) * 384]).astype(BF)
         for i in range(8):
             put(i, 288 + t * 48, g[i * 48 : (i + 1) * 48])
 
 
-def input_gradient_body(part_ref, got_ref, xd_ref, o_ref):
+def input_gradient_body(part_ref, got_ref, xd_ref, blocks_ref, keep_ref, o_ref, same_ref, *block_refs):
+    for s in range(4):
+        block_refs[s][...] = blocks_ref[s * 384 : (s + 1) * 384]
     outs = []
     for patch in range(2):
         xhat, inv = normalize(xd_ref[patch * 128 : patch * 128 + 128, :].astype(F32))
@@ -217,30 +234,29 @@
     o_ref[...] = jnp.concatenate(outs, axis=1).astype(BF)
 
 
-def added(refs, half):
-    rows = refs[6].shape[0] // 2
-    total = refs[6][half * rows : (half + 1) * rows].astype(F32)
-    for (i, _), ref in zip(ORDER, refs):
-        if i == half:
-            total = total + ref[...].astype(F32)
+def added(refs):
+    total = refs[0][...].astype(F32)
+    for ref in refs[1:]:
+        total = total + ref[...].astype(F32)
     return total.astype(BF)
 
 
-def split_body(*refs):
+def split_body(at_ref, *refs):
     sel = selection(384, split_order())
-    for half in range(2):
-        out = nn(sel, added(refs, half)).astype(BF)
-        refs[13][half * 96 : half * 96 + 96] = out[0:96]
-        for t in range(3):
-            refs[7 + half * 3 + t][...] = out[(t + 1) * 96 : (t + 2) * 96]
-
-
-def slot_body(at_ref, done_ref, *refs):
-    total = jnp.concatenate([added(refs, 0), added(refs, 1)], axis=0)
-    slot, half = slot_order(at_ref[0])
+    for k in range(2):
+        total = added([refs[2 * i + (k ^ (step & 1))] for i, step in enumerate((2, 1, 3, 0))])
+        out = nn(sel, total).astype(BF)
+        rows = pl.ds((at_ref[0] ^ k) * 96, 96)
+        for t in range(4):
+            refs[8 + t][rows] = out[t * 96 : (t + 1) * 96]
+
+
+def slot_body(done_ref, *refs):
+    total = added(refs[:4])
+    slot, half = slot_order()
     for h in range(2):
         part = nn(selection(128, jnp.where(half == h, slot, -1)), total).astype(BF)
-        refs[7][:, :, h * 384 : (h + 1) * 384] = part.reshape(16, 8, 384)
+        refs[4][:, :, h * 384 : (h + 1) * 384] = part.reshape(8, 16, 384)
 
 
 def home_body(r_ref, ig_ref, done_ref):
@@ -253,12 +269,10 @@
 
 
 def last_body(r_ref, gq_ref, go_ref):
-    halves = []
-    for h in range(2):
-        total = r_ref[h].astype(F32)
-        for z in range(1, 8):
-            total = total + r_ref[2 * z + h].astype(F32)
-        halves.append(total)
+    total = r_ref[0].astype(F32)
+    for z in range(1, 8):
+        total = total + r_ref[z].astype(F32)
+    halves = total[0:8], total[8:16]
     for h, m in enumerate(halves):
         at = h * 384
         gq_ref[:, at : at + 384] = m[0:3, 0:384]
@@ -270,16 +284,27 @@
 
 
 def local(x, d, w_qkv, w_out):
-    at = jnp.stack([lax.axis_index("c"), lax.axis_index("x"), lax.axis_index("y")]).astype(jnp.int32)
+    core, x0, y0 = (lax.axis_index(a) for a in ("c", "x", "y"))
+    role = core ^ ((x0 + y0) & 1)
+    at = jnp.stack([core, x0, y0, role]).astype(jnp.int32)
 
     def swap(v):
         return lax.ppermute(v, "c", [(0, 1), (1, 0)])
 
-    def spread(blocks, axes):
-        moved = [
-            lax.ppermute(blocks[i * 3 + s - 1], axes[i], [(j, (j + s) % 4) for j in range(4)]) for i, s in ORDER
-        ]
-        return moved + [blocks[6]]
+    def spread(blocks, axes, steps, home):
+        moved = []
+        for s in steps:
+            pairs = []
+            for x in range(4):
+                for y in range(4):
+                    for k in range(2):
+                        u, v = ((x + s) % 4, y) if axes[k] == "x" else (x, (y + s) % 4)
+                        c, d = k ^ ((x + y) & 1), k if home else k ^ ((u + v) & 1)
+                        pairs.append(((x * 2 + c) * 4 + y, (u * 2 + d) * 4 + v))
+            each = len(blocks) // 4
+            for block in blocks[s * each : s * each + each]:
+                moved.append(lax.ppermute(block, ("x", "c", "y"), pairs))
+        return moved
 
     scr = lambda *s: pltpu.VMEM(s, BF)
     packed, = call(
@@ -288,32 +313,47 @@
         [x.reshape(256, 768), d.reshape(256, 768)],
         scratch=[scr(256, 768), scr(256, 768), pltpu.SemaphoreType.DMA((2,))],
         hbm=(0, 1),
-        limit=63,
+        limit=60,
     )
     own = lax.all_to_all(packed, ("x", "zh"), split_axis=0, concat_axis=0, tiled=True)
     oth = swap(own)
-    mine, theirs, xd, *grads = call(
+    xd, *projected = call(
+        own_body,
+        [((512, 768), BF), ((256, 1152), BF), ((256, 384), BF), ((768, 256), BF), ((768, 1152), BF), ((384, 768), BF)],
+        [at, own, w_qkv, w_out],
+        scratch=[pltpu.SemaphoreType.DMA((4,))],
+        smem=(0,),
+        hbm=(2, 3),
+        flops=10**9,
+        nbytes=5 * 10**6,
+        limit=46,
+    )
+    mine, theirs, *grads = call(
         main_body,
-        [((256, 768), F32), ((256, 768), BF), ((512, 768), BF)] + [((384, 384), BF)] * 6 + [((768, 384), BF)],
-        [at, own, oth, w_qkv, w_out],
-        scratch=[scr(512, 1152), scr(512, 768), scr(512, 768), scr(512, 1152), scr(512, 384), scr(384, 512),
-                 scr(384, 512), scr(384, 512), scr(384, 512), scr(384, 512), scr(768, 512), scr(768, 1152),
-                 scr(384, 768), pltpu.SemaphoreType.DMA((4,))],
+        [((256, 768), F32), ((256, 768), BF)] + [((384, 384), BF)] * 4 + [((1536, 384), BF)],
+        [at, oth, xd, *projected],
+        scratch=[scr(512, 1152), scr(512, 768), scr(512, 1152), scr(512, 384), scr(384, 512), scr(384, 512),
+                 scr(384, 512), scr(384, 512), scr(384, 512), scr(768, 512)],
         smem=(0,),
-        hbm=(3, 4),
-        limit=50,
-        flops=6 * 10**9,
+        limit=32,
+        flops=5 * 10**9,
         nbytes=10**7,
     )
-    first = spread(grads, "xy")
     got = swap(theirs)
-    ig, = call(input_gradient_body, [((16, 16, 768), BF)], [mine, got, xd], nbytes=3 * 10**6)
+    ig, keep, *others = call(
+        input_gradient_body,
+        [((16, 16, 768), BF)] + [((384, 384), BF)] * 5,
+        [mine, got, xd, swap(grads[4]), grads[0]],
+        passed={4: 1},
+        nbytes=3 * 10**6,
+    )
+    first = spread([b for pair in zip(grads[:4], others) for b in pair], "xy", (2, 1, 3), False) + [keep, others[0]]
     back = lax.all_to_all(ig, ("x", "zh"), split_axis=0, concat_axis=0, tiled=True)
-    second = call(split_body, [((96, 384), BF)] * 6 + [((192, 384), BF)], first, flops=4_000_000_000)
-    second = spread(second, "yx")
+    second = call(split_body, [((192, 384), BF)] * 4, [at, *first], smem=(0,), flops=4_000_000_000)
+    second = spread(second, "yx", (2, 1, 3, 0), True)
     ig_home, done = call(home_body, [((256, 768), BF), ((8, 128), F32)], [back])
-    slots, = call(slot_body, [((16, 8, 768), BF)], [at, done, *second], smem=(0,))
-    last = lax.all_to_all(slots, ("zh", "zl", "c"), split_axis=0, concat_axis=0, tiled=True)
+    slots, = call(slot_body, [((8, 16, 768), BF)], [done, *second])
+    last = lax.all_to_all(slots, ("zh", "zl"), split_axis=0, concat_axis=0, tiled=True)
     grad_qkv, grad_out = call(last_body, [((3, 2304), F32), ((3, 768), F32)], [last])
     return ig_home.reshape(8, 32, 768), grad_qkv, grad_out
 

time: 110 us -> 97.1 us (0.88)
  blocking collectives: 52.2 us -> 46.2 us
  local copies, waits for them, and re-layouts: 3.04 us -> 0.01 us
  waiting for transfers between devices: 10.8 us -> 8.23 us
  starting transfers between devices: 23.2 us -> 21.7 us
    all_to_all x1, blocking collectives: 18 us -> 11.8 us  [local(): lax.all_to_all(slots, ('zh', 'zl'), split_axis=0, concat_axis=0, tiled=True)]
    unnamed x8 -> x2, local copies, waits for them, and re-layouts: 3.04 us -> 0.01 us
    ppermute x12 -> x10, waiting for transfers between devices: 5.61 us -> 3.64 us  [spread(): moved.append(lax.ppermute(block, ('x', 'c', 'y'), pairs))]
    ppermute x2 -> x3, waiting for transfers between devices: 1.97 us -> 0.01 us  [swap(): return lax.ppermute(v, 'c', [(0, 1), (1, 0)])]
    ppermute x12 -> x10, starting transfers between devices: 16.3 us -> 14.7 us  [spread(): moved.append(lax.ppermute(block, ('x', 'c', 'y'), pairs))]
    all_to_all x1, waiting for transfers between devices: 3.18 us -> 4.59 us  [local(): lax.all_to_all(ig, ('x', 'zh'), split_axis=0, concat_axis=0, tiled=True)]
    pallas_call x7 -> x8, Pallas kernels: 19.6 us -> 19.7 us  [call(): pl.pallas_call(body, out_shape=[jax.ShapeDtypeStruct(s, d) for s, d in ou...]
    ppermute x2 -> x3, starting transfers between devices: 3.36 us -> 3.49 us  [swap(): return lax.ppermute(v, 'c', [(0, 1), (1, 0)])]
  transfers between devices with their start and end apart: 15 -> 14, of which waited for: 3 -> 3; matrix products, arithmetic and copies ran while one was open for 0% -> 0% of each run, Pallas kernels for 4% -> 8%
where the time goes in v4:
time: 97.1 us; the launch traced here: 96.7 us
  blocking collectives  46.2 us (48%)
  starting transfers between devices  21.7 us (22%)
  Pallas kernels  19.7 us (20%)
  waiting for transfers between devices  8.23 us (8%)
    all_to_all x1, blocking collectives, local(): lax.all_to_all(packed, ('x', 'zh'), split_axis=0, concat_axis=0, tiled=True)  34.4 us
    pallas_call x8, Pallas kernels, call(): pl.pallas_call(body, out_shape=[jax.ShapeDtypeStruct(s, d) for s, d in ou...  19.7 us
    ppermute x10, starting transfers between devices, spread(): moved.append(lax.ppermute(block, ('x', 'c', 'y'), pairs))  14.7 us
    all_to_all x1, blocking collectives, local(): lax.all_to_all(slots, ('zh', 'zl'), split_axis=0, concat_axis=0, tiled=True)  11.8 us
    all_to_all x1, waiting for transfers between devices, local(): lax.all_to_all(ig, ('x', 'zh'), split_axis=0, concat_axis=0, tiled=True)  4.59 us
    ppermute x10, waiting for transfers between devices, spread(): moved.append(lax.ppermute(block, ('x', 'c', 'y'), pairs))  3.64 us
    all_to_all x1, starting transfers between devices, local(): lax.all_to_all(ig, ('x', 'zh'), split_axis=0, concat_axis=0, tiled=True)  3.55 us
    ppermute x3, starting transfers between devices, swap(): return lax.ppermute(v, 'c', [(0, 1), (1, 0)])  3.49 us
  transfers between devices with their start and end apart: 14, of which 3 were waited for; matrix products, arithmetic and copies ran while one was open for 0% of the time, Pallas kernels for 8%

profile of v4, /device:TPU:1, one launch (start us, length us, event | category | flops | bytes accessed | tf_op | source)
XLA Modules:
  0.0 96.7 jit_solution(16045153923319952607)
XLA Ops:
  0.6 2.5 %shard_map.67 = bf16[16,32,768]{2,1,0:T(8,128)(2,1)} custom-call(bf16[256,768]{1,0:T(8,128)(2,1)} %bitcast.7, bf16[256,768]{1,0:T(8,128)(2,1)} %bitcast.8), custom_call_target="tpu_custom_call" | custom-call | tf_op jit(solution)/shard_map/pallas_call | solution.py:27
  3.1 0.0 copy-start
  3.1 34.4 %all_to_all.15.own_ref = bf16[16,32,768]{2,1,0:T(8,128)(2,1)S(1)} all-to-all(bf16[16,32,768]{2,1,0:T(8,128)(2,1)} %shard_map.67), channel_id=1, replica_groups=mesh['zh'=4,'x'=4,'c'=2,'zl'=2,'y'=4] {'x','zh'}, dimensions={0} | all-to-all | bytes 1572864 | tf_op jit(solution)/shard_map/all_to_all | solution.py:318
  37.5 3.0 %collective-permute-start = (bf16[16,32,768]{2,1,0:T(8,128)(2,1)S(1)}, bf16[16,32,768]{2,1,0:T(8,128)(2,1)S(1)}, u32[]{:S(2)}, u32[]{:S(2)}) collective-permute-start(bf16[16,32,768]{2,1,0:T(8,128)(2,1)S(1)} %all_to_all.15.own_ref), channel_id=1, source_target_pairs={{0,8},{8,0},{1,9},{9,1},{2,10},{10,2},{3,11},{11,3},{4,12},{12,4},... | collective-permute-start | bytes 2359304 | tf_op jit(solution)/shard_map/ppermute | solution.py:292
  40.5 0.1 pad_add_fusion.at_ref
  40.6 3.6 %shard_map.68 = (bf16[512,768]{1,0:T(8,128)(2,1)S(1)}, bf16[256,1152]{1,0:T(8,128)(2,1)S(1)}, bf16[256,384]{1,0:T(8,128)(2,1)S(1)}, bf16[768,256]{1,0:T(8,128)(2...) custom-call(s32[4]{0:T(128)S(1)} %pad_add_fusion.at_ref, ...), custom_call_target="tpu_custom_call" | custom-call | flops 1000000000 | bytes 5000000 | tf_op jit(solution)/shard_map/pallas_call | solution.py:27
  44.2 0.0 collective-permute-done.oth_ref
  44.2 8.5 %shard_map.69 = (f32[256,768]{1,0:T(8,128)S(1)}, bf16[256,768]{1,0:T(8,128)(2,1)S(1)}, bf16[384,384]{1,0:T(8,128)(2,1)S(1)}, bf16[384,384]{1,0:T(8,128)(2,1)}, b...) custom-call(s32[4]{0:T(128)S(1)} %pad_add_fusion.at_ref, ...), custom_call_target="tpu_custom_call" | custom-call | flops 5000000000 | bytes 10000000 | tf_op jit(solution)/shard_map/pallas_call | solution.py:27
  52.7 0.5 collective-permute-start.1
  53.2 2.9 %collective-permute-start.3 = (bf16[384,384]{1,0:T(8,128)(2,1)S(1)}, bf16[384,384]{1,0:T(8,128)(2,1)S(1)}, u32[]{:S(2)}, u32[]{:S(2)}) collective-permute-start(bf16[384,384]{1,0:T(8,128)(2,1)S(1)} %get-tuple-element.43), channel_id=1, source_target_pairs={{0,32},{8,10},{9,41},{1,3},{2,34},{10,8},{11,43},{3,1},{24,56},{16... | collective-permute-start | bytes 884744 | tf_op jit(solution)/shard_map/ppermute | solution.py:306
  56.2 0.6 collective-permute-start.5
  56.7 2.4 %collective-permute-start.7 = (bf16[384,384]{1,0:T(8,128)(2,1)S(1)}, bf16[384,384]{1,0:T(8,128)(2,1)S(1)}, u32[]{:S(2)}, u32[]{:S(2)}) collective-permute-start(bf16[384,384]{1,0:T(8,128)(2,1)S(1)} %get-tuple-element.47), channel_id=1, source_target_pairs={{0,56},{8,3},{9,49},{1,8},{2,58},{10,1},{11,51},{3,10},{24,0},{16,... | collective-permute-start | bytes 884744 | tf_op jit(solution)/shard_map/ppermute | solution.py:306
  59.1 0.0 collective-permute-done.1.got_ref
  59.1 0.0 collective-permute-done.2.blocks_ref
  59.1 1.5 %shard_map.70 = (bf16[16,16,768]{2,1,0:T(8,128)(2,1)}, bf16[384,384]{1,0:T(8,128)(2,1)S(1)}, bf16[384,384]{1,0:T(8,128)(2,1)S(1)}, bf16[384,384]{1,0:T(8,128)(2,...) custom-call(f32[256,768]{1,0:T(8,128)S(1)} %get-tuple-element.36.part_ref, ...), custom_call_target="tpu_custom_call", output_to_operand_aliasing={{1}: (4, {})} | custom-call | bytes 3000000 | tf_op jit(solution)/shard_map/pallas_call | solution.py:27
  60.6 0.0 collective-permute-start.4
  60.6 0.9 collective-permute-start.6
  61.5 0.0 collective-permute-done.3.refs_0_
  61.5 2.7 %collective-permute-start.8 = (bf16[384,384]{1,0:T(8,128)(2,1)S(1)}, bf16[384,384]{1,0:T(8,128)(2,1)}, u32[]{:S(2)}, u32[]{:S(2)}) collective-permute-start(bf16[384,384]{1,0:T(8,128)(2,1)S(1)} %get-tuple-element.48), channel_id=1, source_target_pairs={{0,56},{8,3},{9,49},{1,8},{2,58},{10,1},{11,51},{3,10},{24,0},{16,... | collective-permute-start | bytes 884744 | tf_op jit(solution)/shard_map/ppermute | solution.py:306
  64.2 3.6 %all-to-all-start.1 = ((bf16[16,16,768]{2,1,0:T(8,128)(2,1)}), bf16[16,16,768]{2,1,0:T(8,128)(2,1)S(1)}, u32[]{:S(2)}, u32[]{:S(2)}) async-start(bf16[16,16,768]{2,1,0:T(8,128)(2,1)} %get-tuple-element.40), calls=%async_computation.1 | async-start | bytes 786432 | tf_op jit(solution)/shard_map/all_to_all | solution.py:351
  67.8 0.3 collective-permute-done.4.refs_1_
  68.0 3.4 %collective-permute-done.6.refs_3_ = bf16[384,384]{1,0:T(8,128)(2,1)S(1)} collective-permute-done((bf16[384,384]{1,0:T(8,128)(2,1)}, bf16[384,384]{1,0:T(8,128)(2,1)S(1)}, u32[]{:S(2)}, u32[]{:S(2)}) %collective-permute-start.6) | collective-permute-done | bytes 294944 | tf_op jit(solution)/shard_map/ppermute | solution.py:306
  71.4 1.6 %shard_map.72 = (bf16[192,384]{1,0:T(8,128)(2,1)S(1)}, bf16[192,384]{1,0:T(8,128)(2,1)S(1)}, bf16[192,384]{1,0:T(8,128)(2,1)S(1)}, bf16[192,384]{1,0:T(8,128)(2,1)S(1)}) custom-call(s32[4]{0:T(128)S(1)} %pad_add_fusion.at_ref, bf16[384,384]{1,0:T(8,128)(2,1)S(1)} %collective-permute-done.3.refs_0_, bf16[384,384]{1,0:T(8,128)(2,1)S(1)} %collective-permute-done.4.refs_1_, ...), custom_call_target="tpu_custom_call" | custom-call | flops 4000000000 | tf_op jit(solution)/shard_map/pallas_call | solution.py:27
  73.0 0.4 collective-permute-start.9
  73.5 1.0 %collective-permute-start.10 = (bf16[192,384]{1,0:T(8,128)(2,1)S(1)}, bf16[192,384]{1,0:T(8,128)(2,1)S(1)}, u32[]{:S(2)}, u32[]{:S(2)}) collective-permute-start(bf16[192,384]{1,0:T(8,128)(2,1)S(1)} %get-tuple-element.52), channel_id=1, source_target_pairs={{0,1},{8,24},{9,2},{1,25},{2,3},{10,26},{11,0},{3,27},{24,17},{16,... | collective-permute-start | bytes 442376 | tf_op jit(solution)/shard_map/ppermute | solution.py:306
  74.5 3.1 %collective-permute-start.11 = (bf16[192,384]{1,0:T(8,128)(2,1)S(1)}, bf16[192,384]{1,0:T(8,128)(2,1)S(1)}, u32[]{:S(2)}, u32[]{:S(2)}) collective-permute-start(bf16[192,384]{1,0:T(8,128)(2,1)S(1)} %get-tuple-element.53), channel_id=1, source_target_pairs={{0,3},{8,56},{9,0},{1,57},{2,1},{10,58},{11,2},{3,59},{24,19},{16,... | collective-permute-start | bytes 442376 | tf_op jit(solution)/shard_map/ppermute | solution.py:306
  77.6 0.7 collective-permute-start.12
  78.3 4.6 %all-to-all-done.1.r_ref = bf16[16,16,768]{2,1,0:T(8,128)(2,1)S(1)} async-done(((bf16[16,16,768]{2,1,0:T(8,128)(2,1)}), bf16[16,16,768]{2,1,0:T(8,128)(2,1)S(1)}, u32[]{:S(2)}, u32[]{:S(2)}) %all-to-all-start.1) | async-done | bytes 393248 | tf_op jit(solution)/shard_map/all_to_all | solution.py:351
  82.9 1.1 %shard_map.71 = (bf16[256,768]{1,0:T(8,128)(2,1)}, f32[8,128]{1,0:T(8,128)S(1)}) custom-call(bf16[16,16,768]{2,1,0:T(8,128)(2,1)S(1)} %all-to-all-done.1.r_ref), custom_call_target="tpu_custom_call" | custom-call | tf_op jit(solution)/shard_map/pallas_call | solution.py:27
  83.9 0.3 shard_map.73
  84.2 11.8 %all_to_all.16.r_ref = bf16[8,16,768]{2,1,0:T(8,128)(2,1)S(1)} all-to-all(bf16[8,16,768]{2,1,0:T(8,128)(2,1)S(1)} %shard_map.73), channel_id=1, replica_groups=mesh['zh'=4,'x'=4,'c'=2,'zl'=2,'y'=4] {'zh','zl'}, dimensions={0} | all-to-all | bytes 393216 | tf_op jit(solution)/shard_map/all_to_all | solution.py:356
  96.1 0.7 shard_map.74
  (9 shorter events, 0.0 us)
Async XLA Ops:
  3.1 37.5 %copy-start = (bf16[768,768]{1,0:T(8,128)(2,1)S(1)}, bf16[768,768]{1,0:T(8,128)(2,1)}, u32[]{:S(2)}) copy-start(bf16[768,768]{1,0:T(8,128)(2,1)} %wout_ref.1) | copy-start | bytes 3538948
  37.5 6.7 %collective-permute-start = (bf16[16,32,768]{2,1,0:T(8,128)(2,1)S(1)}, bf16[16,32,768]{2,1,0:T(8,128)(2,1)S(1)}, u32[]{:S(2)}, u32[]{:S(2)}) collective-permute-start(bf16[16,32,768]{2,1,0:T(8,128)(2,1)S(1)} %all_to_all.15.own_ref), channel_id=1, source_target_pairs={{0,8},{8,0},{1,9},{9,1},{2,10},{10,2},{3,11},{11,3},{4,12},{12,4},... | collective-permute-start | bytes 2359304 | tf_op jit(solution)/shard_map/ppermute | solution.py:292
  52.7 6.4 %collective-permute-start.2 = (bf16[1536,384]{1,0:T(8,128)(2,1)S(1)}, bf16[1536,384]{1,0:T(8,128)(2,1)S(1)}, u32[]{:S(2)}, u32[]{:S(2)}) collective-permute-start(bf16[1536,384]{1,0:T(8,128)(2,1)S(1)} %get-tuple-element.38), channel_id=1, source_target_pairs={{0,8},{8,0},{1,9},{9,1},{2,10},{10,2},{3,11},{11,3},{4,12},{12,4},... | collective-permute-start | bytes 3538952 | tf_op jit(solution)/shard_map/ppermute | solution.py:292
  52.7 6.4 %collective-permute-start.1 = (bf16[256,768]{1,0:T(8,128)(2,1)S(1)}, bf16[256,768]{1,0:T(8,128)(2,1)S(1)}, u32[]{:S(2)}, u32[]{:S(2)}) collective-permute-start(bf16[256,768]{1,0:T(8,128)(2,1)S(1)} %get-tuple-element.37), channel_id=1, source_target_pairs={{0,8},{8,0},{1,9},{9,1},{2,10},{10,2},{3,11},{11,3},{4,12},{12,4},... | collective-permute-start | bytes 1179656 | tf_op jit(solution)/shard_map/ppermute | solution.py:292
  53.2 8.3 %collective-permute-start.3 = (bf16[384,384]{1,0:T(8,128)(2,1)S(1)}, bf16[384,384]{1,0:T(8,128)(2,1)S(1)}, u32[]{:S(2)}, u32[]{:S(2)}) collective-permute-start(bf16[384,384]{1,0:T(8,128)(2,1)S(1)} %get-tuple-element.43), channel_id=1, source_target_pairs={{0,32},{8,10},{9,41},{1,3},{2,34},{10,8},{11,43},{3,1},{24,56},{16... | collective-permute-start | bytes 884744 | tf_op jit(solution)/shard_map/ppermute | solution.py:306
  56.2 11.6 %collective-permute-start.5 = (bf16[384,384]{1,0:T(8,128)(2,1)}, bf16[384,384]{1,0:T(8,128)(2,1)S(1)}, u32[]{:S(2)}, u32[]{:S(2)}) collective-permute-start(bf16[384,384]{1,0:T(8,128)(2,1)} %get-tuple-element.45), channel_id=1, source_target_pairs={{0,24},{8,1},{9,17},{1,10},{2,26},{10,3},{11,19},{3,8},{24,32},{16... | collective-permute-start | bytes 884744 | tf_op jit(solution)/shard_map/ppermute | solution.py:306
  56.7 11.0 %collective-permute-start.7 = (bf16[384,384]{1,0:T(8,128)(2,1)S(1)}, bf16[384,384]{1,0:T(8,128)(2,1)S(1)}, u32[]{:S(2)}, u32[]{:S(2)}) collective-permute-start(bf16[384,384]{1,0:T(8,128)(2,1)S(1)} %get-tuple-element.47), channel_id=1, source_target_pairs={{0,56},{8,3},{9,49},{1,8},{2,58},{10,1},{11,51},{3,10},{24,0},{16,... | collective-permute-start | bytes 884744 | tf_op jit(solution)/shard_map/ppermute | solution.py:306
  60.6 7.4 %collective-permute-start.4 = (bf16[384,384]{1,0:T(8,128)(2,1)}, bf16[384,384]{1,0:T(8,128)(2,1)S(1)}, u32[]{:S(2)}, u32[]{:S(2)}) collective-permute-start(bf16[384,384]{1,0:T(8,128)(2,1)} %get-tuple-element.44), channel_id=1, source_target_pairs={{0,32},{8,10},{9,41},{1,3},{2,34},{10,8},{11,43},{3,1},{24,56},{16... | collective-permute-start | bytes 884744 | tf_op jit(solution)/shard_map/ppermute | solution.py:306
  60.6 10.7 %collective-permute-start.6 = (bf16[384,384]{1,0:T(8,128)(2,1)}, bf16[384,384]{1,0:T(8,128)(2,1)S(1)}, u32[]{:S(2)}, u32[]{:S(2)}) collective-permute-start(bf16[384,384]{1,0:T(8,128)(2,1)} %get-tuple-element.46), channel_id=1, source_target_pairs={{0,24},{8,1},{9,17},{1,10},{2,26},{10,3},{11,19},{3,8},{24,32},{16... | collective-permute-start | bytes 884744 | tf_op jit(solution)/shard_map/ppermute | solution.py:306
  61.5 9.9 %collective-permute-start.8 = (bf16[384,384]{1,0:T(8,128)(2,1)S(1)}, bf16[384,384]{1,0:T(8,128)(2,1)}, u32[]{:S(2)}, u32[]{:S(2)}) collective-permute-start(bf16[384,384]{1,0:T(8,128)(2,1)S(1)} %get-tuple-element.48), channel_id=1, source_target_pairs={{0,56},{8,3},{9,49},{1,8},{2,58},{10,1},{11,51},{3,10},{24,0},{16,... | collective-permute-start | bytes 884744 | tf_op jit(solution)/shard_map/ppermute | solution.py:306
  64.2 18.7 %all-to-all-start.1 = ((bf16[16,16,768]{2,1,0:T(8,128)(2,1)}), bf16[16,16,768]{2,1,0:T(8,128)(2,1)S(1)}, u32[]{:S(2)}, u32[]{:S(2)}) async-start(bf16[16,16,768]{2,1,0:T(8,128)(2,1)} %get-tuple-element.40), calls=%async_computation.1 | async-start | bytes 786432 | tf_op jit(solution)/shard_map/all_to_all | solution.py:351
  73.0 10.9 %collective-permute-start.9 = (bf16[192,384]{1,0:T(8,128)(2,1)S(1)}, bf16[192,384]{1,0:T(8,128)(2,1)S(1)}, u32[]{:S(2)}, u32[]{:S(2)}) collective-permute-start(bf16[192,384]{1,0:T(8,128)(2,1)S(1)} %get-tuple-element.51), channel_id=1, source_target_pairs={{0,2},{8,40},{9,3},{1,41},{2,0},{10,42},{11,1},{3,43},{24,18},{16,... | collective-permute-start | bytes 442376 | tf_op jit(solution)/shard_map/ppermute | solution.py:306
  73.5 10.5 %collective-permute-start.10 = (bf16[192,384]{1,0:T(8,128)(2,1)S(1)}, bf16[192,384]{1,0:T(8,128)(2,1)S(1)}, u32[]{:S(2)}, u32[]{:S(2)}) collective-permute-start(bf16[192,384]{1,0:T(8,128)(2,1)S(1)} %get-tuple-element.52), channel_id=1, source_target_pairs={{0,1},{8,24},{9,2},{1,25},{2,3},{10,26},{11,0},{3,27},{24,17},{16,... | collective-permute-start | bytes 442376 | tf_op jit(solution)/shard_map/ppermute | solution.py:306
  74.5 9.4 %collective-permute-start.11 = (bf16[192,384]{1,0:T(8,128)(2,1)S(1)}, bf16[192,384]{1,0:T(8,128)(2,1)S(1)}, u32[]{:S(2)}, u32[]{:S(2)}) collective-permute-start(bf16[192,384]{1,0:T(8,128)(2,1)S(1)} %get-tuple-element.53), channel_id=1, source_target_pairs={{0,3},{8,56},{9,0},{1,57},{2,1},{10,58},{11,2},{3,59},{24,19},{16,... | collective-permute-start | bytes 442376 | tf_op jit(solution)/shard_map/ppermute | solution.py:306
  77.6 6.3 %collective-permute-start.12 = (bf16[192,384]{1,0:T(8,128)(2,1)S(1)}, bf16[192,384]{1,0:T(8,128)(2,1)S(1)}, u32[]{:S(2)}, u32[]{:S(2)}) collective-permute-start(bf16[192,384]{1,0:T(8,128)(2,1)S(1)} %get-tuple-element.54), channel_id=1, source_target_pairs={{0,0},{8,8},{9,1},{1,9},{2,2},{10,10},{11,3},{3,11},{24,16},{16,24... | collective-permute-start | bytes 442376 | tf_op jit(solution)/shard_map/ppermute | solution.py:306

commit v5 on v4

--- a/solution.py
+++ b/solution.py
@@ -87,7 +87,9 @@
     j = rem - 3 * d
     row = jnp.where(big, jnp.where(m < 2, j, 3 + (j >> 1)), 5 + j)
     half = jnp.where(big, jnp.where(m < 2, m, j & 1), hh)
-    return ((d + jnp.where(big, 0, 4 * k)) << 4) + (k << 3) + row, half
+    d = d + jnp.where(big, 0, 4 * k)
+    slot = ((d & 1) << 2) + (d & 2) + (d >> 2)
+    return (slot << 4) + (k << 3) + row, half
 
 
 def pack_body(x_ref, d_ref, o_ref, x_s, d_s, sems):
@@ -220,6 +222,7 @@
 
 
 def input_gradient_body(part_ref, got_ref, xd_ref, blocks_ref, keep_ref, o_ref, same_ref, *block_refs):
+    same_ref[...] = keep_ref[...]
     for s in range(4):
         block_refs[s][...] = blocks_ref[s * 384 : (s + 1) * 384]
     outs = []
@@ -251,7 +254,7 @@
             refs[8 + t][rows] = out[t * 96 : (t + 1) * 96]
 
 
-def slot_body(done_ref, *refs):
+def slot_body(back_ref, *refs):
     total = added(refs[:4])
     slot, half = slot_order()
     for h in range(2):
@@ -259,16 +262,12 @@
         refs[4][:, :, h * 384 : (h + 1) * 384] = part.reshape(8, 16, 384)
 
 
-def home_body(r_ref, ig_ref, done_ref):
+def last_body(r_ref, ig_ref, gq_ref, go_ref, home_ref):
     sel = selection(256, home_order())
     back = lax.dot_general(
-        sel, r_ref[...].reshape(256, 768), (((0,), (0,)), ((), ())), preferred_element_type=F32
-    )
-    ig_ref[...] = back.astype(BF)
-    done_ref[...] = jnp.zeros_like(done_ref)
-
-
-def last_body(r_ref, gq_ref, go_ref):
+        sel, ig_ref[...].reshape(256, 768), (((0,), (0,)), ((), ())), preferred_element_type=F32
+    )
+    home_ref[...] = back.astype(BF)
     total = r_ref[0].astype(F32)
     for z in range(1, 8):
         total = total + r_ref[z].astype(F32)
@@ -284,7 +283,7 @@
 
 
 def local(x, d, w_qkv, w_out):
-    core, x0, y0 = (lax.axis_index(a) for a in ("c", "x", "y"))
+    core, x0, y0 = (lax.axis_index(a) for a in ("c", ("x1", "x0"), "y"))
     role = core ^ ((x0 + y0) & 1)
     at = jnp.stack([core, x0, y0, role]).astype(jnp.int32)
 
@@ -303,7 +302,7 @@
                         pairs.append(((x * 2 + c) * 4 + y, (u * 2 + d) * 4 + v))
             each = len(blocks) // 4
             for block in blocks[s * each : s * each + each]:
-                moved.append(lax.ppermute(block, ("x", "c", "y"), pairs))
+                moved.append(lax.ppermute(block, ("x1", "x0", "c", "y"), pairs))
         return moved
 
     scr = lambda *s: pltpu.VMEM(s, BF)
@@ -315,7 +314,7 @@
         hbm=(0, 1),
         limit=60,
     )
-    own = lax.all_to_all(packed, ("x", "zh"), split_axis=0, concat_axis=0, tiled=True)
+    own = lax.all_to_all(packed, ("x1", "x0", "zh0", "zh1"), split_axis=0, concat_axis=0, tiled=True)
     oth = swap(own)
     xd, *projected = call(
         own_body,
@@ -344,23 +343,21 @@
         input_gradient_body,
         [((16, 16, 768), BF)] + [((384, 384), BF)] * 5,
         [mine, got, xd, swap(grads[4]), grads[0]],
-        passed={4: 1},
         nbytes=3 * 10**6,
     )
     first = spread([b for pair in zip(grads[:4], others) for b in pair], "xy", (2, 1, 3), False) + [keep, others[0]]
-    back = lax.all_to_all(ig, ("x", "zh"), split_axis=0, concat_axis=0, tiled=True)
+    back = lax.all_to_all(ig, ("x1", "x0", "zh0", "zh1"), split_axis=0, concat_axis=0, tiled=True)
     second = call(split_body, [((192, 384), BF)] * 4, [at, *first], smem=(0,), flops=4_000_000_000)
     second = spread(second, "yx", (2, 1, 3, 0), True)
-    ig_home, done = call(home_body, [((256, 768), BF), ((8, 128), F32)], [back])
-    slots, = call(slot_body, [((8, 16, 768), BF)], [done, *second])
-    last = lax.all_to_all(slots, ("zh", "zl"), split_axis=0, concat_axis=0, tiled=True)
-    grad_qkv, grad_out = call(last_body, [((3, 2304), F32), ((3, 768), F32)], [last])
+    slots, = call(slot_body, [((8, 16, 768), BF)], [back, *second], hbm=(0,))
+    last = lax.all_to_all(slots, ("zl", "zh0", "zh1"), split_axis=0, concat_axis=0, tiled=True)
+    grad_qkv, grad_out, ig_home = call(last_body, [((3, 2304), F32), ((3, 768), F32), ((256, 768), BF)], [last, back])
     return ig_home.reshape(8, 32, 768), grad_qkv, grad_out
 
 
 def solution(mesh):
-    fine = Mesh(mesh.devices.reshape(4, 4, 2, 2, 4), ("zh", "x", "c", "zl", "y"))
-    tm, space = ("zh", "x", "c"), ("zl", "y")
+    fine = Mesh(mesh.devices.reshape(2, 2, 2, 2, 2, 2, 4), ("zh1", "zh0", "x1", "x0", "c", "zl", "y"))
+    tm, space = ("zh1", "zh0", "x1", "x0", "c"), ("zl", "y")
     tokens, rows = P(tm, space, None), P(tm + space, None)
     return jax.shard_map(
         local,

time: 97.1 us -> 93.2 us (0.960)
  blocking collectives: 46.2 us -> 43.7 us
  waiting for transfers between devices: 8.23 us -> 6.16 us
  Pallas kernels: 19.7 us -> 18.4 us
  starting transfers between devices: 21.7 us -> 22.9 us
    all_to_all x1, waiting for transfers between devices: 4.59 us -> 0.01 us  [local(): lax.all_to_all(ig, ('x1', 'x0', 'zh0', 'zh1'), split_axis=0, concat_axis=...]
    ppermute x10, waiting for transfers between devices: 3.64 us -> 6.15 us  [spread(): moved.append(lax.ppermute(block, ('x1', 'x0', 'c', 'y'), pairs))]
    all_to_all x2, blocking collectives: 46.2 us -> 43.7 us  [the longest x1 32.9 us: local(): lax.all_to_all(packed, ('x1', 'x0', 'zh0', 'zh1'), split_axis=0, concat_a...]
    pallas_call x8 -> x7, Pallas kernels: 19.7 us -> 18.4 us  [call(): pl.pallas_call(body, out_shape=[jax.ShapeDtypeStruct(s, d) for s, d in ou...]
  transfers between devices with their start and end apart: 14 -> 14, of which waited for: 3 -> 4; matrix products, arithmetic and copies ran while one was open for 0% -> 0% of each run, Pallas kernels for 8% -> 7%
where the time goes in v5:
time: 93.2 us; the launch traced here: 92 us
  blocking collectives  43.7 us (47%)
  starting transfers between devices  22.9 us (25%)
  Pallas kernels  18.4 us (20%)
  waiting for transfers between devices  6.16 us (7%)
    all_to_all x1, blocking collectives, local(): lax.all_to_all(packed, ('x1', 'x0', 'zh0', 'zh1'), split_axis=0, concat_a...  32.9 us
    pallas_call x7, Pallas kernels, call(): pl.pallas_call(body, out_shape=[jax.ShapeDtypeStruct(s, d) for s, d in ou...  18.4 us
    ppermute x10, starting transfers between devices, spread(): moved.append(lax.ppermute(block, ('x1', 'x0', 'c', 'y'), pairs))  15.4 us
    all_to_all x1, blocking collectives, local(): lax.all_to_all(slots, ('zl', 'zh0', 'zh1'), split_axis=0, concat_axis=0,...  10.9 us
    ppermute x10, waiting for transfers between devices, spread(): moved.append(lax.ppermute(block, ('x1', 'x0', 'c', 'y'), pairs))  6.15 us
    ppermute x3, starting transfers between devices, swap(): return lax.ppermute(v, 'c', [(0, 1), (1, 0)])  4 us
    all_to_all x1, starting transfers between devices, local(): lax.all_to_all(ig, ('x1', 'x0', 'zh0', 'zh1'), split_axis=0, concat_axis=...  3.56 us
  transfers between devices with their start and end apart: 14, of which 4 were waited for; matrix products, arithmetic and copies ran while one was open for 0% of the time, Pallas kernels for 7%

profile of v5, /device:TPU:1, one launch (start us, length us, event | category | flops | bytes accessed | tf_op | source)
XLA Modules:
  0.0 92.0 jit_solution(15679563755826877629)
XLA Ops:
  0.6 2.5 %shard_map.67 = bf16[16,32,768]{2,1,0:T(8,128)(2,1)} custom-call(bf16[256,768]{1,0:T(8,128)(2,1)} %bitcast.7, bf16[256,768]{1,0:T(8,128)(2,1)} %bitcast.8), custom_call_target="tpu_custom_call" | custom-call | tf_op jit(solution)/shard_map/pallas_call | solution.py:27
  3.1 0.0 copy-start
  3.1 32.9 %all_to_all.15.own_ref = bf16[16,32,768]{2,1,0:T(8,128)(2,1)S(1)} all-to-all(bf16[16,32,768]{2,1,0:T(8,128)(2,1)} %shard_map.67), channel_id=1, replica_groups=mesh['zh1'=2,'zh0'=2,'x1'=2,'x0'=2,'c'=2,'zl'=2,'y'=4] {'x1','x0','zh0',..., dimensions={0} | all-to-all | bytes 1572864 | tf_op jit(solution)/shard_map/all_to_all | solution.py:317
  36.0 3.4 %collective-permute-start = (bf16[16,32,768]{2,1,0:T(8,128)(2,1)S(1)}, bf16[16,32,768]{2,1,0:T(8,128)(2,1)S(1)}, u32[]{:S(2)}, u32[]{:S(2)}) collective-permute-start(bf16[16,32,768]{2,1,0:T(8,128)(2,1)S(1)} %all_to_all.15.own_ref), channel_id=1, source_target_pairs={{0,8},{8,0},{1,9},{9,1},{2,10},{10,2},{3,11},{11,3},{4,12},{12,4},... | collective-permute-start | bytes 2359304 | tf_op jit(solution)/shard_map/ppermute | solution.py:291
  39.4 0.1 pad_add_fusion.at_ref
  39.5 3.6 %shard_map.68 = (bf16[512,768]{1,0:T(8,128)(2,1)S(1)}, bf16[256,1152]{1,0:T(8,128)(2,1)S(1)}, bf16[256,384]{1,0:T(8,128)(2,1)S(1)}, bf16[768,256]{1,0:T(8,128)(2...) custom-call(s32[4]{0:T(128)S(1)} %pad_add_fusion.at_ref, ...), custom_call_target="tpu_custom_call" | custom-call | flops 1000000000 | bytes 5000000 | tf_op jit(solution)/shard_map/pallas_call | solution.py:27
  43.1 0.0 collective-permute-done.oth_ref
  43.2 7.8 %shard_map.69 = (f32[256,768]{1,0:T(8,128)S(1)}, bf16[256,768]{1,0:T(8,128)(2,1)S(1)}, bf16[384,384]{1,0:T(8,128)(2,1)S(1)}, bf16[384,384]{1,0:T(8,128)(2,1)S(1)...) custom-call(s32[4]{0:T(128)S(1)} %pad_add_fusion.at_ref, ...), custom_call_target="tpu_custom_call" | custom-call | flops 5000000000 | bytes 10000000 | tf_op jit(solution)/shard_map/pallas_call | solution.py:27
  50.9 0.1 collective-permute-start.2
  51.0 0.5 collective-permute-start.1
  51.5 2.8 %collective-permute-start.3 = (bf16[384,384]{1,0:T(8,128)(2,1)S(1)}, bf16[384,384]{1,0:T(8,128)(2,1)S(1)}, u32[]{:S(2)}, u32[]{:S(2)}) collective-permute-start(bf16[384,384]{1,0:T(8,128)(2,1)S(1)} %get-tuple-element.40), channel_id=1, source_target_pairs={{0,32},{8,10},{9,41},{1,3},{2,34},{10,8},{11,43},{3,1},{24,56},{16... | collective-permute-start | bytes 884744 | tf_op jit(solution)/shard_map/ppermute | solution.py:305
  54.4 0.7 collective-permute-start.5
  55.0 2.3 %collective-permute-start.7 = (bf16[384,384]{1,0:T(8,128)(2,1)S(1)}, bf16[384,384]{1,0:T(8,128)(2,1)S(1)}, u32[]{:S(2)}, u32[]{:S(2)}) collective-permute-start(bf16[384,384]{1,0:T(8,128)(2,1)S(1)} %get-tuple-element.44), channel_id=1, source_target_pairs={{0,56},{8,3},{9,49},{1,8},{2,58},{10,1},{11,51},{3,10},{24,0},{16,... | collective-permute-start | bytes 884744 | tf_op jit(solution)/shard_map/ppermute | solution.py:305
  57.3 1.5 %shard_map.70 = (bf16[16,16,768]{2,1,0:T(8,128)(2,1)}, bf16[384,384]{1,0:T(8,128)(2,1)S(1)}, bf16[384,384]{1,0:T(8,128)(2,1)S(1)}, bf16[384,384]{1,0:T(8,128)(2,...) custom-call(f32[256,768]{1,0:T(8,128)S(1)} %get-tuple-element.35.part_ref, ...), custom_call_target="tpu_custom_call" | custom-call | bytes 3000000 | tf_op jit(solution)/shard_map/pallas_call | solution.py:27
  58.8 0.0 collective-permute-start.4
  58.8 0.9 collective-permute-start.6
  59.7 0.0 collective-permute-done.3.refs_0_
  59.7 2.8 %collective-permute-start.8 = (bf16[384,384]{1,0:T(8,128)(2,1)S(1)}, bf16[384,384]{1,0:T(8,128)(2,1)}, u32[]{:S(2)}, u32[]{:S(2)}) collective-permute-start(bf16[384,384]{1,0:T(8,128)(2,1)S(1)} %get-tuple-element.45), channel_id=1, source_target_pairs={{0,56},{8,3},{9,49},{1,8},{2,58},{10,1},{11,51},{3,10},{24,0},{16,... | collective-permute-start | bytes 884744 | tf_op jit(solution)/shard_map/ppermute | solution.py:305
  62.5 3.6 %all-to-all-start.1 = ((bf16[16,16,768]{2,1,0:T(8,128)(2,1)}), bf16[16,16,768]{2,1,0:T(8,128)(2,1)S(1)}, u32[]{:S(2)}, u32[]{:S(2)}) async-start(bf16[16,16,768]{2,1,0:T(8,128)(2,1)} %get-tuple-element.39), calls=%async_computation.1 | async-start | bytes 786432 | tf_op jit(solution)/shard_map/all_to_all | solution.py:349
  66.1 0.0 collective-permute-done.7.refs_4_
  66.1 0.1 collective-permute-done.4.refs_1_
  66.2 3.1 %collective-permute-done.6.refs_3_ = bf16[384,384]{1,0:T(8,128)(2,1)S(1)} collective-permute-done((bf16[384,384]{1,0:T(8,128)(2,1)}, bf16[384,384]{1,0:T(8,128)(2,1)S(1)}, u32[]{:S(2)}, u32[]{:S(2)}) %collective-permute-start.6) | collective-permute-done | bytes 294944 | tf_op jit(solution)/shard_map/ppermute | solution.py:305
  69.3 1.6 %shard_map.71 = (bf16[192,384]{1,0:T(8,128)(2,1)S(1)}, bf16[192,384]{1,0:T(8,128)(2,1)S(1)}, bf16[192,384]{1,0:T(8,128)(2,1)S(1)}, bf16[192,384]{1,0:T(8,128)(2,1)S(1)}) custom-call(s32[4]{0:T(128)S(1)} %pad_add_fusion.at_ref, bf16[384,384]{1,0:T(8,128)(2,1)S(1)} %collective-permute-done.3.refs_0_, bf16[384,384]{1,0:T(8,128)(2,1)S(1)} %collective-permute-done.4.refs_1_, ...), custom_call_target="tpu_custom_call" | custom-call | flops 4000000000 | tf_op jit(solution)/shard_map/pallas_call | solution.py:27
  70.9 1.5 %collective-permute-start.9 = (bf16[192,384]{1,0:T(8,128)(2,1)S(1)}, bf16[192,384]{1,0:T(8,128)(2,1)S(1)}, u32[]{:S(2)}, u32[]{:S(2)}) collective-permute-start(bf16[192,384]{1,0:T(8,128)(2,1)S(1)} %get-tuple-element.48), channel_id=1, source_target_pairs={{0,2},{8,40},{9,3},{1,41},{2,0},{10,42},{11,1},{3,43},{24,18},{16,... | collective-permute-start | bytes 442376 | tf_op jit(solution)/shard_map/ppermute | solution.py:305
  72.4 1.5 %collective-permute-start.10 = (bf16[192,384]{1,0:T(8,128)(2,1)S(1)}, bf16[192,384]{1,0:T(8,128)(2,1)S(1)}, u32[]{:S(2)}, u32[]{:S(2)}) collective-permute-start(bf16[192,384]{1,0:T(8,128)(2,1)S(1)} %get-tuple-element.49), channel_id=1, source_target_pairs={{0,1},{8,24},{9,2},{1,25},{2,3},{10,26},{11,0},{3,27},{24,17},{16,... | collective-permute-start | bytes 442376 | tf_op jit(solution)/shard_map/ppermute | solution.py:305
  73.9 2.3 %collective-permute-start.11 = (bf16[192,384]{1,0:T(8,128)(2,1)S(1)}, bf16[192,384]{1,0:T(8,128)(2,1)S(1)}, u32[]{:S(2)}, u32[]{:S(2)}) collective-permute-start(bf16[192,384]{1,0:T(8,128)(2,1)S(1)} %get-tuple-element.50), channel_id=1, source_target_pairs={{0,3},{8,56},{9,0},{1,57},{2,1},{10,58},{11,2},{3,59},{24,19},{16,... | collective-permute-start | bytes 442376 | tf_op jit(solution)/shard_map/ppermute | solution.py:305
  76.2 0.7 collective-permute-start.12
  76.9 0.1 collective-permute-done.9.refs_0_
  76.9 2.9 %collective-permute-done.10.refs_1_ = bf16[192,384]{1,0:T(8,128)(2,1)S(1)} collective-permute-done((bf16[192,384]{1,0:T(8,128)(2,1)S(1)}, bf16[192,384]{1,0:T(8,128)(2,1)S(1)}, u32[]{:S(2)}, u32[]{:S(2)}) %collective-permute-start.10) | collective-permute-done | bytes 147488 | tf_op jit(solution)/shard_map/ppermute | solution.py:305
  79.8 0.3 shard_map.72
  80.1 10.9 %all_to_all.16.r_ref = bf16[8,16,768]{2,1,0:T(8,128)(2,1)S(1)} all-to-all(bf16[8,16,768]{2,1,0:T(8,128)(2,1)S(1)} %shard_map.72), channel_id=1, replica_groups=mesh['zh1'=2,'zh0'=2,'x1'=2,'x0'=2,'c'=2,'zl'=2,'y'=4] {'zl','zh0','zh1'}, dimensions={0} | all-to-all | bytes 393216 | tf_op jit(solution)/shard_map/all_to_all | solution.py:353
  91.0 1.1 %shard_map.73 = (f32[3,2304]{1,0:T(4,128)}, f32[3,768]{1,0:T(4,128)}, bf16[256,768]{1,0:T(8,128)(2,1)}) custom-call(bf16[8,16,768]{2,1,0:T(8,128)(2,1)S(1)} %all_to_all.16.r_ref, bf16[16,16,768]{2,1,0:T(8,128)(2,1)S(1)} %all-to-all-done.1.back_ref.ig_ref), custom_call_target="tpu_custom_call" | custom-call | tf_op jit(solution)/shard_map/pallas_call | solution.py:27
  (8 shorter events, 0.0 us)
Async XLA Ops:
  3.1 36.4 %copy-start = (bf16[768,768]{1,0:T(8,128)(2,1)S(1)}, bf16[768,768]{1,0:T(8,128)(2,1)}, u32[]{:S(2)}) copy-start(bf16[768,768]{1,0:T(8,128)(2,1)} %wout_ref.1) | copy-start | bytes 3538948
  36.0 7.1 %collective-permute-start = (bf16[16,32,768]{2,1,0:T(8,128)(2,1)S(1)}, bf16[16,32,768]{2,1,0:T(8,128)(2,1)S(1)}, u32[]{:S(2)}, u32[]{:S(2)}) collective-permute-start(bf16[16,32,768]{2,1,0:T(8,128)(2,1)S(1)} %all_to_all.15.own_ref), channel_id=1, source_target_pairs={{0,8},{8,0},{1,9},{9,1},{2,10},{10,2},{3,11},{11,3},{4,12},{12,4},... | collective-permute-start | bytes 2359304 | tf_op jit(solution)/shard_map/ppermute | solution.py:291
  50.9 6.4 %collective-permute-start.2 = (bf16[1536,384]{1,0:T(8,128)(2,1)S(1)}, bf16[1536,384]{1,0:T(8,128)(2,1)S(1)}, u32[]{:S(2)}, u32[]{:S(2)}) collective-permute-start(bf16[1536,384]{1,0:T(8,128)(2,1)S(1)} %get-tuple-element.37), channel_id=1, source_target_pairs={{0,8},{8,0},{1,9},{9,1},{2,10},{10,2},{3,11},{11,3},{4,12},{12,4},... | collective-permute-start | bytes 3538952 | tf_op jit(solution)/shard_map/ppermute | solution.py:291
  51.0 6.3 %collective-permute-start.1 = (bf16[256,768]{1,0:T(8,128)(2,1)S(1)}, bf16[256,768]{1,0:T(8,128)(2,1)S(1)}, u32[]{:S(2)}, u32[]{:S(2)}) collective-permute-start(bf16[256,768]{1,0:T(8,128)(2,1)S(1)} %get-tuple-element.36), channel_id=1, source_target_pairs={{0,8},{8,0},{1,9},{9,1},{2,10},{10,2},{3,11},{11,3},{4,12},{12,4},... | collective-permute-start | bytes 1179656 | tf_op jit(solution)/shard_map/ppermute | solution.py:291
  51.5 8.1 %collective-permute-start.3 = (bf16[384,384]{1,0:T(8,128)(2,1)S(1)}, bf16[384,384]{1,0:T(8,128)(2,1)S(1)}, u32[]{:S(2)}, u32[]{:S(2)}) collective-permute-start(bf16[384,384]{1,0:T(8,128)(2,1)S(1)} %get-tuple-element.40), channel_id=1, source_target_pairs={{0,32},{8,10},{9,41},{1,3},{2,34},{10,8},{11,43},{3,1},{24,56},{16... | collective-permute-start | bytes 884744 | tf_op jit(solution)/shard_map/ppermute | solution.py:305
  54.4 11.7 %collective-permute-start.5 = (bf16[384,384]{1,0:T(8,128)(2,1)S(1)}, bf16[384,384]{1,0:T(8,128)(2,1)S(1)}, u32[]{:S(2)}, u32[]{:S(2)}) collective-permute-start(bf16[384,384]{1,0:T(8,128)(2,1)S(1)} %get-tuple-element.42), channel_id=1, source_target_pairs={{0,24},{8,1},{9,17},{1,10},{2,26},{10,3},{11,19},{3,8},{24,32},{16... | collective-permute-start | bytes 884744 | tf_op jit(solution)/shard_map/ppermute | solution.py:305
  55.0 11.0 %collective-permute-start.7 = (bf16[384,384]{1,0:T(8,128)(2,1)S(1)}, bf16[384,384]{1,0:T(8,128)(2,1)S(1)}, u32[]{:S(2)}, u32[]{:S(2)}) collective-permute-start(bf16[384,384]{1,0:T(8,128)(2,1)S(1)} %get-tuple-element.44), channel_id=1, source_target_pairs={{0,56},{8,3},{9,49},{1,8},{2,58},{10,1},{11,51},{3,10},{24,0},{16,... | collective-permute-start | bytes 884744 | tf_op jit(solution)/shard_map/ppermute | solution.py:305
  58.8 7.4 %collective-permute-start.4 = (bf16[384,384]{1,0:T(8,128)(2,1)}, bf16[384,384]{1,0:T(8,128)(2,1)S(1)}, u32[]{:S(2)}, u32[]{:S(2)}) collective-permute-start(bf16[384,384]{1,0:T(8,128)(2,1)} %get-tuple-element.41), channel_id=1, source_target_pairs={{0,32},{8,10},{9,41},{1,3},{2,34},{10,8},{11,43},{3,1},{24,56},{16... | collective-permute-start | bytes 884744 | tf_op jit(solution)/shard_map/ppermute | solution.py:305
  58.8 10.4 %collective-permute-start.6 = (bf16[384,384]{1,0:T(8,128)(2,1)}, bf16[384,384]{1,0:T(8,128)(2,1)S(1)}, u32[]{:S(2)}, u32[]{:S(2)}) collective-permute-start(bf16[384,384]{1,0:T(8,128)(2,1)} %get-tuple-element.43), channel_id=1, source_target_pairs={{0,24},{8,1},{9,17},{1,10},{2,26},{10,3},{11,19},{3,8},{24,32},{16... | collective-permute-start | bytes 884744 | tf_op jit(solution)/shard_map/ppermute | solution.py:305
  59.7 9.6 %collective-permute-start.8 = (bf16[384,384]{1,0:T(8,128)(2,1)S(1)}, bf16[384,384]{1,0:T(8,128)(2,1)}, u32[]{:S(2)}, u32[]{:S(2)}) collective-permute-start(bf16[384,384]{1,0:T(8,128)(2,1)S(1)} %get-tuple-element.45), channel_id=1, source_target_pairs={{0,56},{8,3},{9,49},{1,8},{2,58},{10,1},{11,51},{3,10},{24,0},{16,... | collective-permute-start | bytes 884744 | tf_op jit(solution)/shard_map/ppermute | solution.py:305
  62.5 17.3 %all-to-all-start.1 = ((bf16[16,16,768]{2,1,0:T(8,128)(2,1)}), bf16[16,16,768]{2,1,0:T(8,128)(2,1)S(1)}, u32[]{:S(2)}, u32[]{:S(2)}) async-start(bf16[16,16,768]{2,1,0:T(8,128)(2,1)} %get-tuple-element.39), calls=%async_computation.1 | async-start | bytes 786432 | tf_op jit(solution)/shard_map/all_to_all | solution.py:349
  70.9 6.0 %collective-permute-start.9 = (bf16[192,384]{1,0:T(8,128)(2,1)S(1)}, bf16[192,384]{1,0:T(8,128)(2,1)S(1)}, u32[]{:S(2)}, u32[]{:S(2)}) collective-permute-start(bf16[192,384]{1,0:T(8,128)(2,1)S(1)} %get-tuple-element.48), channel_id=1, source_target_pairs={{0,2},{8,40},{9,3},{1,41},{2,0},{10,42},{11,1},{3,43},{24,18},{16,... | collective-permute-start | bytes 442376 | tf_op jit(solution)/shard_map/ppermute | solution.py:305
  72.4 7.4 %collective-permute-start.10 = (bf16[192,384]{1,0:T(8,128)(2,1)S(1)}, bf16[192,384]{1,0:T(8,128)(2,1)S(1)}, u32[]{:S(2)}, u32[]{:S(2)}) collective-permute-start(bf16[192,384]{1,0:T(8,128)(2,1)S(1)} %get-tuple-element.49), channel_id=1, source_target_pairs={{0,1},{8,24},{9,2},{1,25},{2,3},{10,26},{11,0},{3,27},{24,17},{16,... | collective-permute-start | bytes 442376 | tf_op jit(solution)/shard_map/ppermute | solution.py:305
  73.9 5.9 %collective-permute-start.11 = (bf16[192,384]{1,0:T(8,128)(2,1)S(1)}, bf16[192,384]{1,0:T(8,128)(2,1)S(1)}, u32[]{:S(2)}, u32[]{:S(2)}) collective-permute-start(bf16[192,384]{1,0:T(8,128)(2,1)S(1)} %get-tuple-element.50), channel_id=1, source_target_pairs={{0,3},{8,56},{9,0},{1,57},{2,1},{10,58},{11,2},{3,59},{24,19},{16,... | collective-permute-start | bytes 442376 | tf_op jit(solution)/shard_map/ppermute | solution.py:305
  76.2 3.6 %collective-permute-start.12 = (bf16[192,384]{1,0:T(8,128)(2,1)S(1)}, bf16[192,384]{1,0:T(8,128)(2,1)S(1)}, u32[]{:S(2)}, u32[]{:S(2)}) collective-permute-start(bf16[192,384]{1,0:T(8,128)(2,1)S(1)} %get-tuple-element.51), channel_id=1, source_target_pairs={{0,0},{8,8},{9,1},{1,9},{2,2},{10,10},{11,3},{3,11},{24,16},{16,24... | collective-permute-start | bytes 442376 | tf_op jit(solution)/shard_map/ppermute | solution.py:305

commit v6 on v5

--- a/solution.py
+++ b/solution.py
@@ -21,15 +21,13 @@
     return lax.dot_general(a, b, (((1,), (1,)), ((), ())), preferred_element_type=F32)
 
 
-def call(body, outs, ins, scratch=(), smem=(), hbm=(), passed=None, flops=0, nbytes=0, limit=8):
-    passed = passed or {}
-    space = {i: SM for i in smem} | {i: HB for i in (*hbm, *passed)}
+def call(body, outs, ins, scratch=(), smem=(), hbm=(), hbm_outs=(), flops=0, nbytes=0, limit=8):
+    space = {i: SM for i in smem} | {i: HB for i in hbm}
     return pl.pallas_call(
         body,
         out_shape=[jax.ShapeDtypeStruct(s, d) for s, d in outs],
         in_specs=[space.get(i, VM) for i in range(len(ins))],
-        out_specs=[HB if i in passed.values() else VM for i in range(len(outs))],
-        input_output_aliases=passed,
+        out_specs=[HB if i in hbm_outs else VM for i in range(len(outs))],
         scratch_shapes=list(scratch),
         compiler_params=pltpu.CompilerParams(vmem_limit_bytes=limit * 2**20),
         cost_estimate=pl.CostEstimate(flops=flops, bytes_accessed=nbytes, transcendentals=0),
@@ -58,8 +56,9 @@
 def feature_order(n, role, x0, y0):
     f = lanes(n)
     d = third(f)
-    c = (d >> 3) & 1
-    x, y = (((d >> 4) & 3) - x0) & 3, ((d & 3) - y0) & 3
+    x, y = (d >> 4) & 3, d & 3
+    c = ((d >> 3) ^ x ^ y) & 1
+    x, y = (x - x0) & 3, (y - y0) & 3
     first, second = jnp.where(c == 0, x, y), jnp.where(c == 0, y, x)
     low = (d >> 6) * 6 + ((d >> 2) & 1) * 3 + (f - 3 * d)
     return (c ^ role) * (n // 2) + first * (n // 8) + second * (n // 32) + low
@@ -92,15 +91,19 @@
     return (slot << 4) + (k << 3) + row, half
 
 
-def pack_body(x_ref, d_ref, o_ref, x_s, d_s, sems):
+def pack_body(x_ref, d_ref, o_ref, x_s, d_s, p_s, sems):
     copies = [pltpu.make_async_copy(r, s, sems.at[i]) for i, (r, s) in enumerate(((x_ref, x_s), (d_ref, d_s)))]
     for copy in copies:
         copy.start()
     sel = selection(256, home_order())
-    copies[0].wait()
-    o_ref[:, 0:16, :] = nn(sel, x_s[...]).astype(BF).reshape(16, 16, 768)
-    copies[1].wait()
-    o_ref[:, 16:32, :] = nn(sel, d_s[...]).astype(BF).reshape(16, 16, 768)
+    outs = []
+    for i, s in enumerate((x_s, d_s)):
+        copies[i].wait()
+        p_s[i] = nn(sel, s[...]).astype(BF).reshape(16, 16, 768)
+        outs.append(pltpu.make_async_copy(p_s.at[i], o_ref.at[:, i * 16 : i * 16 + 16, :], sems.at[2 + i]))
+        outs[i].start()
+    for copy in outs:
+        copy.wait()
 
 
 def rows_of(ref, first):
@@ -290,7 +293,7 @@
     def swap(v):
         return lax.ppermute(v, "c", [(0, 1), (1, 0)])
 
-    def spread(blocks, axes, steps, home):
+    def spread(blocks, axes, steps):
         moved = []
         for s in steps:
             pairs = []
@@ -298,7 +301,7 @@
                 for y in range(4):
                     for k in range(2):
                         u, v = ((x + s) % 4, y) if axes[k] == "x" else (x, (y + s) % 4)
-                        c, d = k ^ ((x + y) & 1), k if home else k ^ ((u + v) & 1)
+                        c, d = k ^ ((x + y) & 1), k ^ ((u + v) & 1)
                         pairs.append(((x * 2 + c) * 4 + y, (u * 2 + d) * 4 + v))
             each = len(blocks) // 4
             for block in blocks[s * each : s * each + each]:
@@ -310,8 +313,9 @@
         pack_body,
         [((16, 32, 768), BF)],
         [x.reshape(256, 768), d.reshape(256, 768)],
-        scratch=[scr(256, 768), scr(256, 768), pltpu.SemaphoreType.DMA((2,))],
+        scratch=[scr(256, 768), scr(256, 768), scr(2, 16, 16, 768), pltpu.SemaphoreType.DMA((4,))],
         hbm=(0, 1),
+        hbm_outs=(0,),
         limit=60,
     )
     own = lax.all_to_all(packed, ("x1", "x0", "zh0", "zh1"), split_axis=0, concat_axis=0, tiled=True)
@@ -345,10 +349,10 @@
         [mine, got, xd, swap(grads[4]), grads[0]],
         nbytes=3 * 10**6,
     )
-    first = spread([b for pair in zip(grads[:4], others) for b in pair], "xy", (2, 1, 3), False) + [keep, others[0]]
+    first = spread([b for pair in zip(grads[:4], others) for b in pair], "xy", (2, 1, 3)) + [keep, others[0]]
     back = lax.all_to_all(ig, ("x1", "x0", "zh0", "zh1"), split_axis=0, concat_axis=0, tiled=True)
     second = call(split_body, [((192, 384), BF)] * 4, [at, *first], smem=(0,), flops=4_000_000_000)
-    second = spread(second, "yx", (2, 1, 3, 0), True)
+    second = spread(second, "yx", (2, 1, 3)) + [second[0]]
     slots, = call(slot_body, [((8, 16, 768), BF)], [back, *second], hbm=(0,))
     last = lax.all_to_all(slots, ("zl", "zh0", "zh1"), split_axis=0, concat_axis=0, tiled=True)
     grad_qkv, grad_out, ig_home = call(last_body, [((3, 2304), F32), ((3, 768), F32), ((256, 768), BF)], [last, back])

time: 93.2 us -> 93 us (level)
  waiting for transfers between devices: 6.16 us -> 7.8 us
  starting transfers between devices: 22.9 us -> 21.5 us
    ppermute x10 -> x9, waiting for transfers between devices: 6.15 us -> 7.79 us  [spread(): moved.append(lax.ppermute(block, ('x1', 'x0', 'c', 'y'), pairs))]
    ppermute x10 -> x9, starting transfers between devices: 15.4 us -> 13.9 us  [spread(): moved.append(lax.ppermute(block, ('x1', 'x0', 'c', 'y'), pairs))]
  transfers between devices with their start and end apart: 14 -> 13, of which waited for: 4 -> 4; matrix products, arithmetic and copies ran while one was open for 0% -> 0% of each run, Pallas kernels for 7% -> 8%
where the time goes in v6:
time: 93 us; the launch traced here: 91.9 us
  blocking collectives  43.4 us (47%)
  starting transfers between devices  21.5 us (23%)
  Pallas kernels  18.4 us (20%)
  waiting for transfers between devices  7.8 us (8%)
    all_to_all x1, blocking collectives, local(): lax.all_to_all(packed, ('x1', 'x0', 'zh0', 'zh1'), split_axis=0, concat_a...  32.9 us
    pallas_call x7, Pallas kernels, call(): pl.pallas_call(body, out_shape=[jax.ShapeDtypeStruct(s, d) for s, d in ou...  18.4 us
    ppermute x9, starting transfers between devices, spread(): moved.append(lax.ppermute(block, ('x1', 'x0', 'c', 'y'), pairs))  13.9 us
    all_to_all x1, blocking collectives, local(): lax.all_to_all(slots, ('zl', 'zh0', 'zh1'), split_axis=0, concat_axis=0,...  10.5 us
    ppermute x9, waiting for transfers between devices, spread(): moved.append(lax.ppermute(block, ('x1', 'x0', 'c', 'y'), pairs))  7.79 us
    ppermute x3, starting transfers between devices, swap(): return lax.ppermute(v, 'c', [(0, 1), (1, 0)])  4.04 us
    all_to_all x1, starting transfers between devices, local(): lax.all_to_all(ig, ('x1', 'x0', 'zh0', 'zh1'), split_axis=0, concat_axis=...  3.56 us
  transfers between devices with their start and end apart: 13, of which 4 were waited for; matrix products, arithmetic and copies ran while one was open for 0% of the time, Pallas kernels for 8%

profile of v6, /device:TPU:1, one launch (start us, length us, event | category | flops | bytes accessed | tf_op | source)
XLA Modules:
  0.0 91.9 jit_solution(9934538635101070319)
XLA Ops:
  0.6 2.4 %shard_map.67 = bf16[16,32,768]{2,1,0:T(8,128)(2,1)} custom-call(bf16[256,768]{1,0:T(8,128)(2,1)} %bitcast.7, bf16[256,768]{1,0:T(8,128)(2,1)} %bitcast.8), custom_call_target="tpu_custom_call" | custom-call | tf_op jit(solution)/shard_map/pallas_call | solution.py:26
  3.0 0.0 copy-start
  3.0 32.9 %all_to_all.15.own_ref = bf16[16,32,768]{2,1,0:T(8,128)(2,1)S(1)} all-to-all(bf16[16,32,768]{2,1,0:T(8,128)(2,1)} %shard_map.67), channel_id=1, replica_groups=mesh['zh1'=2,'zh0'=2,'x1'=2,'x0'=2,'c'=2,'zl'=2,'y'=4] {'x1','x0','zh0',..., dimensions={0} | all-to-all | bytes 1572864 | tf_op jit(solution)/shard_map/all_to_all | solution.py:321
  35.9 3.5 %collective-permute-start = (bf16[16,32,768]{2,1,0:T(8,128)(2,1)S(1)}, bf16[16,32,768]{2,1,0:T(8,128)(2,1)S(1)}, u32[]{:S(2)}, u32[]{:S(2)}) collective-permute-start(bf16[16,32,768]{2,1,0:T(8,128)(2,1)S(1)} %all_to_all.15.own_ref), channel_id=1, source_target_pairs={{0,8},{8,0},{1,9},{9,1},{2,10},{10,2},{3,11},{11,3},{4,12},{12,4},... | collective-permute-start | bytes 2359304 | tf_op jit(solution)/shard_map/ppermute | solution.py:294
  39.3 0.1 pad_add_fusion.at_ref
  39.4 3.6 %shard_map.68 = (bf16[512,768]{1,0:T(8,128)(2,1)S(1)}, bf16[256,1152]{1,0:T(8,128)(2,1)S(1)}, bf16[256,384]{1,0:T(8,128)(2,1)S(1)}, bf16[768,256]{1,0:T(8,128)(2...) custom-call(s32[4]{0:T(128)S(1)} %pad_add_fusion.at_ref, ...), custom_call_target="tpu_custom_call" | custom-call | flops 1000000000 | bytes 5000000 | tf_op jit(solution)/shard_map/pallas_call | solution.py:26
  43.0 0.0 collective-permute-done.oth_ref
  43.0 7.8 %shard_map.69 = (f32[256,768]{1,0:T(8,128)S(1)}, bf16[256,768]{1,0:T(8,128)(2,1)S(1)}, bf16[384,384]{1,0:T(8,128)(2,1)S(1)}, bf16[384,384]{1,0:T(8,128)(2,1)S(1)...) custom-call(s32[4]{0:T(128)S(1)} %pad_add_fusion.at_ref, ...), custom_call_target="tpu_custom_call" | custom-call | flops 5000000000 | bytes 10000000 | tf_op jit(solution)/shard_map/pallas_call | solution.py:26
  50.8 0.1 collective-permute-start.2
  50.9 0.5 collective-permute-start.1
  51.4 2.8 %collective-permute-start.3 = (bf16[384,384]{1,0:T(8,128)(2,1)S(1)}, bf16[384,384]{1,0:T(8,128)(2,1)S(1)}, u32[]{:S(2)}, u32[]{:S(2)}) collective-permute-start(bf16[384,384]{1,0:T(8,128)(2,1)S(1)} %get-tuple-element.40), channel_id=1, source_target_pairs={{0,32},{8,10},{9,41},{1,3},{2,34},{10,8},{11,43},{3,1},{24,56},{16... | collective-permute-start | bytes 884744 | tf_op jit(solution)/shard_map/ppermute | solution.py:308
  54.2 0.7 collective-permute-start.5
  54.9 2.3 %collective-permute-start.7 = (bf16[384,384]{1,0:T(8,128)(2,1)S(1)}, bf16[384,384]{1,0:T(8,128)(2,1)S(1)}, u32[]{:S(2)}, u32[]{:S(2)}) collective-permute-start(bf16[384,384]{1,0:T(8,128)(2,1)S(1)} %get-tuple-element.44), channel_id=1, source_target_pairs={{0,56},{8,3},{9,49},{1,8},{2,58},{10,1},{11,51},{3,10},{24,0},{16,... | collective-permute-start | bytes 884744 | tf_op jit(solution)/shard_map/ppermute | solution.py:308
  57.2 0.0 collective-permute-done.2.blocks_ref
  57.2 1.6 %shard_map.70 = (bf16[16,16,768]{2,1,0:T(8,128)(2,1)}, bf16[384,384]{1,0:T(8,128)(2,1)S(1)}, bf16[384,384]{1,0:T(8,128)(2,1)S(1)}, bf16[384,384]{1,0:T(8,128)(2,...) custom-call(f32[256,768]{1,0:T(8,128)S(1)} %get-tuple-element.35.part_ref, ...), custom_call_target="tpu_custom_call" | custom-call | bytes 3000000 | tf_op jit(solution)/shard_map/pallas_call | solution.py:26
  58.8 0.9 collective-permute-start.6
  59.7 2.7 %collective-permute-start.8 = (bf16[384,384]{1,0:T(8,128)(2,1)}, bf16[384,384]{1,0:T(8,128)(2,1)}, u32[]{:S(2)}, u32[]{:S(2)}) collective-permute-start(bf16[384,384]{1,0:T(8,128)(2,1)} %get-tuple-element.45), channel_id=1, source_target_pairs={{0,56},{8,3},{9,49},{1,8},{2,58},{10,1},{11,51},{3,10},{24,0},{16,... | collective-permute-start | bytes 884744 | tf_op jit(solution)/shard_map/ppermute | solution.py:308
  62.4 3.6 %all-to-all-start.1 = ((bf16[16,16,768]{2,1,0:T(8,128)(2,1)}), bf16[16,16,768]{2,1,0:T(8,128)(2,1)S(1)}, u32[]{:S(2)}, u32[]{:S(2)}) async-start(bf16[16,16,768]{2,1,0:T(8,128)(2,1)} %get-tuple-element.39), calls=%async_computation.1 | async-start | bytes 786432 | tf_op jit(solution)/shard_map/all_to_all | solution.py:353
  65.9 0.0 collective-permute-done.5.refs_2_
  66.0 0.2 collective-permute-done.4.refs_1_
  66.2 3.2 %collective-permute-done.6.refs_3_ = bf16[384,384]{1,0:T(8,128)(2,1)} collective-permute-done((bf16[384,384]{1,0:T(8,128)(2,1)}, bf16[384,384]{1,0:T(8,128)(2,1)}, u32[]{:S(2)}, u32[]{:S(2)}) %collective-permute-start.6) | collective-permute-done | bytes 294944 | tf_op jit(solution)/shard_map/ppermute | solution.py:308
  69.3 0.0 collective-permute-done.8.refs_5_
  69.3 1.7 %shard_map.71 = (bf16[192,384]{1,0:T(8,128)(2,1)S(1)}, bf16[192,384]{1,0:T(8,128)(2,1)S(1)}, bf16[192,384]{1,0:T(8,128)(2,1)S(1)}, bf16[192,384]{1,0:T(8,128)(2,1)S(1)}) custom-call(s32[4]{0:T(128)S(1)} %pad_add_fusion.at_ref, bf16[384,384]{1,0:T(8,128)(2,1)S(1)} %collective-permute-done.3.refs_0_, bf16[384,384]{1,0:T(8,128)(2,1)S(1)} %collective-permute-done.4.refs_1_, ...), custom_call_target="tpu_custom_call" | custom-call | flops 4000000000 | tf_op jit(solution)/shard_map/pallas_call | solution.py:26
  71.1 1.6 %collective-permute-start.9 = (bf16[192,384]{1,0:T(8,128)(2,1)S(1)}, bf16[192,384]{1,0:T(8,128)(2,1)S(1)}, u32[]{:S(2)}, u32[]{:S(2)}) collective-permute-start(bf16[192,384]{1,0:T(8,128)(2,1)S(1)} %get-tuple-element.48), channel_id=1, source_target_pairs={{0,2},{8,40},{9,11},{1,33},{2,0},{10,42},{11,9},{3,35},{24,26},{16... | collective-permute-start | bytes 442376 | tf_op jit(solution)/shard_map/ppermute | solution.py:308
  72.7 1.0 %collective-permute-start.10 = (bf16[192,384]{1,0:T(8,128)(2,1)S(1)}, bf16[192,384]{1,0:T(8,128)(2,1)S(1)}, u32[]{:S(2)}, u32[]{:S(2)}) collective-permute-start(bf16[192,384]{1,0:T(8,128)(2,1)S(1)} %get-tuple-element.49), channel_id=1, source_target_pairs={{0,9},{8,16},{9,2},{1,25},{2,11},{10,18},{11,0},{3,27},{24,17},{16... | collective-permute-start | bytes 442376 | tf_op jit(solution)/shard_map/ppermute | solution.py:308
  73.7 2.0 %collective-permute-start.11 = (bf16[192,384]{1,0:T(8,128)(2,1)S(1)}, bf16[192,384]{1,0:T(8,128)(2,1)S(1)}, u32[]{:S(2)}, u32[]{:S(2)}) collective-permute-start(bf16[192,384]{1,0:T(8,128)(2,1)S(1)} %get-tuple-element.50), channel_id=1, source_target_pairs={{0,11},{8,48},{9,0},{1,57},{2,9},{10,50},{11,2},{3,59},{24,19},{16... | collective-permute-start | bytes 442376 | tf_op jit(solution)/shard_map/ppermute | solution.py:308
  75.6 1.5 %collective-permute-done.9.refs_0_ = bf16[192,384]{1,0:T(8,128)(2,1)S(1)} collective-permute-done((bf16[192,384]{1,0:T(8,128)(2,1)S(1)}, bf16[192,384]{1,0:T(8,128)(2,1)S(1)}, u32[]{:S(2)}, u32[]{:S(2)}) %collective-permute-start.9) | collective-permute-done | bytes 147488 | tf_op jit(solution)/shard_map/ppermute | solution.py:308
  77.1 2.9 %collective-permute-done.10.refs_1_ = bf16[192,384]{1,0:T(8,128)(2,1)S(1)} collective-permute-done((bf16[192,384]{1,0:T(8,128)(2,1)S(1)}, bf16[192,384]{1,0:T(8,128)(2,1)S(1)}, u32[]{:S(2)}, u32[]{:S(2)}) %collective-permute-start.10) | collective-permute-done | bytes 147488 | tf_op jit(solution)/shard_map/ppermute | solution.py:308
  80.0 0.0 collective-permute-done.11.refs_2_
  80.0 0.3 shard_map.72
  80.3 10.5 %all_to_all.16.r_ref = bf16[8,16,768]{2,1,0:T(8,128)(2,1)S(1)} all-to-all(bf16[8,16,768]{2,1,0:T(8,128)(2,1)S(1)} %shard_map.72), channel_id=1, replica_groups=mesh['zh1'=2,'zh0'=2,'x1'=2,'x0'=2,'c'=2,'zl'=2,'y'=4] {'zl','zh0','zh1'}, dimensions={0} | all-to-all | bytes 393216 | tf_op jit(solution)/shard_map/all_to_all | solution.py:357
  90.9 1.1 %shard_map.73 = (f32[3,2304]{1,0:T(4,128)}, f32[3,768]{1,0:T(4,128)}, bf16[256,768]{1,0:T(8,128)(2,1)}) custom-call(bf16[8,16,768]{2,1,0:T(8,128)(2,1)S(1)} %all_to_all.16.r_ref, bf16[16,16,768]{2,1,0:T(8,128)(2,1)S(1)} %all-to-all-done.1.back_ref.ig_ref), custom_call_target="tpu_custom_call" | custom-call | tf_op jit(solution)/shard_map/pallas_call | solution.py:26
  (6 shorter events, 0.0 us)
Async XLA Ops:
  3.0 36.4 %copy-start = (bf16[768,768]{1,0:T(8,128)(2,1)S(1)}, bf16[768,768]{1,0:T(8,128)(2,1)}, u32[]{:S(2)}) copy-start(bf16[768,768]{1,0:T(8,128)(2,1)} %wout_ref.1) | copy-start | bytes 3538948
  35.9 7.2 %collective-permute-start = (bf16[16,32,768]{2,1,0:T(8,128)(2,1)S(1)}, bf16[16,32,768]{2,1,0:T(8,128)(2,1)S(1)}, u32[]{:S(2)}, u32[]{:S(2)}) collective-permute-start(bf16[16,32,768]{2,1,0:T(8,128)(2,1)S(1)} %all_to_all.15.own_ref), channel_id=1, source_target_pairs={{0,8},{8,0},{1,9},{9,1},{2,10},{10,2},{3,11},{11,3},{4,12},{12,4},... | collective-permute-start | bytes 2359304 | tf_op jit(solution)/shard_map/ppermute | solution.py:294
  50.8 6.4 %collective-permute-start.2 = (bf16[1536,384]{1,0:T(8,128)(2,1)S(1)}, bf16[1536,384]{1,0:T(8,128)(2,1)S(1)}, u32[]{:S(2)}, u32[]{:S(2)}) collective-permute-start(bf16[1536,384]{1,0:T(8,128)(2,1)S(1)} %get-tuple-element.37), channel_id=1, source_target_pairs={{0,8},{8,0},{1,9},{9,1},{2,10},{10,2},{3,11},{11,3},{4,12},{12,4},... | collective-permute-start | bytes 3538952 | tf_op jit(solution)/shard_map/ppermute | solution.py:294
  50.9 6.3 %collective-permute-start.1 = (bf16[256,768]{1,0:T(8,128)(2,1)S(1)}, bf16[256,768]{1,0:T(8,128)(2,1)S(1)}, u32[]{:S(2)}, u32[]{:S(2)}) collective-permute-start(bf16[256,768]{1,0:T(8,128)(2,1)S(1)} %get-tuple-element.36), channel_id=1, source_target_pairs={{0,8},{8,0},{1,9},{9,1},{2,10},{10,2},{3,11},{11,3},{4,12},{12,4},... | collective-permute-start | bytes 1179656 | tf_op jit(solution)/shard_map/ppermute | solution.py:294
  51.4 8.2 %collective-permute-start.3 = (bf16[384,384]{1,0:T(8,128)(2,1)S(1)}, bf16[384,384]{1,0:T(8,128)(2,1)S(1)}, u32[]{:S(2)}, u32[]{:S(2)}) collective-permute-start(bf16[384,384]{1,0:T(8,128)(2,1)S(1)} %get-tuple-element.40), channel_id=1, source_target_pairs={{0,32},{8,10},{9,41},{1,3},{2,34},{10,8},{11,43},{3,1},{24,56},{16... | collective-permute-start | bytes 884744 | tf_op jit(solution)/shard_map/ppermute | solution.py:308
  54.2 11.7 %collective-permute-start.5 = (bf16[384,384]{1,0:T(8,128)(2,1)S(1)}, bf16[384,384]{1,0:T(8,128)(2,1)S(1)}, u32[]{:S(2)}, u32[]{:S(2)}) collective-permute-start(bf16[384,384]{1,0:T(8,128)(2,1)S(1)} %get-tuple-element.42), channel_id=1, source_target_pairs={{0,24},{8,1},{9,17},{1,10},{2,26},{10,3},{11,19},{3,8},{24,32},{16... | collective-permute-start | bytes 884744 | tf_op jit(solution)/shard_map/ppermute | solution.py:308
  54.9 11.0 %collective-permute-start.7 = (bf16[384,384]{1,0:T(8,128)(2,1)S(1)}, bf16[384,384]{1,0:T(8,128)(2,1)S(1)}, u32[]{:S(2)}, u32[]{:S(2)}) collective-permute-start(bf16[384,384]{1,0:T(8,128)(2,1)S(1)} %get-tuple-element.44), channel_id=1, source_target_pairs={{0,56},{8,3},{9,49},{1,8},{2,58},{10,1},{11,51},{3,10},{24,0},{16,... | collective-permute-start | bytes 884744 | tf_op jit(solution)/shard_map/ppermute | solution.py:308
  58.8 7.4 %collective-permute-start.4 = (bf16[384,384]{1,0:T(8,128)(2,1)}, bf16[384,384]{1,0:T(8,128)(2,1)S(1)}, u32[]{:S(2)}, u32[]{:S(2)}) collective-permute-start(bf16[384,384]{1,0:T(8,128)(2,1)} %get-tuple-element.41), channel_id=1, source_target_pairs={{0,32},{8,10},{9,41},{1,3},{2,34},{10,8},{11,43},{3,1},{24,56},{16... | collective-permute-start | bytes 884744 | tf_op jit(solution)/shard_map/ppermute | solution.py:308
  58.8 10.6 %collective-permute-start.6 = (bf16[384,384]{1,0:T(8,128)(2,1)}, bf16[384,384]{1,0:T(8,128)(2,1)}, u32[]{:S(2)}, u32[]{:S(2)}) collective-permute-start(bf16[384,384]{1,0:T(8,128)(2,1)} %get-tuple-element.43), channel_id=1, source_target_pairs={{0,24},{8,1},{9,17},{1,10},{2,26},{10,3},{11,19},{3,8},{24,32},{16... | collective-permute-start | bytes 884744 | tf_op jit(solution)/shard_map/ppermute | solution.py:308
  59.7 9.7 %collective-permute-start.8 = (bf16[384,384]{1,0:T(8,128)(2,1)}, bf16[384,384]{1,0:T(8,128)(2,1)}, u32[]{:S(2)}, u32[]{:S(2)}) collective-permute-start(bf16[384,384]{1,0:T(8,128)(2,1)} %get-tuple-element.45), channel_id=1, source_target_pairs={{0,56},{8,3},{9,49},{1,8},{2,58},{10,1},{11,51},{3,10},{24,0},{16,... | collective-permute-start | bytes 884744 | tf_op jit(solution)/shard_map/ppermute | solution.py:308
  62.4 17.7 %all-to-all-start.1 = ((bf16[16,16,768]{2,1,0:T(8,128)(2,1)}), bf16[16,16,768]{2,1,0:T(8,128)(2,1)S(1)}, u32[]{:S(2)}, u32[]{:S(2)}) async-start(bf16[16,16,768]{2,1,0:T(8,128)(2,1)} %get-tuple-element.39), calls=%async_computation.1 | async-start | bytes 786432 | tf_op jit(solution)/shard_map/all_to_all | solution.py:353
  71.1 6.0 %collective-permute-start.9 = (bf16[192,384]{1,0:T(8,128)(2,1)S(1)}, bf16[192,384]{1,0:T(8,128)(2,1)S(1)}, u32[]{:S(2)}, u32[]{:S(2)}) collective-permute-start(bf16[192,384]{1,0:T(8,128)(2,1)S(1)} %get-tuple-element.48), channel_id=1, source_target_pairs={{0,2},{8,40},{9,11},{1,33},{2,0},{10,42},{11,9},{3,35},{24,26},{16... | collective-permute-start | bytes 442376 | tf_op jit(solution)/shard_map/ppermute | solution.py:308
  72.7 7.4 %collective-permute-start.10 = (bf16[192,384]{1,0:T(8,128)(2,1)S(1)}, bf16[192,384]{1,0:T(8,128)(2,1)S(1)}, u32[]{:S(2)}, u32[]{:S(2)}) collective-permute-start(bf16[192,384]{1,0:T(8,128)(2,1)S(1)} %get-tuple-element.49), channel_id=1, source_target_pairs={{0,9},{8,16},{9,2},{1,25},{2,11},{10,18},{11,0},{3,27},{24,17},{16... | collective-permute-start | bytes 442376 | tf_op jit(solution)/shard_map/ppermute | solution.py:308
  73.7 6.4 %collective-permute-start.11 = (bf16[192,384]{1,0:T(8,128)(2,1)S(1)}, bf16[192,384]{1,0:T(8,128)(2,1)S(1)}, u32[]{:S(2)}, u32[]{:S(2)}) collective-permute-start(bf16[192,384]{1,0:T(8,128)(2,1)S(1)} %get-tuple-element.50), channel_id=1, source_target_pairs={{0,11},{8,48},{9,0},{1,57},{2,9},{10,50},{11,2},{3,59},{24,19},{16... | collective-permute-start | bytes 442376 | tf_op jit(solution)/shard_map/ppermute | solution.py:308

commit v7 on v6

--- a/solution.py
+++ b/solution.py
@@ -265,12 +265,14 @@
         refs[4][:, :, h * 384 : (h + 1) * 384] = part.reshape(8, 16, 384)
 
 
-def last_body(r_ref, ig_ref, gq_ref, go_ref, home_ref):
+def last_body(r_ref, ig_ref, gq_ref, go_ref, home_ref, home_s, sem):
     sel = selection(256, home_order())
     back = lax.dot_general(
         sel, ig_ref[...].reshape(256, 768), (((0,), (0,)), ((), ())), preferred_element_type=F32
     )
-    home_ref[...] = back.astype(BF)
+    home_s[...] = back.astype(BF)
+    copy = pltpu.make_async_copy(home_s, home_ref, sem.at[0])
+    copy.start()
     total = r_ref[0].astype(F32)
     for z in range(1, 8):
         total = total + r_ref[z].astype(F32)
@@ -283,6 +285,7 @@
         gq_ref[1:2, 1536 + at : 1536 + at + 384] = m[3:4, 384:768]
         gq_ref[2:3, 1536 + at : 1536 + at + 384] = m[4:5, 0:384]
     go_ref[...] = halves[0][5:8] + halves[1][5:8]
+    copy.wait()
 
 
 def local(x, d, w_qkv, w_out):
@@ -355,7 +358,13 @@
     second = spread(second, "yx", (2, 1, 3)) + [second[0]]
     slots, = call(slot_body, [((8, 16, 768), BF)], [back, *second], hbm=(0,))
     last = lax.all_to_all(slots, ("zl", "zh0", "zh1"), split_axis=0, concat_axis=0, tiled=True)
-    grad_qkv, grad_out, ig_home = call(last_body, [((3, 2304), F32), ((3, 768), F32), ((256, 768), BF)], [last, back])
+    grad_qkv, grad_out, ig_home = call(
+        last_body,
+        [((3, 2304), F32), ((3, 768), F32), ((256, 768), BF)],
+        [last, back],
+        scratch=[scr(256, 768), pltpu.SemaphoreType.DMA((1,))],
+        hbm_outs=(2,),
+    )
     return ig_home.reshape(8, 32, 768), grad_qkv, grad_out
 
 

time: 93 us -> 93.8 us (level)
  transfers between devices with their start and end apart: 13 -> 13, of which waited for: 4 -> 4; matrix products, arithmetic and copies ran while one was open for 0% -> 0% of each run, Pallas kernels for 8% -> 7%
where the time goes in v7:
time: 93.8 us; the launch traced here: 92.7 us
  blocking collectives  43.4 us (46%)
  starting transfers between devices  21.5 us (23%)
  Pallas kernels  19.1 us (20%)
  waiting for transfers between devices  7.8 us (8%)
    all_to_all x1, blocking collectives, local(): lax.all_to_all(packed, ('x1', 'x0', 'zh0', 'zh1'), split_axis=0, concat_a...  32.9 us
    pallas_call x7, Pallas kernels, call(): pl.pallas_call(body, out_shape=[jax.ShapeDtypeStruct(s, d) for s, d in ou...  19.1 us
    ppermute x9, starting transfers between devices, spread(): moved.append(lax.ppermute(block, ('x1', 'x0', 'c', 'y'), pairs))  13.9 us
    all_to_all x1, blocking collectives, local(): lax.all_to_all(slots, ('zl', 'zh0', 'zh1'), split_axis=0, concat_axis=0,...  10.5 us
    ppermute x9, waiting for transfers between devices, spread(): moved.append(lax.ppermute(block, ('x1', 'x0', 'c', 'y'), pairs))  7.79 us
    ppermute x3, starting transfers between devices, swap(): return lax.ppermute(v, 'c', [(0, 1), (1, 0)])  4.04 us
    all_to_all x1, starting transfers between devices, local(): lax.all_to_all(ig, ('x1', 'x0', 'zh0', 'zh1'), split_axis=0, concat_axis=...  3.56 us
  transfers between devices with their start and end apart: 13, of which 4 were waited for; matrix products, arithmetic and copies ran while one was open for 0% of the time, Pallas kernels for 7%

profile of v7, /device:TPU:1, one launch (start us, length us, event | category | flops | bytes accessed | tf_op | source)
XLA Modules:
  0.0 92.7 jit_solution(6829755089300903545)
XLA Ops:
  0.6 2.4 %shard_map.67 = bf16[16,32,768]{2,1,0:T(8,128)(2,1)} custom-call(bf16[256,768]{1,0:T(8,128)(2,1)} %bitcast.7, bf16[256,768]{1,0:T(8,128)(2,1)} %bitcast.8), custom_call_target="tpu_custom_call" | custom-call | tf_op jit(solution)/shard_map/pallas_call | solution.py:26
  3.0 0.0 copy-start
  3.0 32.9 %all_to_all.15.own_ref = bf16[16,32,768]{2,1,0:T(8,128)(2,1)S(1)} all-to-all(bf16[16,32,768]{2,1,0:T(8,128)(2,1)} %shard_map.67), channel_id=1, replica_groups=mesh['zh1'=2,'zh0'=2,'x1'=2,'x0'=2,'c'=2,'zl'=2,'y'=4] {'x1','x0','zh0',..., dimensions={0} | all-to-all | bytes 1572864 | tf_op jit(solution)/shard_map/all_to_all | solution.py:324
  35.9 3.5 %collective-permute-start = (bf16[16,32,768]{2,1,0:T(8,128)(2,1)S(1)}, bf16[16,32,768]{2,1,0:T(8,128)(2,1)S(1)}, u32[]{:S(2)}, u32[]{:S(2)}) collective-permute-start(bf16[16,32,768]{2,1,0:T(8,128)(2,1)S(1)} %all_to_all.15.own_ref), channel_id=1, source_target_pairs={{0,8},{8,0},{1,9},{9,1},{2,10},{10,2},{3,11},{11,3},{4,12},{12,4},... | collective-permute-start | bytes 2359304 | tf_op jit(solution)/shard_map/ppermute | solution.py:297
  39.3 0.1 pad_add_fusion.at_ref
  39.4 3.6 %shard_map.68 = (bf16[512,768]{1,0:T(8,128)(2,1)S(1)}, bf16[256,1152]{1,0:T(8,128)(2,1)S(1)}, bf16[256,384]{1,0:T(8,128)(2,1)S(1)}, bf16[768,256]{1,0:T(8,128)(2...) custom-call(s32[4]{0:T(128)S(1)} %pad_add_fusion.at_ref, ...), custom_call_target="tpu_custom_call" | custom-call | flops 1000000000 | bytes 5000000 | tf_op jit(solution)/shard_map/pallas_call | solution.py:26
  43.0 7.8 %shard_map.69 = (f32[256,768]{1,0:T(8,128)S(1)}, bf16[256,768]{1,0:T(8,128)(2,1)S(1)}, bf16[384,384]{1,0:T(8,128)(2,1)S(1)}, bf16[384,384]{1,0:T(8,128)(2,1)S(1)...) custom-call(s32[4]{0:T(128)S(1)} %pad_add_fusion.at_ref, ...), custom_call_target="tpu_custom_call" | custom-call | flops 5000000000 | bytes 10000000 | tf_op jit(solution)/shard_map/pallas_call | solution.py:26
  50.8 0.1 collective-permute-start.2
  50.9 0.5 collective-permute-start.1
  51.4 2.8 %collective-permute-start.3 = (bf16[384,384]{1,0:T(8,128)(2,1)S(1)}, bf16[384,384]{1,0:T(8,128)(2,1)S(1)}, u32[]{:S(2)}, u32[]{:S(2)}) collective-permute-start(bf16[384,384]{1,0:T(8,128)(2,1)S(1)} %get-tuple-element.40), channel_id=1, source_target_pairs={{0,32},{8,10},{9,41},{1,3},{2,34},{10,8},{11,43},{3,1},{24,56},{16... | collective-permute-start | bytes 884744 | tf_op jit(solution)/shard_map/ppermute | solution.py:311
  54.2 0.7 collective-permute-start.5
  54.9 2.3 %collective-permute-start.7 = (bf16[384,384]{1,0:T(8,128)(2,1)S(1)}, bf16[384,384]{1,0:T(8,128)(2,1)S(1)}, u32[]{:S(2)}, u32[]{:S(2)}) collective-permute-start(bf16[384,384]{1,0:T(8,128)(2,1)S(1)} %get-tuple-element.44), channel_id=1, source_target_pairs={{0,56},{8,3},{9,49},{1,8},{2,58},{10,1},{11,51},{3,10},{24,0},{16,... | collective-permute-start | bytes 884744 | tf_op jit(solution)/shard_map/ppermute | solution.py:311
  57.2 0.0 collective-permute-done.1.got_ref
  57.2 1.6 %shard_map.70 = (bf16[16,16,768]{2,1,0:T(8,128)(2,1)}, bf16[384,384]{1,0:T(8,128)(2,1)S(1)}, bf16[384,384]{1,0:T(8,128)(2,1)S(1)}, bf16[384,384]{1,0:T(8,128)(2,...) custom-call(f32[256,768]{1,0:T(8,128)S(1)} %get-tuple-element.35.part_ref, ...), custom_call_target="tpu_custom_call" | custom-call | bytes 3000000 | tf_op jit(solution)/shard_map/pallas_call | solution.py:26
  58.8 0.0 collective-permute-start.4
  58.8 0.9 collective-permute-start.6
  59.6 0.0 collective-permute-done.3.refs_0_
  59.7 2.7 %collective-permute-start.8 = (bf16[384,384]{1,0:T(8,128)(2,1)}, bf16[384,384]{1,0:T(8,128)(2,1)}, u32[]{:S(2)}, u32[]{:S(2)}) collective-permute-start(bf16[384,384]{1,0:T(8,128)(2,1)} %get-tuple-element.45), channel_id=1, source_target_pairs={{0,56},{8,3},{9,49},{1,8},{2,58},{10,1},{11,51},{3,10},{24,0},{16,... | collective-permute-start | bytes 884744 | tf_op jit(solution)/shard_map/ppermute | solution.py:311
  62.4 3.6 %all-to-all-start.1 = ((bf16[16,16,768]{2,1,0:T(8,128)(2,1)}), bf16[16,16,768]{2,1,0:T(8,128)(2,1)S(1)}, u32[]{:S(2)}, u32[]{:S(2)}) async-start(bf16[16,16,768]{2,1,0:T(8,128)(2,1)} %get-tuple-element.39), calls=%async_computation.1 | async-start | bytes 786432 | tf_op jit(solution)/shard_map/all_to_all | solution.py:356
  65.9 0.0 collective-permute-done.7.refs_4_
  66.0 0.2 collective-permute-done.4.refs_1_
  66.2 3.2 %collective-permute-done.6.refs_3_ = bf16[384,384]{1,0:T(8,128)(2,1)} collective-permute-done((bf16[384,384]{1,0:T(8,128)(2,1)}, bf16[384,384]{1,0:T(8,128)(2,1)}, u32[]{:S(2)}, u32[]{:S(2)}) %collective-permute-start.6) | collective-permute-done | bytes 294944 | tf_op jit(solution)/shard_map/ppermute | solution.py:311
  69.3 1.7 %shard_map.71 = (bf16[192,384]{1,0:T(8,128)(2,1)S(1)}, bf16[192,384]{1,0:T(8,128)(2,1)S(1)}, bf16[192,384]{1,0:T(8,128)(2,1)S(1)}, bf16[192,384]{1,0:T(8,128)(2,1)S(1)}) custom-call(s32[4]{0:T(128)S(1)} %pad_add_fusion.at_ref, bf16[384,384]{1,0:T(8,128)(2,1)S(1)} %collective-permute-done.3.refs_0_, bf16[384,384]{1,0:T(8,128)(2,1)S(1)} %collective-permute-done.4.refs_1_, ...), custom_call_target="tpu_custom_call" | custom-call | flops 4000000000 | tf_op jit(solution)/shard_map/pallas_call | solution.py:26
  71.1 1.6 %collective-permute-start.9 = (bf16[192,384]{1,0:T(8,128)(2,1)S(1)}, bf16[192,384]{1,0:T(8,128)(2,1)S(1)}, u32[]{:S(2)}, u32[]{:S(2)}) collective-permute-start(bf16[192,384]{1,0:T(8,128)(2,1)S(1)} %get-tuple-element.48), channel_id=1, source_target_pairs={{0,2},{8,40},{9,11},{1,33},{2,0},{10,42},{11,9},{3,35},{24,26},{16... | collective-permute-start | bytes 442376 | tf_op jit(solution)/shard_map/ppermute | solution.py:311
  72.7 1.0 %collective-permute-start.10 = (bf16[192,384]{1,0:T(8,128)(2,1)S(1)}, bf16[192,384]{1,0:T(8,128)(2,1)S(1)}, u32[]{:S(2)}, u32[]{:S(2)}) collective-permute-start(bf16[192,384]{1,0:T(8,128)(2,1)S(1)} %get-tuple-element.49), channel_id=1, source_target_pairs={{0,9},{8,16},{9,2},{1,25},{2,11},{10,18},{11,0},{3,27},{24,17},{16... | collective-permute-start | bytes 442376 | tf_op jit(solution)/shard_map/ppermute | solution.py:311
  73.7 2.0 %collective-permute-start.11 = (bf16[192,384]{1,0:T(8,128)(2,1)S(1)}, bf16[192,384]{1,0:T(8,128)(2,1)S(1)}, u32[]{:S(2)}, u32[]{:S(2)}) collective-permute-start(bf16[192,384]{1,0:T(8,128)(2,1)S(1)} %get-tuple-element.50), channel_id=1, source_target_pairs={{0,11},{8,48},{9,0},{1,57},{2,9},{10,50},{11,2},{3,59},{24,19},{16... | collective-permute-start | bytes 442376 | tf_op jit(solution)/shard_map/ppermute | solution.py:311
  75.6 1.5 %collective-permute-done.9.refs_0_ = bf16[192,384]{1,0:T(8,128)(2,1)S(1)} collective-permute-done((bf16[192,384]{1,0:T(8,128)(2,1)S(1)}, bf16[192,384]{1,0:T(8,128)(2,1)S(1)}, u32[]{:S(2)}, u32[]{:S(2)}) %collective-permute-start.9) | collective-permute-done | bytes 147488 | tf_op jit(solution)/shard_map/ppermute | solution.py:311
  77.1 2.9 %collective-permute-done.10.refs_1_ = bf16[192,384]{1,0:T(8,128)(2,1)S(1)} collective-permute-done((bf16[192,384]{1,0:T(8,128)(2,1)S(1)}, bf16[192,384]{1,0:T(8,128)(2,1)S(1)}, u32[]{:S(2)}, u32[]{:S(2)}) %collective-permute-start.10) | collective-permute-done | bytes 147488 | tf_op jit(solution)/shard_map/ppermute | solution.py:311
  80.0 0.0 collective-permute-done.11.refs_2_
  80.0 0.3 shard_map.72
  80.3 10.5 %all_to_all.16.r_ref = bf16[8,16,768]{2,1,0:T(8,128)(2,1)S(1)} all-to-all(bf16[8,16,768]{2,1,0:T(8,128)(2,1)S(1)} %shard_map.72), channel_id=1, replica_groups=mesh['zh1'=2,'zh0'=2,'x1'=2,'x0'=2,'c'=2,'zl'=2,'y'=4] {'zl','zh0','zh1'}, dimensions={0} | all-to-all | bytes 393216 | tf_op jit(solution)/shard_map/all_to_all | solution.py:360
  90.9 1.7 %shard_map.73 = (f32[3,2304]{1,0:T(4,128)}, f32[3,768]{1,0:T(4,128)}, bf16[256,768]{1,0:T(8,128)(2,1)}) custom-call(bf16[8,16,768]{2,1,0:T(8,128)(2,1)S(1)} %all_to_all.16.r_ref, bf16[16,16,768]{2,1,0:T(8,128)(2,1)S(1)} %all-to-all-done.1.back_ref.ig_ref), custom_call_target="tpu_custom_call" | custom-call | tf_op jit(solution)/shard_map/pallas_call | solution.py:26
  (6 shorter events, 0.0 us)
Async XLA Ops:
  3.0 36.4 %copy-start = (bf16[768,768]{1,0:T(8,128)(2,1)S(1)}, bf16[768,768]{1,0:T(8,128)(2,1)}, u32[]{:S(2)}) copy-start(bf16[768,768]{1,0:T(8,128)(2,1)} %wout_ref.1) | copy-start | bytes 3538948
  35.9 7.2 %collective-permute-start = (bf16[16,32,768]{2,1,0:T(8,128)(2,1)S(1)}, bf16[16,32,768]{2,1,0:T(8,128)(2,1)S(1)}, u32[]{:S(2)}, u32[]{:S(2)}) collective-permute-start(bf16[16,32,768]{2,1,0:T(8,128)(2,1)S(1)} %all_to_all.15.own_ref), channel_id=1, source_target_pairs={{0,8},{8,0},{1,9},{9,1},{2,10},{10,2},{3,11},{11,3},{4,12},{12,4},... | collective-permute-start | bytes 2359304 | tf_op jit(solution)/shard_map/ppermute | solution.py:297
  50.8 6.4 %collective-permute-start.2 = (bf16[1536,384]{1,0:T(8,128)(2,1)S(1)}, bf16[1536,384]{1,0:T(8,128)(2,1)S(1)}, u32[]{:S(2)}, u32[]{:S(2)}) collective-permute-start(bf16[1536,384]{1,0:T(8,128)(2,1)S(1)} %get-tuple-element.37), channel_id=1, source_target_pairs={{0,8},{8,0},{1,9},{9,1},{2,10},{10,2},{3,11},{11,3},{4,12},{12,4},... | collective-permute-start | bytes 3538952 | tf_op jit(solution)/shard_map/ppermute | solution.py:297
  50.9 6.3 %collective-permute-start.1 = (bf16[256,768]{1,0:T(8,128)(2,1)S(1)}, bf16[256,768]{1,0:T(8,128)(2,1)S(1)}, u32[]{:S(2)}, u32[]{:S(2)}) collective-permute-start(bf16[256,768]{1,0:T(8,128)(2,1)S(1)} %get-tuple-element.36), channel_id=1, source_target_pairs={{0,8},{8,0},{1,9},{9,1},{2,10},{10,2},{3,11},{11,3},{4,12},{12,4},... | collective-permute-start | bytes 1179656 | tf_op jit(solution)/shard_map/ppermute | solution.py:297
  51.4 8.2 %collective-permute-start.3 = (bf16[384,384]{1,0:T(8,128)(2,1)S(1)}, bf16[384,384]{1,0:T(8,128)(2,1)S(1)}, u32[]{:S(2)}, u32[]{:S(2)}) collective-permute-start(bf16[384,384]{1,0:T(8,128)(2,1)S(1)} %get-tuple-element.40), channel_id=1, source_target_pairs={{0,32},{8,10},{9,41},{1,3},{2,34},{10,8},{11,43},{3,1},{24,56},{16... | collective-permute-start | bytes 884744 | tf_op jit(solution)/shard_map/ppermute | solution.py:311
  54.2 11.7 %collective-permute-start.5 = (bf16[384,384]{1,0:T(8,128)(2,1)S(1)}, bf16[384,384]{1,0:T(8,128)(2,1)S(1)}, u32[]{:S(2)}, u32[]{:S(2)}) collective-permute-start(bf16[384,384]{1,0:T(8,128)(2,1)S(1)} %get-tuple-element.42), channel_id=1, source_target_pairs={{0,24},{8,1},{9,17},{1,10},{2,26},{10,3},{11,19},{3,8},{24,32},{16... | collective-permute-start | bytes 884744 | tf_op jit(solution)/shard_map/ppermute | solution.py:311
  54.9 11.0 %collective-permute-start.7 = (bf16[384,384]{1,0:T(8,128)(2,1)S(1)}, bf16[384,384]{1,0:T(8,128)(2,1)S(1)}, u32[]{:S(2)}, u32[]{:S(2)}) collective-permute-start(bf16[384,384]{1,0:T(8,128)(2,1)S(1)} %get-tuple-element.44), channel_id=1, source_target_pairs={{0,56},{8,3},{9,49},{1,8},{2,58},{10,1},{11,51},{3,10},{24,0},{16,... | collective-permute-start | bytes 884744 | tf_op jit(solution)/shard_map/ppermute | solution.py:311
  58.8 7.4 %collective-permute-start.4 = (bf16[384,384]{1,0:T(8,128)(2,1)}, bf16[384,384]{1,0:T(8,128)(2,1)S(1)}, u32[]{:S(2)}, u32[]{:S(2)}) collective-permute-start(bf16[384,384]{1,0:T(8,128)(2,1)} %get-tuple-element.41), channel_id=1, source_target_pairs={{0,32},{8,10},{9,41},{1,3},{2,34},{10,8},{11,43},{3,1},{24,56},{16... | collective-permute-start | bytes 884744 | tf_op jit(solution)/shard_map/ppermute | solution.py:311
  58.8 10.6 %collective-permute-start.6 = (bf16[384,384]{1,0:T(8,128)(2,1)}, bf16[384,384]{1,0:T(8,128)(2,1)}, u32[]{:S(2)}, u32[]{:S(2)}) collective-permute-start(bf16[384,384]{1,0:T(8,128)(2,1)} %get-tuple-element.43), channel_id=1, source_target_pairs={{0,24},{8,1},{9,17},{1,10},{2,26},{10,3},{11,19},{3,8},{24,32},{16... | collective-permute-start | bytes 884744 | tf_op jit(solution)/shard_map/ppermute | solution.py:311
  59.7 9.7 %collective-permute-start.8 = (bf16[384,384]{1,0:T(8,128)(2,1)}, bf16[384,384]{1,0:T(8,128)(2,1)}, u32[]{:S(2)}, u32[]{:S(2)}) collective-permute-start(bf16[384,384]{1,0:T(8,128)(2,1)} %get-tuple-element.45), channel_id=1, source_target_pairs={{0,56},{8,3},{9,49},{1,8},{2,58},{10,1},{11,51},{3,10},{24,0},{16,... | collective-permute-start | bytes 884744 | tf_op jit(solution)/shard_map/ppermute | solution.py:311
  62.4 17.7 %all-to-all-start.1 = ((bf16[16,16,768]{2,1,0:T(8,128)(2,1)}), bf16[16,16,768]{2,1,0:T(8,128)(2,1)S(1)}, u32[]{:S(2)}, u32[]{:S(2)}) async-start(bf16[16,16,768]{2,1,0:T(8,128)(2,1)} %get-tuple-element.39), calls=%async_computation.1 | async-start | bytes 786432 | tf_op jit(solution)/shard_map/all_to_all | solution.py:356
  71.1 6.0 %collective-permute-start.9 = (bf16[192,384]{1,0:T(8,128)(2,1)S(1)}, bf16[192,384]{1,0:T(8,128)(2,1)S(1)}, u32[]{:S(2)}, u32[]{:S(2)}) collective-permute-start(bf16[192,384]{1,0:T(8,128)(2,1)S(1)} %get-tuple-element.48), channel_id=1, source_target_pairs={{0,2},{8,40},{9,11},{1,33},{2,0},{10,42},{11,9},{3,35},{24,26},{16... | collective-permute-start | bytes 442376 | tf_op jit(solution)/shard_map/ppermute | solution.py:311
  72.7 7.4 %collective-permute-start.10 = (bf16[192,384]{1,0:T(8,128)(2,1)S(1)}, bf16[192,384]{1,0:T(8,128)(2,1)S(1)}, u32[]{:S(2)}, u32[]{:S(2)}) collective-permute-start(bf16[192,384]{1,0:T(8,128)(2,1)S(1)} %get-tuple-element.49), channel_id=1, source_target_pairs={{0,9},{8,16},{9,2},{1,25},{2,11},{10,18},{11,0},{3,27},{24,17},{16... | collective-permute-start | bytes 442376 | tf_op jit(solution)/shard_map/ppermute | solution.py:311
  73.7 6.4 %collective-permute-start.11 = (bf16[192,384]{1,0:T(8,128)(2,1)S(1)}, bf16[192,384]{1,0:T(8,128)(2,1)S(1)}, u32[]{:S(2)}, u32[]{:S(2)}) collective-permute-start(bf16[192,384]{1,0:T(8,128)(2,1)S(1)} %get-tuple-element.50), channel_id=1, source_target_pairs={{0,11},{8,48},{9,0},{1,57},{2,9},{10,50},{11,2},{3,59},{24,19},{16... | collective-permute-start | bytes 442376 | tf_op jit(solution)/shard_map/ppermute | solution.py:311

commit v8 on v6

--- a/solution.py
+++ b/solution.py
@@ -338,7 +338,7 @@
         scratch=[scr(512, 1152), scr(512, 768), scr(512, 1152), scr(512, 384), scr(384, 512), scr(384, 512),
                  scr(384, 512), scr(384, 512), scr(384, 512), scr(768, 512)],
         smem=(0,),
-        limit=32,
+        limit=24,
         flops=5 * 10**9,
         nbytes=10**7,
     )

time: 93 us -> 93 us (level)
  no operation moved by 1% of the time
where the time goes in v8:
time: 93 us; the launch traced here: 91.9 us
  blocking collectives  43.4 us (47%)
  starting transfers between devices  21.5 us (23%)
  Pallas kernels  18.4 us (20%)
  waiting for transfers between devices  7.8 us (8%)
    all_to_all x1, blocking collectives, local(): lax.all_to_all(packed, ('x1', 'x0', 'zh0', 'zh1'), split_axis=0, concat_a...  32.9 us
    pallas_call x7, Pallas kernels, call(): pl.pallas_call(body, out_shape=[jax.ShapeDtypeStruct(s, d) for s, d in ou...  18.4 us
    ppermute x9, starting transfers between devices, spread(): moved.append(lax.ppermute(block, ('x1', 'x0', 'c', 'y'), pairs))  13.9 us
    all_to_all x1, blocking collectives, local(): lax.all_to_all(slots, ('zl', 'zh0', 'zh1'), split_axis=0, concat_axis=0,...  10.5 us
    ppermute x9, waiting for transfers between devices, spread(): moved.append(lax.ppermute(block, ('x1', 'x0', 'c', 'y'), pairs))  7.79 us
    ppermute x3, starting transfers between devices, swap(): return lax.ppermute(v, 'c', [(0, 1), (1, 0)])  4.04 us
    all_to_all x1, starting transfers between devices, local(): lax.all_to_all(ig, ('x1', 'x0', 'zh0', 'zh1'), split_axis=0, concat_axis=...  3.56 us
  transfers between devices with their start and end apart: 13, of which 4 were waited for; matrix products, arithmetic and copies ran while one was open for 0% of the time, Pallas kernels for 8%

profile of v8, /device:TPU:1, one launch (start us, length us, event | category | flops | bytes accessed | tf_op | source)
XLA Modules:
  0.0 91.9 jit_solution(9934538635101070319)
XLA Ops:
  0.6 2.4 %shard_map.67 = bf16[16,32,768]{2,1,0:T(8,128)(2,1)} custom-call(bf16[256,768]{1,0:T(8,128)(2,1)} %bitcast.7, bf16[256,768]{1,0:T(8,128)(2,1)} %bitcast.8), custom_call_target="tpu_custom_call" | custom-call | tf_op jit(solution)/shard_map/pallas_call | solution.py:26
  3.0 0.0 copy-start
  3.0 32.9 %all_to_all.15.own_ref = bf16[16,32,768]{2,1,0:T(8,128)(2,1)S(1)} all-to-all(bf16[16,32,768]{2,1,0:T(8,128)(2,1)} %shard_map.67), channel_id=1, replica_groups=mesh['zh1'=2,'zh0'=2,'x1'=2,'x0'=2,'c'=2,'zl'=2,'y'=4] {'x1','x0','zh0',..., dimensions={0} | all-to-all | bytes 1572864 | tf_op jit(solution)/shard_map/all_to_all | solution.py:321
  35.9 3.5 %collective-permute-start = (bf16[16,32,768]{2,1,0:T(8,128)(2,1)S(1)}, bf16[16,32,768]{2,1,0:T(8,128)(2,1)S(1)}, u32[]{:S(2)}, u32[]{:S(2)}) collective-permute-start(bf16[16,32,768]{2,1,0:T(8,128)(2,1)S(1)} %all_to_all.15.own_ref), channel_id=1, source_target_pairs={{0,8},{8,0},{1,9},{9,1},{2,10},{10,2},{3,11},{11,3},{4,12},{12,4},... | collective-permute-start | bytes 2359304 | tf_op jit(solution)/shard_map/ppermute | solution.py:294
  39.3 0.1 pad_add_fusion.at_ref
  39.4 3.6 %shard_map.68 = (bf16[512,768]{1,0:T(8,128)(2,1)S(1)}, bf16[256,1152]{1,0:T(8,128)(2,1)S(1)}, bf16[256,384]{1,0:T(8,128)(2,1)S(1)}, bf16[768,256]{1,0:T(8,128)(2...) custom-call(s32[4]{0:T(128)S(1)} %pad_add_fusion.at_ref, ...), custom_call_target="tpu_custom_call" | custom-call | flops 1000000000 | bytes 5000000 | tf_op jit(solution)/shard_map/pallas_call | solution.py:26
  43.0 0.0 collective-permute-done.oth_ref
  43.0 7.8 %shard_map.69 = (f32[256,768]{1,0:T(8,128)S(1)}, bf16[256,768]{1,0:T(8,128)(2,1)S(1)}, bf16[384,384]{1,0:T(8,128)(2,1)S(1)}, bf16[384,384]{1,0:T(8,128)(2,1)S(1)...) custom-call(s32[4]{0:T(128)S(1)} %pad_add_fusion.at_ref, ...), custom_call_target="tpu_custom_call" | custom-call | flops 5000000000 | bytes 10000000 | tf_op jit(solution)/shard_map/pallas_call | solution.py:26
  50.8 0.1 collective-permute-start.2
  50.9 0.5 collective-permute-start.1
  51.4 2.8 %collective-permute-start.3 = (bf16[384,384]{1,0:T(8,128)(2,1)S(1)}, bf16[384,384]{1,0:T(8,128)(2,1)S(1)}, u32[]{:S(2)}, u32[]{:S(2)}) collective-permute-start(bf16[384,384]{1,0:T(8,128)(2,1)S(1)} %get-tuple-element.40), channel_id=1, source_target_pairs={{0,32},{8,10},{9,41},{1,3},{2,34},{10,8},{11,43},{3,1},{24,56},{16... | collective-permute-start | bytes 884744 | tf_op jit(solution)/shard_map/ppermute | solution.py:308
  54.2 0.7 collective-permute-start.5
  54.9 2.3 %collective-permute-start.7 = (bf16[384,384]{1,0:T(8,128)(2,1)S(1)}, bf16[384,384]{1,0:T(8,128)(2,1)S(1)}, u32[]{:S(2)}, u32[]{:S(2)}) collective-permute-start(bf16[384,384]{1,0:T(8,128)(2,1)S(1)} %get-tuple-element.44), channel_id=1, source_target_pairs={{0,56},{8,3},{9,49},{1,8},{2,58},{10,1},{11,51},{3,10},{24,0},{16,... | collective-permute-start | bytes 884744 | tf_op jit(solution)/shard_map/ppermute | solution.py:308
  57.2 0.0 collective-permute-done.2.blocks_ref
  57.2 1.6 %shard_map.70 = (bf16[16,16,768]{2,1,0:T(8,128)(2,1)}, bf16[384,384]{1,0:T(8,128)(2,1)S(1)}, bf16[384,384]{1,0:T(8,128)(2,1)S(1)}, bf16[384,384]{1,0:T(8,128)(2,...) custom-call(f32[256,768]{1,0:T(8,128)S(1)} %get-tuple-element.35.part_ref, ...), custom_call_target="tpu_custom_call" | custom-call | bytes 3000000 | tf_op jit(solution)/shard_map/pallas_call | solution.py:26
  58.8 0.9 collective-permute-start.6
  59.7 2.7 %collective-permute-start.8 = (bf16[384,384]{1,0:T(8,128)(2,1)}, bf16[384,384]{1,0:T(8,128)(2,1)}, u32[]{:S(2)}, u32[]{:S(2)}) collective-permute-start(bf16[384,384]{1,0:T(8,128)(2,1)} %get-tuple-element.45), channel_id=1, source_target_pairs={{0,56},{8,3},{9,49},{1,8},{2,58},{10,1},{11,51},{3,10},{24,0},{16,... | collective-permute-start | bytes 884744 | tf_op jit(solution)/shard_map/ppermute | solution.py:308
  62.4 3.6 %all-to-all-start.1 = ((bf16[16,16,768]{2,1,0:T(8,128)(2,1)}), bf16[16,16,768]{2,1,0:T(8,128)(2,1)S(1)}, u32[]{:S(2)}, u32[]{:S(2)}) async-start(bf16[16,16,768]{2,1,0:T(8,128)(2,1)} %get-tuple-element.39), calls=%async_computation.1 | async-start | bytes 786432 | tf_op jit(solution)/shard_map/all_to_all | solution.py:353
  65.9 0.0 collective-permute-done.5.refs_2_
  66.0 0.2 collective-permute-done.4.refs_1_
  66.2 3.2 %collective-permute-done.6.refs_3_ = bf16[384,384]{1,0:T(8,128)(2,1)} collective-permute-done((bf16[384,384]{1,0:T(8,128)(2,1)}, bf16[384,384]{1,0:T(8,128)(2,1)}, u32[]{:S(2)}, u32[]{:S(2)}) %collective-permute-start.6) | collective-permute-done | bytes 294944 | tf_op jit(solution)/shard_map/ppermute | solution.py:308
  69.3 0.0 collective-permute-done.8.refs_5_
  69.3 1.7 %shard_map.71 = (bf16[192,384]{1,0:T(8,128)(2,1)S(1)}, bf16[192,384]{1,0:T(8,128)(2,1)S(1)}, bf16[192,384]{1,0:T(8,128)(2,1)S(1)}, bf16[192,384]{1,0:T(8,128)(2,1)S(1)}) custom-call(s32[4]{0:T(128)S(1)} %pad_add_fusion.at_ref, bf16[384,384]{1,0:T(8,128)(2,1)S(1)} %collective-permute-done.3.refs_0_, bf16[384,384]{1,0:T(8,128)(2,1)S(1)} %collective-permute-done.4.refs_1_, ...), custom_call_target="tpu_custom_call" | custom-call | flops 4000000000 | tf_op jit(solution)/shard_map/pallas_call | solution.py:26
  71.1 1.6 %collective-permute-start.9 = (bf16[192,384]{1,0:T(8,128)(2,1)S(1)}, bf16[192,384]{1,0:T(8,128)(2,1)S(1)}, u32[]{:S(2)}, u32[]{:S(2)}) collective-permute-start(bf16[192,384]{1,0:T(8,128)(2,1)S(1)} %get-tuple-element.48), channel_id=1, source_target_pairs={{0,2},{8,40},{9,11},{1,33},{2,0},{10,42},{11,9},{3,35},{24,26},{16... | collective-permute-start | bytes 442376 | tf_op jit(solution)/shard_map/ppermute | solution.py:308
  72.7 1.0 %collective-permute-start.10 = (bf16[192,384]{1,0:T(8,128)(2,1)S(1)}, bf16[192,384]{1,0:T(8,128)(2,1)S(1)}, u32[]{:S(2)}, u32[]{:S(2)}) collective-permute-start(bf16[192,384]{1,0:T(8,128)(2,1)S(1)} %get-tuple-element.49), channel_id=1, source_target_pairs={{0,9},{8,16},{9,2},{1,25},{2,11},{10,18},{11,0},{3,27},{24,17},{16... | collective-permute-start | bytes 442376 | tf_op jit(solution)/shard_map/ppermute | solution.py:308
  73.7 2.0 %collective-permute-start.11 = (bf16[192,384]{1,0:T(8,128)(2,1)S(1)}, bf16[192,384]{1,0:T(8,128)(2,1)S(1)}, u32[]{:S(2)}, u32[]{:S(2)}) collective-permute-start(bf16[192,384]{1,0:T(8,128)(2,1)S(1)} %get-tuple-element.50), channel_id=1, source_target_pairs={{0,11},{8,48},{9,0},{1,57},{2,9},{10,50},{11,2},{3,59},{24,19},{16... | collective-permute-start | bytes 442376 | tf_op jit(solution)/shard_map/ppermute | solution.py:308
  75.6 1.5 %collective-permute-done.9.refs_0_ = bf16[192,384]{1,0:T(8,128)(2,1)S(1)} collective-permute-done((bf16[192,384]{1,0:T(8,128)(2,1)S(1)}, bf16[192,384]{1,0:T(8,128)(2,1)S(1)}, u32[]{:S(2)}, u32[]{:S(2)}) %collective-permute-start.9) | collective-permute-done | bytes 147488 | tf_op jit(solution)/shard_map/ppermute | solution.py:308
  77.1 2.9 %collective-permute-done.10.refs_1_ = bf16[192,384]{1,0:T(8,128)(2,1)S(1)} collective-permute-done((bf16[192,384]{1,0:T(8,128)(2,1)S(1)}, bf16[192,384]{1,0:T(8,128)(2,1)S(1)}, u32[]{:S(2)}, u32[]{:S(2)}) %collective-permute-start.10) | collective-permute-done | bytes 147488 | tf_op jit(solution)/shard_map/ppermute | solution.py:308
  80.0 0.0 collective-permute-done.11.refs_2_
  80.0 0.3 shard_map.72
  80.3 10.5 %all_to_all.16.r_ref = bf16[8,16,768]{2,1,0:T(8,128)(2,1)S(1)} all-to-all(bf16[8,16,768]{2,1,0:T(8,128)(2,1)S(1)} %shard_map.72), channel_id=1, replica_groups=mesh['zh1'=2,'zh0'=2,'x1'=2,'x0'=2,'c'=2,'zl'=2,'y'=4] {'zl','zh0','zh1'}, dimensions={0} | all-to-all | bytes 393216 | tf_op jit(solution)/shard_map/all_to_all | solution.py:357
  90.9 1.1 %shard_map.73 = (f32[3,2304]{1,0:T(4,128)}, f32[3,768]{1,0:T(4,128)}, bf16[256,768]{1,0:T(8,128)(2,1)}) custom-call(bf16[8,16,768]{2,1,0:T(8,128)(2,1)S(1)} %all_to_all.16.r_ref, bf16[16,16,768]{2,1,0:T(8,128)(2,1)S(1)} %all-to-all-done.1.back_ref.ig_ref), custom_call_target="tpu_custom_call" | custom-call | tf_op jit(solution)/shard_map/pallas_call | solution.py:26
  (6 shorter events, 0.0 us)
Async XLA Ops:
  3.0 36.4 %copy-start = (bf16[768,768]{1,0:T(8,128)(2,1)S(1)}, bf16[768,768]{1,0:T(8,128)(2,1)}, u32[]{:S(2)}) copy-start(bf16[768,768]{1,0:T(8,128)(2,1)} %wout_ref.1) | copy-start | bytes 3538948
  35.9 7.2 %collective-permute-start = (bf16[16,32,768]{2,1,0:T(8,128)(2,1)S(1)}, bf16[16,32,768]{2,1,0:T(8,128)(2,1)S(1)}, u32[]{:S(2)}, u32[]{:S(2)}) collective-permute-start(bf16[16,32,768]{2,1,0:T(8,128)(2,1)S(1)} %all_to_all.15.own_ref), channel_id=1, source_target_pairs={{0,8},{8,0},{1,9},{9,1},{2,10},{10,2},{3,11},{11,3},{4,12},{12,4},... | collective-permute-start | bytes 2359304 | tf_op jit(solution)/shard_map/ppermute | solution.py:294
  50.8 6.4 %collective-permute-start.2 = (bf16[1536,384]{1,0:T(8,128)(2,1)S(1)}, bf16[1536,384]{1,0:T(8,128)(2,1)S(1)}, u32[]{:S(2)}, u32[]{:S(2)}) collective-permute-start(bf16[1536,384]{1,0:T(8,128)(2,1)S(1)} %get-tuple-element.37), channel_id=1, source_target_pairs={{0,8},{8,0},{1,9},{9,1},{2,10},{10,2},{3,11},{11,3},{4,12},{12,4},... | collective-permute-start | bytes 3538952 | tf_op jit(solution)/shard_map/ppermute | solution.py:294
  50.9 6.3 %collective-permute-start.1 = (bf16[256,768]{1,0:T(8,128)(2,1)S(1)}, bf16[256,768]{1,0:T(8,128)(2,1)S(1)}, u32[]{:S(2)}, u32[]{:S(2)}) collective-permute-start(bf16[256,768]{1,0:T(8,128)(2,1)S(1)} %get-tuple-element.36), channel_id=1, source_target_pairs={{0,8},{8,0},{1,9},{9,1},{2,10},{10,2},{3,11},{11,3},{4,12},{12,4},... | collective-permute-start | bytes 1179656 | tf_op jit(solution)/shard_map/ppermute | solution.py:294
  51.4 8.2 %collective-permute-start.3 = (bf16[384,384]{1,0:T(8,128)(2,1)S(1)}, bf16[384,384]{1,0:T(8,128)(2,1)S(1)}, u32[]{:S(2)}, u32[]{:S(2)}) collective-permute-start(bf16[384,384]{1,0:T(8,128)(2,1)S(1)} %get-tuple-element.40), channel_id=1, source_target_pairs={{0,32},{8,10},{9,41},{1,3},{2,34},{10,8},{11,43},{3,1},{24,56},{16... | collective-permute-start | bytes 884744 | tf_op jit(solution)/shard_map/ppermute | solution.py:308
  54.2 11.7 %collective-permute-start.5 = (bf16[384,384]{1,0:T(8,128)(2,1)S(1)}, bf16[384,384]{1,0:T(8,128)(2,1)S(1)}, u32[]{:S(2)}, u32[]{:S(2)}) collective-permute-start(bf16[384,384]{1,0:T(8,128)(2,1)S(1)} %get-tuple-element.42), channel_id=1, source_target_pairs={{0,24},{8,1},{9,17},{1,10},{2,26},{10,3},{11,19},{3,8},{24,32},{16... | collective-permute-start | bytes 884744 | tf_op jit(solution)/shard_map/ppermute | solution.py:308
  54.9 11.0 %collective-permute-start.7 = (bf16[384,384]{1,0:T(8,128)(2,1)S(1)}, bf16[384,384]{1,0:T(8,128)(2,1)S(1)}, u32[]{:S(2)}, u32[]{:S(2)}) collective-permute-start(bf16[384,384]{1,0:T(8,128)(2,1)S(1)} %get-tuple-element.44), channel_id=1, source_target_pairs={{0,56},{8,3},{9,49},{1,8},{2,58},{10,1},{11,51},{3,10},{24,0},{16,... | collective-permute-start | bytes 884744 | tf_op jit(solution)/shard_map/ppermute | solution.py:308
  58.8 7.4 %collective-permute-start.4 = (bf16[384,384]{1,0:T(8,128)(2,1)}, bf16[384,384]{1,0:T(8,128)(2,1)S(1)}, u32[]{:S(2)}, u32[]{:S(2)}) collective-permute-start(bf16[384,384]{1,0:T(8,128)(2,1)} %get-tuple-element.41), channel_id=1, source_target_pairs={{0,32},{8,10},{9,41},{1,3},{2,34},{10,8},{11,43},{3,1},{24,56},{16... | collective-permute-start | bytes 884744 | tf_op jit(solution)/shard_map/ppermute | solution.py:308
  58.8 10.6 %collective-permute-start.6 = (bf16[384,384]{1,0:T(8,128)(2,1)}, bf16[384,384]{1,0:T(8,128)(2,1)}, u32[]{:S(2)}, u32[]{:S(2)}) collective-permute-start(bf16[384,384]{1,0:T(8,128)(2,1)} %get-tuple-element.43), channel_id=1, source_target_pairs={{0,24},{8,1},{9,17},{1,10},{2,26},{10,3},{11,19},{3,8},{24,32},{16... | collective-permute-start | bytes 884744 | tf_op jit(solution)/shard_map/ppermute | solution.py:308
  59.7 9.7 %collective-permute-start.8 = (bf16[384,384]{1,0:T(8,128)(2,1)}, bf16[384,384]{1,0:T(8,128)(2,1)}, u32[]{:S(2)}, u32[]{:S(2)}) collective-permute-start(bf16[384,384]{1,0:T(8,128)(2,1)} %get-tuple-element.45), channel_id=1, source_target_pairs={{0,56},{8,3},{9,49},{1,8},{2,58},{10,1},{11,51},{3,10},{24,0},{16,... | collective-permute-start | bytes 884744 | tf_op jit(solution)/shard_map/ppermute | solution.py:308
  62.4 17.7 %all-to-all-start.1 = ((bf16[16,16,768]{2,1,0:T(8,128)(2,1)}), bf16[16,16,768]{2,1,0:T(8,128)(2,1)S(1)}, u32[]{:S(2)}, u32[]{:S(2)}) async-start(bf16[16,16,768]{2,1,0:T(8,128)(2,1)} %get-tuple-element.39), calls=%async_computation.1 | async-start | bytes 786432 | tf_op jit(solution)/shard_map/all_to_all | solution.py:353
  71.1 6.0 %collective-permute-start.9 = (bf16[192,384]{1,0:T(8,128)(2,1)S(1)}, bf16[192,384]{1,0:T(8,128)(2,1)S(1)}, u32[]{:S(2)}, u32[]{:S(2)}) collective-permute-start(bf16[192,384]{1,0:T(8,128)(2,1)S(1)} %get-tuple-element.48), channel_id=1, source_target_pairs={{0,2},{8,40},{9,11},{1,33},{2,0},{10,42},{11,9},{3,35},{24,26},{16... | collective-permute-start | bytes 442376 | tf_op jit(solution)/shard_map/ppermute | solution.py:308
  72.7 7.4 %collective-permute-start.10 = (bf16[192,384]{1,0:T(8,128)(2,1)S(1)}, bf16[192,384]{1,0:T(8,128)(2,1)S(1)}, u32[]{:S(2)}, u32[]{:S(2)}) collective-permute-start(bf16[192,384]{1,0:T(8,128)(2,1)S(1)} %get-tuple-element.49), channel_id=1, source_target_pairs={{0,9},{8,16},{9,2},{1,25},{2,11},{10,18},{11,0},{3,27},{24,17},{16... | collective-permute-start | bytes 442376 | tf_op jit(solution)/shard_map/ppermute | solution.py:308
  73.7 6.4 %collective-permute-start.11 = (bf16[192,384]{1,0:T(8,128)(2,1)S(1)}, bf16[192,384]{1,0:T(8,128)(2,1)S(1)}, u32[]{:S(2)}, u32[]{:S(2)}) collective-permute-start(bf16[192,384]{1,0:T(8,128)(2,1)S(1)} %get-tuple-element.50), channel_id=1, source_target_pairs={{0,11},{8,48},{9,0},{1,57},{2,9},{10,50},{11,2},{3,59},{24,19},{16... | collective-permute-start | bytes 442376 | tf_op jit(solution)/shard_map/ppermute | solution.py:308
